TPU v7x, 32 devices: a whole 2x2x4 slice. The times are simulated.
32 devices in a mesh: seq: 2 (over y), ctx: 16 (over z, x, core).
Axes of the slice: x: 2, y: 2, z: 4, core: 2. Of those that a mesh axis runs over, the one named last changes fastest.
Arguments:
- inputs: bfloat16 [2, 4096, 768], P('seq', 'ctx'), may hold values from -6 to 6
- cotangent: bfloat16 [2, 4096, 768], P('seq', 'ctx'), may hold values from -6 to 6
- gain_attn: bfloat16 [768], P(('seq', 'ctx')), may hold values from 0.099609375 to 1.8984375
- w_query: bfloat16 [768, 768], P(('seq', 'ctx')), may hold values from -0.09375 to 0.09375
- w_key: bfloat16 [768, 768], P(('seq', 'ctx')), may hold values from -0.09375 to 0.09375
- w_value: bfloat16 [768, 768], P(('seq', 'ctx')), may hold values from -0.21875 to 0.21875
- w_output: bfloat16 [768, 768], P(('seq', 'ctx')), may hold values from -1.75 to 1.75
- bias_table: bfloat16 [32, 12], replicated, may hold values from 89 to 107
- gain_ffn: bfloat16 [768], P(('seq', 'ctx')), may hold values from 0.099609375 to 1.8984375
- w_router: bfloat16 [768, 16], P(('seq', 'ctx')), may hold values from -0.109375 to 0.109375
- w_in: bfloat16 [16, 768, 3072], P('ctx'), may hold values from -0.21875 to 0.21875
- w_out: bfloat16 [16, 3072, 768], P('ctx'), may hold values from -1.75 to 1.75
- segments: int32 [2, 4096], P('seq', 'ctx'), may hold values from 0 to 15, never falling along the last dimension, each value on 1 to 512 neighbouring positions
- routes: int32 [2, 4096, 1], P('seq', 'ctx'), may hold values from 0 to 15; in each aligned block of 256 rows (0 to 255, 256 to 511, ..., all dimensions but the last counted through in order) at most 18 rows name the same one
Outputs:
- output: bfloat16 [2, 4096, 768], P('seq', 'ctx')
- grad_inputs: bfloat16 [2, 4096, 768], P('seq', 'ctx')
- grad_gain_attn: float32 [768], P(('seq', 'ctx'))
- grad_w_query: float32 [768, 768], P(('seq', 'ctx'))
- grad_w_key: float32 [768, 768], P(('seq', 'ctx'))
- grad_w_value: float32 [768, 768], P(('seq', 'ctx'))
- grad_w_output: float32 [768, 768], P(('seq', 'ctx'))
- grad_bias_table: float32 [32, 12], replicated
- grad_gain_ffn: float32 [768], P(('seq', 'ctx'))
- grad_w_router: float32 [768, 16], P(('seq', 'ctx'))
- grad_w_in: float32 [16, 768, 3072], P('ctx')
- grad_w_out: float32 [16, 3072, 768], P('ctx')
Inputs may be any that keep to these rules, and one draw needn't show every extreme that they name: `segments`: segment numbers never fall along a sequence; each document spans 1 to 512 positions, and one in each sequence exactly 512. `routes`: within each aligned block of 256 positions no expert is chosen more than 18 times; some expert is chosen exactly 18 times in some blocks.
All inputs are finite; a program needn't handle non-finite values.
Results may differ from a plain program's by a relative error of at most 0.015.
The roundings to bfloat16 on the way count: a program that leaves them out, or rounds other values in their place, can miss the bound.
Values may be sent and summed in bfloat16 or wider, within the bound.
No kernel may reach another device: no remote copies, remote signals or barrier semaphores. Data moves between devices by JAX's collectives and lax.ppermute only.
A program may use at most 192 MiB of HBM per device.

v0:
```python
import functools

import jax
import jax.numpy as jnp
from jax import lax
from jax.experimental import pallas as pl
from jax.experimental.pallas import tpu as pltpu
from jax.sharding import PartitionSpec as P

EPSILON = 1e-06
NEGATIVE = -1e30
THRESHOLDS = (12, 16, 23, 32, 46, 64, 91)
AXES = ("seq", "ctx")
BLK = 256
LANES = 128
FAR = 91
GELU_A = 0.7978845608028654
GELU_B = 0.044715

BF16 = jnp.bfloat16
F32 = jnp.float32
VMEM = pltpu.VMEM


def params(mib=48):
    return pltpu.CompilerParams(vmem_limit_bytes=mib * 1024 * 1024)


def whole(shape):
    return pl.BlockSpec(shape, lambda *_: (0,) * len(shape))


def smem():
    return pl.BlockSpec(memory_space=pltpu.SMEM)


def anywhere():
    return pl.BlockSpec(memory_space=pl.ANY)


def nn(a, b):
    return lax.dot_general(a, b, (((1,), (0,)), ((), ())), preferred_element_type=F32)


def nt(a, b):
    return lax.dot_general(a, b, (((1,), (1,)), ((), ())), preferred_element_type=F32)


def tn(a, b):
    return lax.dot_general(a, b, (((0,), (0,)), ((), ())), preferred_element_type=F32)


def iota(shape, dim):
    return lax.broadcasted_iota(jnp.int32, shape, dim)


def bucket_of(offset_pos):
    distance = jnp.abs(offset_pos)
    far_bucket = jnp.full(distance.shape, 8, jnp.int32)
    for border in THRESHOLDS:
        far_bucket = far_bucket + (distance >= border).astype(jnp.int32)
    near_bucket = jnp.where(distance < 8, distance, far_bucket)
    return near_bucket + jnp.where(offset_pos > 0, 16, 0).astype(jnp.int32)


def three_parts(value):
    high = value.astype(BF16)
    rest = value - high.astype(F32)
    middle = rest.astype(BF16)
    return high, middle, (rest - middle.astype(F32)).astype(BF16)


def fill_message(out_ref, flat_ref, msg_ref, cap, depth, values=None):
    groups = flat_ref.shape[0] // cap
    parts = flat_ref.shape[1] // LANES
    for group in range(groups):
        for part in range(parts):
            first = group * depth + part * cap
            msg_ref[first : first + cap, :] = flat_ref[
                group * cap : (group + 1) * cap, part * LANES : (part + 1) * LANES
            ]
        first = group * depth + parts * cap
        msg_ref[first : (group + 1) * depth, :] = jnp.zeros(
            ((group + 1) * depth - first, LANES), F32
        )
        if values is not None:
            for part, piece in enumerate(values):
                msg_ref[first + part : first + part + 1, :] = piece[group : group + 1, :]
    out_ref[...] = msg_ref[...].astype(BF16)


def read_message(message, flat_ref, msg_ref, cap, depth):
    groups = flat_ref.shape[0] // cap
    parts = flat_ref.shape[1] // LANES
    msg_ref[...] = message.astype(F32)
    values = []
    for group in range(groups):
        for part in range(parts):
            first = group * depth + part * cap
            flat_ref[group * cap : (group + 1) * cap, part * LANES : (part + 1) * LANES] = msg_ref[
                first : first + cap, :
            ]
        first = group * depth + parts * cap
        values.append(jnp.sum(msg_ref[first : first + 3, :], axis=0, keepdims=True))
    return jnp.concatenate(values, axis=0)


def values_in(group_hot, slot_hot, value):
    return [
        nn(group_hot, jnp.where(slot_hot, piece, jnp.zeros_like(piece)))
        for piece in three_parts(value)
    ]


def values_out(group_hot, slot_hot, values):
    spread = sum(nn(group_hot, piece) for piece in three_parts(values))
    return jnp.sum(jnp.where(slot_hot, spread, 0.0), axis=1, keepdims=True)


def slot_places(count, groups, cap):
    row = iota((count, 1), 0)
    group = jnp.zeros((count, 1), jnp.int32)
    for border in range(1, groups):
        group = group + (row >= border * cap).astype(jnp.int32)
    by_row = (iota((count, groups), 1) == group).astype(BF16)
    first = iota((groups, count), 0) * cap
    place = iota((groups, count), 1)
    by_col = ((place >= first) & (place < first + cap)).astype(BF16)
    slot_hot = iota((count, LANES), 1) == row - group * cap
    return by_row, by_col, slot_hot


def message_kernel(cap, depth, rows_ref, meta_ref, later_ref, out_ref, flat, msg):
    del later_ref
    hot = (iota((flat.shape[0], rows_ref.shape[0]), 0) == meta_ref[0:1, :]).astype(BF16)
    flat[...] = nn(hot, rows_ref[...])
    fill_message(out_ref, flat, msg, cap, depth)


def rows_kernel(cap, depth, message_ref, out_ref, flat, msg):
    read_message(message_ref[...], flat, msg, cap, depth)
    out_ref[...] = flat[...].astype(BF16)


def picked_rows(columns, first, count=8):
    pick = (iota((count, LANES), 1) == iota((count, LANES), 0) + first).astype(BF16)
    return nt(pick, columns)


def qkv_kernel(experts, x_ref, wa_ref, wb_ref, hid_ref, q_ref, k_ref, v_ref, gain_ref):
    half = q_ref.shape[1]
    split = wa_ref.shape[1]
    cut = split - half
    gains = picked_rows(wb_ref[:, split - LANES :], experts)
    gain_ref[...] = gains
    tokens = x_ref[...].astype(F32)
    scale = lax.rsqrt(jnp.mean(tokens * tokens, axis=-1, keepdims=True) + EPSILON)
    hidden = (tokens * scale * gains[0:1, :]).astype(BF16)
    hid_ref[...] = hidden
    first = nn(hidden, wa_ref[...]).astype(BF16)
    second = nn(hidden, wb_ref[:, : split - LANES]).astype(BF16)
    q_ref[...] = first[:, :half]
    k_ref[:, :cut] = first[:, half:]
    k_ref[:, cut:] = second[:, : half - cut]
    v_ref[...] = second[:, half - cut :]


def bias_kernel(table_ref, later_ref, bias_ref, prev_ref, next_ref):
    del later_ref
    heads, near = bias_ref.shape[0], bias_ref.shape[2]
    wide = near + BLK
    table = table_ref[...]
    buckets = table.shape[1]
    apart = iota((buckets, wide), 1) - (wide // 2)
    ahead = nn(table, (bucket_of(apart) == iota((buckets, wide), 0)).astype(BF16))
    behind = nn(table, (bucket_of(-apart) == iota((buckets, wide), 0)).astype(BF16))
    for head in range(heads):
        row = pltpu.roll(ahead[head : head + 1, :], wide - (wide // 2 - LANES), 1)
        full = jnp.broadcast_to(row, (BLK, wide))
        full = pltpu.roll(full, 0, 1, stride=1, stride_axis=0)
        bias_ref[head] = full[:, :near].astype(BF16)
        row = behind[head : head + 1, :]
        for out_ref, ahead_by in ((prev_ref, BLK), (next_ref, -LANES)):
            moved = pltpu.roll(row, (wide // 2 + ahead_by) % wide, 1)
            full = jnp.broadcast_to(moved, (LANES, wide))
            full = pltpu.roll(full, 0, 1, stride=1, stride_axis=0)
            out_ref[head] = full[:, :BLK].astype(BF16)


def own_half(value, turn):
    lane = iota(value.shape, 1)
    keep = (lane < LANES // 2) if turn == 0 else (lane >= LANES // 2)
    return jnp.where(keep, value, jnp.zeros_like(value))


def scores_of(query, keys, bias, left, right, mask):
    raw = nt(query, keys)
    near = bias.shape[1]
    edge = (keys.shape[0] - near) // 2
    raw = jnp.concatenate(
        [
            raw[:, :edge] + left,
            raw[:, edge : edge + near] + bias.astype(F32),
            raw[:, edge + near :] + right,
        ],
        axis=1,
    )
    return jnp.where(mask, raw, NEGATIVE)


def attend_kernel(
    far_ref, q_ref, k_ref, v_ref, bias_ref, code_ref, ctx_ref, low_ref, lse_ref, lse_row_ref
):
    pair = pl.program_id(0)
    own = q_ref.shape[0]
    window = 5 * BLK
    lane = iota((BLK, LANES), 1)
    code_row = picked_rows(code_ref[...], 0)
    lse_row_ref[...] = jnp.zeros_like(lse_row_ref)
    for block in range(own // BLK):
        rows = slice(block * BLK, (block + 1) * BLK)
        cols = slice(block * BLK, block * BLK + window)
        query = q_ref[rows, :]
        keys = k_ref[cols, :]
        values = v_ref[cols, :]
        code_col = code_ref[own + block * BLK : own + (block + 1) * BLK, 0:1].astype(F32)
        mask = code_col == code_row[0:1, cols]
        outs = []
        logs = jnp.zeros((BLK, LANES), F32)
        for turn in range(2):
            head = pair * 2 + turn
            scores = scores_of(
                own_half(query, turn), keys, bias_ref[turn], far_ref[0, head], far_ref[1, head], mask
            )
            top = jnp.max(scores, axis=1, keepdims=True)
            weight = jnp.exp(scores - top)
            total = jnp.sum(weight, axis=1, keepdims=True)
            outs.append(nn((weight * (1.0 / total)).astype(BF16), values))
            logs = jnp.where(lane == turn, top + jnp.log(total), logs)
        context = jnp.where(lane < LANES // 2, outs[0], outs[1])
        ctx_ref[rows, :] = context
        low_ref[rows, :] = context.astype(BF16)
        lse_ref[rows, :] = logs
        lse_row_ref[0, 0:2, rows] = jnp.transpose(logs)[0:2, :]


def rolled_left(value, steps):
    return value if steps == 0 else pltpu.roll(value, value.shape[1] - steps, 1)


def diagonal_sums(value):
    eight = jnp.zeros((8, value.shape[1]), F32)
    for first in range(0, value.shape[0], 8):
        eight = eight + rolled_left(value[first : first + 8], first)
    one = jnp.zeros((1, value.shape[1]), F32)
    for row in range(8):
        one = one + rolled_left(eight[row : row + 1], row)
    return one


def own_backward_kernel(
    far_ref,
    q_ref,
    k_ref,
    v_ref,
    gctx_ref,
    ctx_ref,
    lse_ref,
    bias_ref,
    code_ref,
    dq_ref,
    dk_ref,
    dv_ref,
    tab_ref,
):
    pair = pl.program_id(0)
    blocks = q_ref.shape[0] // BLK
    window = 5 * BLK
    near = bias_ref.shape[2]
    edge = (window - near) // 2
    lane = iota((BLK, LANES), 1)
    own = q_ref.shape[0]
    code_row = picked_rows(code_ref[...], 0)
    dk_ref[...] = jnp.zeros_like(dk_ref)
    dv_ref[...] = jnp.zeros_like(dv_ref)
    near_sum = [jnp.zeros((BLK, near), F32), jnp.zeros((BLK, near), F32)]
    left_sum = [jnp.zeros((BLK, edge), F32), jnp.zeros((BLK, edge), F32)]
    right_sum = [jnp.zeros((BLK, edge), F32), jnp.zeros((BLK, edge), F32)]
    for block in range(blocks):
        rows = slice(block * BLK, (block + 1) * BLK)
        cols = slice(block * BLK, block * BLK + window)
        keys = k_ref[cols, :]
        values = v_ref[cols, :]
        code_col = code_ref[own + block * BLK : own + (block + 1) * BLK, 0:1].astype(F32)
        mask = code_col == code_row[0:1, cols]
        mine = slice((blocks - block) * BLK, (2 * blocks - block) * BLK)
        gctx_all = gctx_ref[rows, :]
        product = gctx_all.astype(F32) * ctx_ref[rows, :]
        logs = lse_ref[rows, :]
        outs = []
        for turn in range(2):
            head = pair * 2 + turn
            query = own_half(q_ref[rows, :], turn)
            gctx = own_half(gctx_all, turn)
            scores = scores_of(
                query, keys, bias_ref[turn], far_ref[0, head], far_ref[1, head], mask
            )
            probs = jnp.exp(scores - logs[:, turn : turn + 1])
            delta = jnp.sum(own_half(product, turn), axis=1, keepdims=True)
            grads = (probs * (nt(gctx, values) - delta)).astype(BF16)
            outs.append(nn(grads, keys))
            dk_ref[...] += tn(grads[:, mine], query)
            dv_ref[...] += tn(probs[:, mine].astype(BF16), gctx)
            wide = grads.astype(F32)
            left_sum[turn] = left_sum[turn] + wide[:, :edge]
            near_sum[turn] = near_sum[turn] + wide[:, edge : edge + near]
            right_sum[turn] = right_sum[turn] + wide[:, edge + near :]
        dq_ref[rows, :] = jnp.where(lane < LANES // 2, outs[0], outs[1]).astype(BF16)
    apart = iota((BLK, near), 1) - (2 * BLK - edge) - iota((BLK, near), 0)
    tab_lane = iota((1, LANES), 1)
    hot = (bucket_of(iota((near, LANES), 0) - LANES) == iota((near, LANES), 1)).astype(F32)
    for turn in range(2):
        total = near_sum[turn]
        left = jnp.sum(left_sum[turn]) + jnp.sum(jnp.where(apart <= -FAR, total, 0.0))
        right = jnp.sum(right_sum[turn]) + jnp.sum(jnp.where(apart >= FAR, total, 0.0))
        close = jnp.where(jnp.abs(apart) < FAR, total, 0.0)
        diagonal = diagonal_sums(close)
        sums = lax.dot_general(
            diagonal,
            hot,
            (((1,), (0,)), ((), ())),
            precision=lax.Precision.HIGHEST,
            preferred_element_type=F32,
        )
        sums = sums + jnp.where(tab_lane == 15, left, 0.0) + jnp.where(tab_lane == 31, right, 0.0)
        tab_ref[0, turn : turn + 1, :] = sums


def halo_backward_kernel(
    far_ref,
    qp_ref,
    qn_ref,
    k_ref,
    v_ref,
    gp_ref,
    gn_ref,
    lp_ref,
    ln_ref,
    deltap_ref,
    deltan_ref,
    biasp_ref,
    biasn_ref,
    code_ref,
    dka_ref,
    dva_ref,
    tab_in_ref,
    dk_ref,
    dv_ref,
    tab_ref,
):
    pair = pl.program_id(0)
    own = k_ref.shape[0]
    half = LANES
    code_row = picked_rows(code_ref[...], 0)
    tab_ref[...] = tab_in_ref[...]
    total_k = dka_ref[...]
    total_v = dva_ref[...]
    parts = []
    for side in range(2):
        q_side = qp_ref if side == 0 else qn_ref
        g_side = gp_ref if side == 0 else gn_ref
        for block in range(2):
            far_block = block == side
            rows = slice(block * BLK, (block + 1) * BLK)
            if far_block:
                cols = slice(0, BLK) if side == 0 else slice(own - BLK, own)
            else:
                cols = slice(0, own)
            parts.append((side, rows, cols, far_block, q_side, g_side))
    add_k = [jnp.zeros((BLK, LANES), F32), jnp.zeros((BLK, LANES), F32)]
    add_v = [jnp.zeros((BLK, LANES), F32), jnp.zeros((BLK, LANES), F32)]
    for side, rows, cols, far_block, q_side, g_side in parts:
        keys = k_ref[cols, :]
        values = v_ref[cols, :]
        count = cols.stop - cols.start
        lse_ref = lp_ref if side == 0 else ln_ref
        delta_ref = deltap_ref if side == 0 else deltan_ref
        code_col = code_ref[own + cols.start : own + cols.stop, 0:1].astype(F32)
        first = 2 * own * side + rows.start
        mask = code_col == code_row[0:1, first : first + BLK]
        for turn in range(2):
            head = pair * 2 + turn
            query = own_half(q_side[rows, :], turn)
            gctx = own_half(g_side[rows, :], turn)
            raw = nt(keys, query)
            far = far_ref[1 - side, head]
            if far_block:
                raw = raw + far
            elif side == 0:
                raw = jnp.concatenate(
                    [raw[:half] + biasp_ref[turn].astype(F32), raw[half:] + far], axis=0
                )
            else:
                raw = jnp.concatenate(
                    [raw[: count - half] + far, raw[count - half :] + biasn_ref[turn].astype(F32)],
                    axis=0,
                )
            scores = jnp.where(mask, raw, NEGATIVE)
            logs = lse_ref[0, turn : turn + 1, rows]
            delta = delta_ref[pl.ds(head, 1), rows]
            probs = jnp.exp(scores - logs)
            grads = (probs * (nt(values, gctx) - delta)).astype(BF16)
            got_k = nn(grads, query)
            got_v = nn(probs.astype(BF16), gctx)
            for index in range(count // BLK):
                place = (cols.start // BLK) + index
                part = slice(index * BLK, (index + 1) * BLK)
                add_k[place] = add_k[place] + got_k[part]
                add_v[place] = add_v[place] + got_v[part]
    dk_ref[...] = (total_k + jnp.concatenate(add_k, axis=0)).astype(BF16)
    dv_ref[...] = (total_v + jnp.concatenate(add_v, axis=0)).astype(BF16)


def delta_kernel(core_ref, mine_ref, came_ref, ctx_ref, gctx_ref, delta_ref):
    core = core_ref[0]
    tok = mine_ref.shape[0]
    width = mine_ref.shape[1]
    gctx_ref[pl.ds(pl.multiple_of(core * tok, tok), tok), :] = mine_ref[...]
    gctx_ref[pl.ds(pl.multiple_of((1 - core) * tok, tok), tok), :] = came_ref[...]
    product = gctx_ref[...].astype(F32) * ctx_ref[...]
    head_rows = delta_ref.shape[0]
    pick = (iota((head_rows, width), 1) // (LANES // 2) == iota((head_rows, width), 0)).astype(F32)
    delta_ref[...] = lax.dot_general(
        pick,
        product,
        (((1,), (1,)), ((), ())),
        precision=lax.Precision.HIGHEST,
        preferred_element_type=F32,
    )


def token_columns(meta_ref, probs):
    route_hot = iota(probs.shape, 1) == meta_ref[:, 1:2]
    slot_hot = iota((probs.shape[0], LANES), 1) == meta_ref[:, 2:3]
    gate = jnp.sum(jnp.where(route_hot, probs, 0.0), axis=1, keepdims=True)
    return route_hot, slot_hot, gate


def before_kernel(
    cap,
    depth,
    experts,
    core_ref,
    x_ref,
    own_ref,
    came_ref,
    wo_ref,
    small_ref,
    gain_ref,
    meta_col_ref,
    meta_row_ref,
    mid_ref,
    hid_ref,
    prob_ref,
    msg_out_ref,
    flat,
    msg,
):
    core = core_ref[0]
    tok = x_ref.shape[0]
    width = own_ref.shape[1]
    rows = pl.ds(pl.multiple_of(core * tok, tok), tok)
    own_w = wo_ref[pl.ds(pl.multiple_of(core * width, width), width), :]
    other_w = wo_ref[pl.ds(pl.multiple_of((1 - core) * width, width), width), :]
    attended = nn(own_ref[rows, :], own_w) + nn(came_ref[rows, :], other_w)
    middle = x_ref[...].astype(F32) + attended
    mid_ref[...] = middle
    scale = lax.rsqrt(jnp.mean(middle * middle, axis=-1, keepdims=True) + EPSILON)
    hidden = (middle * scale * gain_ref[1:2, :]).astype(BF16)
    hid_ref[...] = hidden
    logits = nn(hidden, small_ref[...])
    lane = iota(logits.shape, 1)
    logits = jnp.where(lane < experts, logits, NEGATIVE)
    weight = jnp.exp(logits - jnp.max(logits, axis=1, keepdims=True))
    probs = weight / jnp.sum(weight, axis=1, keepdims=True)
    prob_ref[...] = probs
    _, slot_hot, gate = token_columns(meta_col_ref, probs)
    route_rows = (iota((experts, tok), 0) == meta_row_ref[1:2, :]).astype(BF16)
    values = values_in(route_rows, slot_hot, gate)
    hot = (iota((flat.shape[0], tok), 0) == meta_row_ref[0:1, :]).astype(BF16)
    flat[...] = nn(hot, hidden)
    fill_message(msg_out_ref, flat, msg, cap, depth, values)


def gelu_parts(before):
    square = before * before
    inner = jnp.tanh(before * (GELU_A + (GELU_A * GELU_B) * square))
    half = 0.5 + 0.5 * inner
    slope = half + (before * (1.0 - inner * inner)) * (
        0.5 * GELU_A + (1.5 * GELU_A * GELU_B) * square
    )
    return before * half, slope


def expert_kernel(
    cap,
    depth,
    msg_ref,
    cot_ref,
    win_ref,
    wout_ref,
    earlier_a_ref,
    earlier_b_ref,
    rows_ref,
    grad_ref,
    act_ref,
    gbef_ref,
    made_ref,
    back_msg_ref,
    made_acc,
    back_acc,
    msg,
):
    del earlier_a_ref, earlier_b_ref
    step = pl.program_id(0)
    count = rows_ref.shape[0]
    groups = count // cap

    @pl.when(step == 0)
    def _():
        values = read_message(msg_ref[...], made_acc, msg, cap, depth)
        rows_ref[...] = made_acc[...].astype(BF16)
        by_row, _, slot_hot = slot_places(count, groups, cap)
        gate = values_out(by_row, slot_hot, values)
        grad_ref[...] = (gate * cot_ref[...].astype(F32)).astype(BF16)
        made_acc[...] = jnp.zeros_like(made_acc)
        back_acc[...] = jnp.zeros_like(back_acc)

    w_in = win_ref[0]
    w_out = wout_ref[0]
    before = nn(rows_ref[...], w_in)
    grad_active = nt(grad_ref[...], w_out)
    active, slope = gelu_parts(before)
    active = active.astype(BF16)
    grad_before = (grad_active * slope).astype(BF16)
    act_ref[...] = active
    gbef_ref[...] = grad_before
    made_acc[...] += nn(active, w_out)
    back_acc[...] += nt(grad_before, w_in)

    @pl.when(step == pl.num_programs(0) - 1)
    def _():
        produced = made_acc[...].astype(BF16)
        made_ref[...] = produced
        grad_gate = jnp.sum(
            cot_ref[...].astype(F32) * produced.astype(F32), axis=1, keepdims=True
        )
        _, by_col, slot_hot = slot_places(count, groups, cap)
        values = values_in(by_col, slot_hot, grad_gate)
        fill_message(back_msg_ref, back_acc, msg, cap, depth, values)


def spread_kernel(cap, depth, rows_ref, later_ref, out_ref, flat, msg):
    del later_ref
    flat[...] = rows_ref[...].astype(F32)
    fill_message(out_ref, flat, msg, cap, depth)


def expert_grads_kernel(
    cap,
    depth,
    rows_ref,
    grad_ref,
    act_ref,
    gbef_ref,
    msgs_ref,
    cots_ref,
    win_ref,
    wout_ref,
    din_ref,
    dout_ref,
    all_rows,
    all_grad,
    flat,
    msg,
):
    count = rows_ref.shape[0]
    size = msg.shape[0]

    @pl.when(pl.program_id(0) == 0)
    def _():
        all_rows[:count, :] = rows_ref[...]
        all_grad[:count, :] = grad_ref[...]
        by_row, _, slot_hot = slot_places(count, count // cap, cap)
        for other in range(msgs_ref.shape[0] // size):
            message = msgs_ref[other * size : (other + 1) * size, :]
            values = read_message(message, flat, msg, cap, depth)
            gate = values_out(by_row, slot_hot, values)
            first = (other + 1) * count
            all_rows[first : first + count, :] = flat[...].astype(BF16)
            cots = cots_ref[other * count : (other + 1) * count, :].astype(F32)
            all_grad[first : first + count, :] = (gate * cots).astype(BF16)

    w_in = win_ref[0]
    w_out = wout_ref[0]
    active, slope = gelu_parts(nn(all_rows[count:, :], w_in))
    grad_before = (nt(all_grad[count:, :], w_out) * slope).astype(BF16)
    actives = jnp.concatenate([act_ref[...], active.astype(BF16)], axis=0)
    grads = jnp.concatenate([gbef_ref[...], grad_before], axis=0)
    din_ref[0] = tn(all_rows[...], grads)
    dout_ref[0] = tn(actives, all_grad[...])


def sums_kernel(
    chip_rows,
    bits_ref,
    hid_ref,
    dq_ref,
    dk_ref,
    dv_ref,
    extra_ref,
    senda_ref,
    keepa_ref,
    sendb_ref,
    keepb_ref,
    total,
):
    rows = hid_ref.shape[1]
    half = dq_ref.shape[1]
    split = keepa_ref.shape[1]
    cut = split - half
    hidden = hid_ref[...]
    bit_a = bits_ref[0]
    bit_b = bits_ref[1]
    chunk = keepa_ref.shape[0]
    total[:, :half] = tn(hidden, dq_ref[...])
    total[:, half:] = tn(hidden, dk_ref[:, :cut])
    keepa_ref[...] = total[pl.ds(pl.multiple_of(bit_a * chunk, chunk), chunk), :]
    senda_ref[...] = total[pl.ds(pl.multiple_of((1 - bit_a) * chunk, chunk), chunk), :].astype(BF16)
    total[:, : half - cut] = tn(hidden, dk_ref[:, cut:])
    total[:, half - cut : split - LANES] = tn(hidden, dv_ref[...])
    total[:, split - LANES :] = extra_ref[...]
    chunk = chip_rows
    for index in range(rows // (2 * chunk)):
        first = index * 2 * chunk
        out = slice(index * chunk, (index + 1) * chunk)
        keepb_ref[out, :] = total[pl.ds(pl.multiple_of(first + bit_b * chunk, 8), chunk), :]
        gone = total[pl.ds(pl.multiple_of(first + (1 - bit_b) * chunk, 8), chunk), :]
        sendb_ref[out, :] = gone.astype(BF16)


def input_kernel(core_ref, dq_ref, dk_ref, dv_ref, wa_ref, wb_ref, later_ref, keep_ref, send_ref):
    del later_ref
    core = core_ref[0]
    half = dq_ref.shape[1]
    split = wa_ref.shape[1]
    cut = split - half
    tok = keep_ref.shape[0]
    for out_ref, which in ((send_ref, 1 - core), (keep_ref, core)):
        rows = pl.ds(pl.multiple_of(which * tok, tok), tok)
        out_ref[...] = (
            nt(dq_ref[rows, :], wa_ref[:, :half])
            + nt(dk_ref[rows, :cut], wa_ref[:, half:])
            + nt(dk_ref[rows, cut:], wb_ref[:, : half - cut])
            + nt(dv_ref[rows, :], wb_ref[:, half - cut : split - LANES])
        )


def after_kernel(
    cap,
    depth,
    experts,
    core_ref,
    msg_in_ref,
    cot_ref,
    mid_ref,
    hid_ref,
    prob_ref,
    small_ref,
    gain_ref,
    wo_ref,
    meta_ref,
    earlier_ref,
    gmid_ref,
    gmine_ref,
    gtheirs_ref,
    mine_ref,
    theirs_ref,
    sums_ref,
    flat,
    msg,
    low_scr,
):
    del earlier_ref
    core = core_ref[0]
    width = mine_ref.shape[1]
    tok = cot_ref.shape[0]
    values = read_message(msg_in_ref[...], flat, msg, cap, depth)
    hot = (iota((tok, flat.shape[0]), 1) == meta_ref[:, 0:1]).astype(BF16)
    came = nn(hot, flat[...].astype(BF16))
    probs = prob_ref[...]
    route_hot, slot_hot, gate = token_columns(meta_ref, probs)
    by_route = (iota((tok, experts), 1) == meta_ref[:, 1:2]).astype(BF16)
    grad_gate = values_out(by_route, slot_hot, values)
    grad_logits = (grad_gate * probs * (route_hot.astype(F32) - gate)).astype(BF16)
    grad_hidden = came + nt(grad_logits, small_ref[...])
    middle = mid_ref[...]
    scale = lax.rsqrt(jnp.mean(middle * middle, axis=-1, keepdims=True) + EPSILON)
    normed = middle * scale
    grad_normed = grad_hidden * gain_ref[1:2, :]
    grad_middle = cot_ref[...].astype(F32) + scale * (
        grad_normed - normed * jnp.mean(grad_normed * normed, axis=-1, keepdims=True)
    )
    gmid_ref[...] = grad_middle
    low = grad_middle.astype(BF16)
    low_scr[...] = low
    gmine_ref[...] = low_scr[:, pl.ds(pl.multiple_of(core * width, width), width)]
    gtheirs_ref[...] = low_scr[:, pl.ds(pl.multiple_of((1 - core) * width, width), width)]
    own_w = wo_ref[pl.ds(pl.multiple_of(core * width, width), width), :]
    other_w = wo_ref[pl.ds(pl.multiple_of((1 - core) * width, width), width), :]
    theirs_ref[...] = nt(low, other_w).astype(BF16)
    mine_ref[...] = nt(low, own_w).astype(BF16)
    router = tn(hid_ref[...], grad_logits)
    gain = lax.dot_general(
        grad_hidden * normed,
        jnp.ones((tok, LANES), F32),
        (((0,), (0,)), ((), ())),
        precision=lax.Precision.HIGHEST,
        preferred_element_type=F32,
    )
    lane = iota(router.shape, 1)
    sums_ref[...] = jnp.where(lane < experts, router, jnp.where(lane == experts, gain, 0.0))


def output_kernel(cap, depth, msg_in_ref, mid_ref, prob_ref, meta_ref, out_ref, flat, msg):
    tok = out_ref.shape[0]
    read_message(msg_in_ref[...], flat, msg, cap, depth)
    hot = (iota((tok, flat.shape[0]), 1) == meta_ref[:, 0:1]).astype(BF16)
    combined = nn(hot, flat[...].astype(BF16))
    _, _, gate = token_columns(meta_ref, prob_ref[...])
    out_ref[...] = (mid_ref[...] + gate * combined).astype(BF16)


class Place:
    def __init__(self):
        self.n_seq = lax.axis_size("seq")
        self.n_ctx = lax.axis_size("ctx")
        self.count = self.n_seq * self.n_ctx
        self.index = lax.axis_index("seq") * self.n_ctx + lax.axis_index("ctx")
        self.core = self.index % 2
        ctx_bits = (self.n_ctx - 1).bit_length()
        self.bits = (self.count - 1).bit_length()
        self.far_bits = list(range(ctx_bits - 1, 1, -1))
        self.near_bits = [1]
        self.seq_bits = list(range(self.bits - 1, ctx_bits - 1, -1))

    def swap(self, value, bit):
        pairs = [(i, i ^ (1 << bit)) for i in range(self.count)]
        return lax.ppermute(value, AXES, pairs)

    def bit(self, which):
        return (self.index >> which) & 1

    def shift(self, value, steps):
        pairs = []
        for row in range(self.n_seq):
            for col in range(self.n_ctx):
                if 0 <= col + steps < self.n_ctx:
                    pairs.append((row * self.n_ctx + col, row * self.n_ctx + col + steps))
        return lax.ppermute(value, AXES, pairs)

    def ordered(self, own, came, bit, axis, join):
        mine = self.bit(bit) == 1
        return join([jnp.where(mine, came, own), jnp.where(mine, own, came)], axis=axis)

    def stage(self, block, bit, done):
        axis = sum(1 for other in done if other > bit)
        return self.ordered(block, self.swap(block, bit), bit, axis, jnp.stack), done + [bit]

    def gather(self, block, order, done=()):
        done = list(done)
        for bit in order:
            block, done = self.stage(block, bit, done)
        return block.reshape((-1,) + block.shape[len(done) + 1 :])

    def scatter_on(self, gone, kept, order, first, keep):
        value = kept + self.swap(gone, first).astype(F32)
        return value, self.scatter(value, order, keep)

    def scatter(self, value, order, keep=()):
        left = sorted(list(order) + list(keep), reverse=True)
        value = value.reshape((2,) * len(left) + (-1,) + value.shape[1:])
        for bit in order:
            axis = left.index(bit)
            mine = self.bit(bit)
            gone = lax.dynamic_index_in_dim(value, 1 - mine, axis, keepdims=False).astype(BF16)
            kept = lax.dynamic_index_in_dim(value, mine, axis, keepdims=False)
            value = kept + self.swap(gone, bit).astype(F32)
            left.remove(bit)
        return value.reshape((-1,) + value.shape[-1:])

    def total(self, value):
        for bit in range(1, self.bits):
            value = value + self.swap(value, bit)
        return value


def call(
    kernel,
    outs,
    *args,
    us=2.0,
    grid=None,
    in_specs=None,
    out_specs=None,
    scratch=(),
    smem_first=False,
    mib=58,
):
    if in_specs is None:
        in_specs = [whole(a.shape) for a in args]
        if smem_first:
            in_specs[0] = smem()
    if out_specs is None:
        out_specs = [whole(o[0]) for o in outs]
    shapes = [jax.ShapeDtypeStruct(*o) for o in outs]
    return pl.pallas_call(
        kernel,
        out_shape=shapes,
        grid=grid if grid is not None else (1,),
        in_specs=in_specs,
        out_specs=out_specs,
        scratch_shapes=list(scratch),
        compiler_params=params(mib),
        cost_estimate=pl.CostEstimate(
            flops=int(us * 1.15e9), transcendentals=0, bytes_accessed=0
        ),
    )(*args)


def local(
    inputs,
    cotangent,
    gain_attn,
    w_query,
    w_key,
    w_value,
    w_output,
    bias_table,
    gain_ffn,
    w_router,
    w_in,
    w_out,
    segments,
    routes,
):
    place = Place()
    core = place.core
    core_arg = core.reshape(1).astype(jnp.int32)
    x = inputs[0]
    cot = cotangent[0]
    tok, width = x.shape
    heads = bias_table.shape[1]
    buckets = bias_table.shape[0]
    mine_heads = heads // 2
    half = width // 2
    pairs = half // LANES
    experts = w_router.shape[1]
    hidden_units = w_in.shape[2]
    rows_dev = w_query.shape[0]
    cap = max(2, (9 * tok + 8 * experts - 1) // (8 * experts))
    parts = width // LANES
    depth = -(-(parts * cap + 3) // 16) * 16
    n_ctx = place.n_ctx
    slots = n_ctx * cap
    far, near_bits, seq_bits = place.far_bits, place.near_bits, place.seq_bits
    rows_all = 6 * tok
    own_rows = 2 * tok

    wo = lax.all_gather(w_output, AXES, axis=0, tiled=True)
    small_w = jnp.concatenate(
        [
            w_router,
            gain_attn[:, None],
            gain_ffn[:, None],
            jnp.zeros((rows_dev, LANES - experts - 2), BF16),
        ],
        axis=1,
    )
    both = [
        jnp.concatenate(
            [w[:, side * half : (side + 1) * half] for w in (w_query, w_key, w_value)] + [small_w],
            axis=1,
        )
        for side in range(2)
    ]
    ours = jnp.where(core == 0, both[0], both[1])
    theirs = jnp.where(core == 0, both[1], both[0])
    block = place.ordered(ours, place.swap(theirs, 0), 0, 0, jnp.concatenate)
    done = []
    for bit in far:
        block, done = place.stage(block, bit, done)
    split = block.shape[-1] // 2
    later_a, done_a = block[..., :split], done
    for bit in near_bits:
        later_a, done_a = place.stage(later_a, bit, done_a)
    w_a = place.gather(later_a, seq_bits, done_a)
    w_b = place.gather(block[..., split:], seq_bits + near_bits, done)

    code = (segments[0] + 1).astype(BF16)
    x_ext = jnp.concatenate([x, jnp.broadcast_to(code[:, None], (tok, LANES))], axis=1)
    before_x = place.shift(x_ext, 2)
    after_x = place.shift(x_ext, -2)
    three = jnp.stack([before_x, x_ext, after_x])
    three_came = place.swap(three, 0)
    x_all = place.ordered(three, three_came, 0, 1, jnp.concatenate).reshape(
        rows_all, width + LANES
    )
    code_block = pl.BlockSpec((rows_all, LANES), lambda *_: (0, parts))

    near = 2 * BLK
    table_mine = lax.dynamic_slice_in_dim(bias_table, core * mine_heads, mine_heads, 1)
    far_bias = jnp.stack([table_mine[15], table_mine[31]]).astype(F32)
    bias, bias_prev, bias_next = call(
        bias_kernel,
        [
            ((mine_heads, BLK, near), BF16),
            ((mine_heads, LANES, BLK), BF16),
            ((mine_heads, LANES, BLK), BF16),
        ],
        jnp.pad(table_mine.T, ((0, 8 - mine_heads), (0, 0))),
        x_all,
        us=3.0,
        in_specs=[whole((8, buckets)), anywhere()],
    )

    route = routes[0, :, 0]
    route_hot = (route[:, None] == iota((tok, experts), 1)).astype(F32)
    earlier = (iota((tok, tok), 1) < iota((tok, tok), 0)).astype(F32)
    slot = jnp.sum(jnp.dot(earlier, route_hot) * route_hot, axis=1).astype(jnp.int32)
    meta = jnp.stack([route * cap + slot, route, slot])
    meta_row = jnp.pad(meta, ((0, 5), (0, 0)))
    meta_col = jnp.pad(meta.T, ((0, 0), (0, LANES - 3)))

    def exchange(message):
        message = message.reshape(n_ctx, depth, LANES)
        message = lax.all_to_all(message, "ctx", split_axis=0, concat_axis=0, tiled=True)
        return message.reshape(n_ctx * depth, LANES)

    msg_shape = (n_ctx * depth, LANES)
    msg_scratch = [VMEM((slots, width), F32), VMEM(msg_shape, F32)]

    hid_all, q_all, k_all, v_all, gains = call(
        functools.partial(qkv_kernel, experts),
        [((rows_all, width), BF16)] + [((rows_all, half), BF16)] * 3 + [((8, width), F32)],
        x_all,
        w_a,
        w_b,
        us=6.0,
        grid=(rows_all // own_rows,),
        in_specs=[
            pl.BlockSpec((own_rows, width), lambda i: (i, 0)),
            whole((width, split)),
            whole((width, split)),
        ],
        out_specs=[pl.BlockSpec((own_rows, width), lambda i: (i, 0))]
        + [pl.BlockSpec((own_rows, half), lambda i: (i, 0))] * 3
        + [whole((8, width))],
    )

    cot_msg = call(
        functools.partial(message_kernel, cap, depth),
        [(msg_shape, BF16)],
        cot,
        meta_row,
        gains,
        in_specs=[whole((tok, width)), whole((8, tok)), anywhere()],
        scratch=msg_scratch,
    )[0]
    cot_in = exchange(cot_msg)
    cot_rows = call(
        functools.partial(rows_kernel, cap, depth),
        [((slots, width), BF16)],
        cot_in,
        scratch=msg_scratch,
    )[0]

    hid_block = pl.BlockSpec((own_rows, width), lambda *_: (1, 0))
    small_block = pl.BlockSpec((width, LANES), lambda *_: (0, split // LANES - 1))

    own_block = pl.BlockSpec((own_rows, LANES), lambda p: (1, p))
    all_block = pl.BlockSpec((rows_all, LANES), lambda p: (0, p))
    out_block = pl.BlockSpec((own_rows, LANES), lambda p: (0, p))
    bias_block = pl.BlockSpec((2, BLK, near), lambda p: (p, 0, 0))
    lse_block = pl.BlockSpec((1, 8, own_rows), lambda p: (p, 0, 0))
    ctx_f, ctx_low, lse, lse_rows = call(
        attend_kernel,
        [
            ((own_rows, half), F32),
            ((own_rows, half), BF16),
            ((own_rows, half), F32),
            ((pairs, 8, own_rows), F32),
        ],
        far_bias,
        q_all,
        k_all,
        v_all,
        bias,
        x_all,
        us=12.0,
        grid=(pairs,),
        in_specs=[smem(), own_block, all_block, all_block, bias_block, code_block],
        out_specs=[out_block] * 3 + [lse_block],
    )

    ctx_came = place.swap(ctx_low, 0)
    mid, hid_two, probs, msg = call(
        functools.partial(before_kernel, cap, depth, experts),
        [
            ((tok, width), F32),
            ((tok, width), BF16),
            ((tok, LANES), F32),
            (msg_shape, BF16),
        ],
        core_arg,
        x,
        ctx_low,
        ctx_came,
        wo,
        w_b,
        gains,
        meta_col,
        meta_row,
        us=4.0,
        in_specs=[
            smem(),
            whole((tok, width)),
            whole((own_rows, half)),
            whole((own_rows, half)),
            whole((width, width)),
            small_block,
            whole((8, width)),
            whole((tok, LANES)),
            whole((8, tok)),
        ],
        scratch=msg_scratch,
    )
    msg_in = exchange(msg)
    lse_prev = place.shift(lse_rows, 2)
    lse_next = place.shift(lse_rows, -2)

    fblk = 512
    win_block = pl.BlockSpec((1, width, fblk), lambda i: (0, 0, i))
    wout_block = pl.BlockSpec((1, fblk, width), lambda i: (0, i, 0))
    act_block = pl.BlockSpec((slots, fblk), lambda i: (0, i))
    e_rows, e_grad, e_act, e_gbef, made, back_msg = call(
        functools.partial(expert_kernel, cap, depth),
        [((slots, width), BF16)] * 2
        + [((slots, hidden_units), BF16)] * 2
        + [((slots, width), BF16), (msg_shape, BF16)],
        msg_in,
        cot_rows,
        w_in,
        w_out,
        lse_prev,
        lse_next,
        us=12.0,
        grid=(hidden_units // fblk,),
        in_specs=[
            whole(msg_shape),
            whole((slots, width)),
            win_block,
            wout_block,
            anywhere(),
            anywhere(),
        ],
        out_specs=[whole((slots, width))] * 2
        + [act_block] * 2
        + [whole((slots, width)), whole(msg_shape)],
        scratch=[VMEM((slots, width), F32)] + msg_scratch,
    )
    back_in = exchange(back_msg)

    def from_others(value):
        total = value
        for bit in seq_bits:
            total = jnp.concatenate([total, place.swap(total, bit)], axis=0)
        return total[value.shape[0] :]

    if place.n_seq == 2:
        msgs = place.swap(msg_in, seq_bits[0])
        cots = place.swap(cot_rows, seq_bits[0])
    else:
        msgs = from_others(msg_in)
        cots = from_others(cot_rows)
    all_slots = place.n_seq * slots
    grad_w_in, grad_w_out = call(
        functools.partial(expert_grads_kernel, cap, depth),
        [(w_in.shape, F32), (w_out.shape, F32)],
        e_rows,
        e_grad,
        e_act,
        e_gbef,
        msgs,
        cots,
        w_in,
        w_out,
        us=16.0,
        grid=(hidden_units // fblk,),
        in_specs=[
            whole((slots, width)),
            whole((slots, width)),
            act_block,
            act_block,
            whole(msgs.shape),
            whole(cots.shape),
            win_block,
            wout_block,
        ],
        out_specs=[win_block, wout_block],
        scratch=[VMEM((all_slots, width), BF16), VMEM((all_slots, width), BF16)] + msg_scratch,
    )

    grad_mid, gattn_mine, gattn_theirs, gctx_mine, gctx_theirs, extra = call(
        functools.partial(after_kernel, cap, depth, experts),
        [((tok, width), F32)] + [((tok, half), BF16)] * 4 + [((width, LANES), F32)],
        core_arg,
        back_in,
        cot,
        mid,
        hid_two,
        probs,
        w_b,
        gains,
        wo,
        meta_col,
        grad_w_out,
        us=5.0,
        in_specs=[
            smem(),
            whole(msg_shape),
            whole((tok, width)),
            whole((tok, width)),
            whole((tok, width)),
            whole((tok, LANES)),
            small_block,
            whole((8, width)),
            whole((width, width)),
            whole((tok, LANES)),
            anywhere(),
        ],
        scratch=msg_scratch + [VMEM((tok, width), BF16)],
    )

    gctx_came = place.swap(gctx_theirs, 0)
    gctx, delta = call(
        delta_kernel,
        [((own_rows, half), BF16), ((8, own_rows), F32)],
        core_arg,
        gctx_mine,
        gctx_came,
        ctx_f,
        us=2.0,
        smem_first=True,
    )
    gctx_prev = place.shift(gctx, 2)
    gctx_next = place.shift(gctx, -2)
    delta_prev = place.shift(delta, 2)
    delta_next = place.shift(delta, -2)

    dq, dk_own, dv_own, tab = call(
        own_backward_kernel,
        [
            ((own_rows, half), BF16),
            ((own_rows, half), F32),
            ((own_rows, half), F32),
            ((pairs, 8, LANES), F32),
        ],
        far_bias,
        q_all,
        k_all,
        v_all,
        gctx,
        ctx_f,
        lse,
        bias,
        x_all,
        us=15.0,
        grid=(pairs,),
        in_specs=[
            smem(),
            own_block,
            all_block,
            all_block,
            out_block,
            out_block,
            out_block,
            bias_block,
            code_block,
        ],
        out_specs=[out_block] * 3 + [pl.BlockSpec((1, 8, LANES), lambda p: (p, 0, 0))],
    )

    delta_block = whole((8, own_rows))
    halo_bias = pl.BlockSpec((2, LANES, BLK), lambda p: (p, 0, 0))
    tab_block = pl.BlockSpec((1, 8, LANES), lambda p: (p, 0, 0))
    dk, dv, tab = call(
        halo_backward_kernel,
        [((own_rows, half), BF16)] * 2 + [((pairs, 8, LANES), F32)],
        far_bias,
        q_all,
        q_all,
        k_all,
        v_all,
        gctx_prev,
        gctx_next,
        lse_prev,
        lse_next,
        delta_prev,
        delta_next,
        bias_prev,
        bias_next,
        x_all,
        dk_own,
        dv_own,
        tab,
        us=9.0,
        grid=(pairs,),
        in_specs=[
            smem(),
            pl.BlockSpec((own_rows, LANES), lambda p: (0, p)),
            pl.BlockSpec((own_rows, LANES), lambda p: (2, p)),
            own_block,
            own_block,
            out_block,
            out_block,
            lse_block,
            lse_block,
            delta_block,
            delta_block,
            halo_bias,
            halo_bias,
            code_block,
            out_block,
            out_block,
            tab_block,
        ],
        out_specs=[out_block] * 2 + [tab_block],
    )

    ga_cols = place.ordered(gattn_mine, place.swap(gattn_theirs, 0), 0, 0, jnp.concatenate)
    ctx_full = place.ordered(ctx_low, ctx_came, 0, 1, jnp.concatenate)
    back_far = far[::-1]
    head_bits = seq_bits + near_bits
    sum_o = place.scatter(tn(ctx_full, ga_cols), head_bits, back_far)
    chip_rows = 2 * rows_dev
    order_a = seq_bits + near_bits
    order_b = near_bits + seq_bits
    if chip_rows % 16 == 0:
        bits = jnp.stack([place.bit(order_a[0]), place.bit(order_b[0])]).astype(jnp.int32)
        gone_a, kept_a, gone_b, kept_b = call(
            functools.partial(sums_kernel, chip_rows),
            [
                ((width // 2, split), BF16),
                ((width // 2, split), F32),
                ((width // 2, split), BF16),
                ((width // 2, split), F32),
            ],
            bits,
            hid_all,
            dq,
            dk,
            dv,
            extra,
            us=4.0,
            in_specs=[
                smem(),
                hid_block,
                whole((own_rows, half)),
                whole((own_rows, half)),
                whole((own_rows, half)),
                whole((width, LANES)),
            ],
            scratch=[VMEM((width, split), F32)],
        )
        soon = gone_a
        later, sum_a = place.scatter_on(gone_a, kept_a, order_a[1:], order_a[0], back_far)
        _, sum_b = place.scatter_on(gone_b, kept_b, order_b[1:], order_b[0], back_far)
    else:
        hid_one = hid_all[own_rows : 2 * own_rows]
        cut = split - half
        total_a = tn(hid_one, jnp.concatenate([dq, dk[:, :cut]], axis=1))
        total_b = tn(hid_one, jnp.concatenate([dk[:, cut:], dv], axis=1))
        soon = later = total_a
        sum_a = place.scatter(total_a, order_a, back_far)
        sum_b = place.scatter(jnp.concatenate([total_b, extra], axis=1), order_b, back_far)
    sums = place.scatter(jnp.concatenate([sum_a, sum_b, sum_o], axis=1), back_far)
    sums = sums.reshape(2, rows_dev, sums.shape[1])
    gone = lax.dynamic_index_in_dim(sums, 1 - core, 0, keepdims=False)
    kept = lax.dynamic_index_in_dim(sums, core, 0, keepdims=False)
    came = place.swap(gone, 0)

    def columns(first):
        return place.ordered(
            kept[:, first : first + half], came[:, first : first + half], 0, 1, jnp.concatenate
        )

    sum_q, sum_k, sum_v = columns(0), columns(half), columns(2 * half)
    sum_out = columns(3 * half + LANES)
    extra_sum = kept[:, 3 * half : 3 * half + LANES] + came[:, 3 * half : 3 * half + LANES]
    grad_router = extra_sum[:, :experts]
    grad_gain_two = extra_sum[:, experts]
    weighted = (
        sum_q * w_query.astype(F32) + sum_k * w_key.astype(F32) + sum_v * w_value.astype(F32)
    )
    grad_gain_one = jnp.sum(weighted, axis=1) / gain_attn.astype(F32)

    part, part_gone = call(
        input_kernel,
        [((tok, width), F32), ((tok, width), F32)],
        core_arg,
        dq,
        dk,
        dv,
        w_a,
        w_b,
        later,
        us=4.0,
        in_specs=[smem()]
        + [whole((own_rows, half))] * 3
        + [whole((width, split))] * 2
        + [anywhere()],
    )
    grad_hidden = part + place.swap(part_gone, 0)
    tokens = x.astype(F32)
    scale_one = lax.rsqrt(jnp.mean(tokens * tokens, axis=-1, keepdims=True) + EPSILON)
    normed_one = tokens * scale_one
    grad_normed = grad_hidden * gains[0:1]
    grad_tokens = grad_mid + scale_one * (
        grad_normed - normed_one * jnp.mean(grad_normed * normed_one, axis=-1, keepdims=True)
    )

    made_msg = call(
        functools.partial(spread_kernel, cap, depth),
        [(msg_shape, BF16)],
        made,
        soon,
        in_specs=[whole((slots, width)), anywhere()],
        scratch=msg_scratch,
    )[0]
    made_in = exchange(made_msg)
    output = call(
        functools.partial(output_kernel, cap, depth),
        [((tok, width), BF16)],
        made_in,
        mid,
        probs,
        meta_col,
        scratch=msg_scratch,
    )[0]

    table = place.total(tab[:, :2].reshape(mine_heads, LANES))
    table = place.ordered(table, place.swap(table, 0), 0, 0, jnp.concatenate)
    table_sum = table[:, :buckets].T

    return (
        output[None],
        grad_tokens.astype(BF16)[None],
        grad_gain_one,
        sum_q,
        sum_k,
        sum_v,
        sum_out,
        table_sum,
        grad_gain_two,
        grad_router,
        grad_w_in,
        grad_w_out,
    )


def solution(mesh):
    rows = P(("seq", "ctx"), None)
    flat = P(("seq", "ctx"))
    tokens = P("seq", "ctx", None)
    expert = P("ctx", None, None)
    return jax.shard_map(
        local,
        mesh=mesh,
        in_specs=(
            tokens,
            tokens,
            flat,
            rows,
            rows,
            rows,
            rows,
            P(),
            flat,
            rows,
            expert,
            expert,
            P("seq", "ctx"),
            tokens,
        ),
        out_specs=(
            tokens,
            tokens,
            flat,
            rows,
            rows,
            rows,
            rows,
            P(),
            flat,
            rows,
            expert,
            expert,
        ),
        check_vma=False,
    )
```

profile of v0, /device:TPU:0, one launch (start us, length us, event | category | flops | bytes accessed | tf_op | source)
XLA Modules:
  0.0 283.1 jit_solution(17092095911733596962)
XLA Ops:
  9.2 4.9 %collective-permute-start = (bf16[256,896]{1,0:T(8,128)(2,1)S(1)}, bf16[256,896]{1,0:T(8,128)(2,1)S(1)}, u32[]{:S(2)}, u32[]{:S(2)}) collective-permute-start(bf16[256,896]{1,0:T(8,128)(2,1)S(1)} %get-tuple-element.171), channel_id=1, source_target_pairs={{0,2},{1,3},{2,4},{3,5},{4,6},{5,7},{6,8},{7,9},{8,10},{9,11},{10,... | collective-permute-start | bytes 1376264 | tf_op jit(solution)/shard_map/ppermute | solution.py:770
  17.3 4.7 %collective-permute-start.4 = (bf16[48,1280]{1,0:T(8,128)(2,1)S(1)}, bf16[48,1280]{1,0:T(8,128)(2,1)S(1)}, u32[]{:S(2)}, u32[]{:S(2)}) collective-permute-start(bf16[48,1280]{1,0:T(8,128)(2,1)S(1)} %pad_maximum_fusion.10), channel_id=1, source_target_pairs={{0,8},{1,9},{2,10},{3,11},{4,12},{5,13},{6,14},{7,15},{8,0},{9,1},... | collective-permute-start | bytes 368648 | tf_op jit(solution)/shard_map/ppermute | solution.py:759
  22.0 13.7 %collective-permute-done.4 = bf16[48,1280]{1,0:T(8,128)(2,1)S(1)} collective-permute-done((bf16[48,1280]{1,0:T(8,128)(2,1)S(1)}, bf16[48,1280]{1,0:T(8,128)(2,1)S(1)}, u32[]{:S(2)}, u32[]{:S(2)}) %collective-permute-start.4) | collective-permute-done | bytes 122912 | tf_op jit(solution)/shard_map/ppermute | solution.py:759
  36.0 6.1 %collective-permute-done.5 = bf16[2,48,1280]{2,1,0:T(8,128)(2,1)S(1)} collective-permute-done((bf16[2,48,1280]{2,1,0:T(8,128)(2,1)S(1)}, bf16[2,48,1280]{2,1,0:T(8,128)(2,1)S(1)}, u32[]{:S(2)}, u32[]{:S(2)}) %collective-permute-start.5) | collective-permute-done | bytes 245792 | tf_op jit(solution)/shard_map/ppermute | solution.py:759
  45.1 3.7 %collective-permute-done.8 = bf16[2,2,48,640]{3,2,0,1:T(8,128)(2,1)S(1)} collective-permute-done((bf16[2,2,48,640]{3,2,0,1:T(8,128)(2,1)S(1)}, bf16[2,2,48,640]{3,2,0,1:T(8,128)(2,1)S(1)}, u32[]{:S(2)}, u32[]{:S(2)}) %collective-permute-start.8) | collective-permute-done | bytes 245792 | tf_op jit(solution)/shard_map/ppermute | solution.py:759
  54.1 6.6 %collective-permute-done.9 = bf16[2,2,2,48,640]{4,3,1,2,0:T(8,128)(2,1)} collective-permute-done((bf16[2,2,2,48,640]{4,3,1,2,0:T(8,128)(2,1)}, bf16[2,2,2,48,640]{4,3,1,2,0:T(8,128)(2,1)}, u32[]{:S(2)}, u32[]{:S(2)}) %collective-permute-start.9) | collective-permute-done | bytes 491552 | tf_op jit(solution)/shard_map/ppermute | solution.py:759
  63.0 3.0 %collective-permute-done.7 = bf16[2,2,2,48,640]{4,3,0,1,2:T(8,128)(2,1)S(1)} collective-permute-done((bf16[2,2,2,48,640]{4,3,0,1,2:T(8,128)(2,1)S(1)}, bf16[2,2,2,48,640]{4,3,0,1,2:T(8,128)(2,1)S(1)}, u32[]{:S(2)}, u32[]{:S(2)}) %collective-permute-start.7) | collective-permute-done | bytes 491552 | tf_op jit(solution)/shard_map/ppermute | solution.py:759
  69.4 6.8 %shard_map.229 = (bf16[1536,768]{1,0:T(8,128)(2,1)}, bf16[1536,384]{1,0:T(8,128)(2,1)}, bf16[1536,384]{1,0:T(8,128)(2,1)}, bf16[1536,384]{1,0:T(8,128)(2,1)}, f32[8,768]{1,0:T(8,128)}) custom-call(bf16[1536,896]{1,0:T(8,128)(2,1)} %bitcast.101, bf16[768,640]{1,0:T(8,128)(2,1)} %bitcast.115, bf16[768,640]{1,0:T(8,128)(2,1)} %bitcast.111), custom_call_target="tpu_custom_call" | custom-call | flops 6899999744 | tf_op jit(solution)/shard_map/pallas_call | solution.py:827
  78.2 3.6 %all-to-all-start.1 = ((bf16[16,112,128]{2,1,0:T(8,128)(2,1)}), bf16[16,112,128]{2,1,0:T(8,128)(2,1)S(1)}, u32[]{:S(2)}, u32[]{:S(2)}) async-start(bf16[16,112,128]{2,1,0:T(8,128)(2,1)} %bitcast.127), calls=%async_computation.1 | async-start | bytes 917504 | tf_op jit(solution)/shard_map/all_to_all | solution.py:947
  81.8 2.8 %shard_map.230 = (bf16[6,256,512]{2,1,0:T(8,128)(2,1)}, bf16[6,128,256]{2,1,0:T(8,128)(2,1)}, bf16[6,128,256]{2,1,0:T(8,128)(2,1)}) custom-call(bf16[8,32]{1,0:T(8,128)(2,1)} %pad.12.clone.table_ref, bf16[1536,896]{1,0:T(8,128)(2,1)} %bitcast.102), custom_call_target="tpu_custom_call" | custom-call | flops 3449999872 | tf_op jit(solution)/shard_map/pallas_call | solution.py:827
  84.6 12.9 %shard_map.231 = (f32[512,384]{1,0:T(8,128)}, bf16[512,384]{1,0:T(8,128)(2,1)}, f32[512,384]{1,0:T(8,128)}, f32[3,8,512]{2,1,0:T(8,128)}) custom-call(f32[2,6]{1,0:T(2,128)} %maximum_convert_fusion.far_ref, bf16[1536,384]{1,0:T(8,128)(2,1)} %get-tuple-element.57.q_ref.qp_ref.qn_ref, bf16[1536,384]{1,0:T(8,128)(2,1)} %get-tuple-element.58.k_ref, ...), custom_call_target="tpu_custom_call" | custom-call | flops 13799999488 | tf_op jit(solution)/shard_map/pallas_call | solution.py:827
  100.3 4.1 %shard_map.232 = (f32[256,768]{1,0:T(8,128)}, bf16[256,768]{1,0:T(8,128)(2,1)}, f32[256,128]{1,0:T(8,128)}, bf16[1792,128]{1,0:T(8,128)(2,1)}) custom-call(s32[1]{0:T(128)} %bitcast.core_ref, bf16[256,768]{1,0:T(8,128)(2,1)} %bitcast.96, bf16[512,384]{1,0:T(8,128)(2,1)} %get-tuple-element.61.own_ref, bf16[512,384]{1,0:T(8,128)(2,1)} %copy-done.13, ...), custom_call_target="tpu_custom_call" | custom-call | flops 4600000000 | tf_op jit(solution)/shard_map/pallas_call | solution.py:827
  104.5 6.0 %all-to-all-start = ((bf16[16,112,128]{2,1,0:T(8,128)(2,1)}), bf16[16,112,128]{2,1,0:T(8,128)(2,1)S(1)}, u32[]{:S(2)}, u32[]{:S(2)}) async-start(bf16[16,112,128]{2,1,0:T(8,128)(2,1)} %bitcast.125), calls=%async_computation | async-start | bytes 917504 | tf_op jit(solution)/shard_map/all_to_all | solution.py:947
  111.3 3.8 %collective-permute-start.11 = (f32[3,8,512]{2,1,0:T(8,128)S(1)}, f32[3,8,512]{2,1,0:T(8,128)S(1)}, u32[]{:S(2)}, u32[]{:S(2)}) collective-permute-start(f32[3,8,512]{2,1,0:T(8,128)S(1)} %copy-done.33), channel_id=1, source_target_pairs={{0,2},{1,3},{2,4},{3,5},{4,6},{5,7},{6,8},{7,9},{8,10},{9,11},{10,... | collective-permute-start | bytes 147464 | tf_op jit(solution)/shard_map/ppermute | solution.py:770
  119.0 4.7 %all-to-all-done = bf16[16,112,128]{2,1,0:T(8,128)(2,1)S(1)} async-done(((bf16[16,112,128]{2,1,0:T(8,128)(2,1)}), bf16[16,112,128]{2,1,0:T(8,128)(2,1)S(1)}, u32[]{:S(2)}, u32[]{:S(2)}) %all-to-all-start) | async-done | bytes 458784 | tf_op jit(solution)/shard_map/all_to_all | solution.py:947
  125.5 12.3 %shard_map.235 = (bf16[288,768]{1,0:T(8,128)(2,1)}, bf16[288,768]{1,0:T(8,128)(2,1)}, bf16[288,3072]{1,0:T(8,128)(2,1)}, bf16[288,3072]{1,0:T(8,128)(2,1)}, bf16...) custom-call(bf16[1792,128]{1,0:T(8,128)(2,1)} %bitcast.122, bf16[288,768]{1,0:T(8,128)(2,1)} %shard_map.234.cot_ref, ...), custom_call_target="tpu_custom_call" | custom-call | flops 13799999488 | tf_op jit(solution)/shard_map/pallas_call | solution.py:827
  137.8 4.0 %all-to-all-start.2 = ((bf16[16,112,128]{2,1,0:T(8,128)(2,1)}), bf16[16,112,128]{2,1,0:T(8,128)(2,1)S(1)}, u32[]{:S(2)}, u32[]{:S(2)}) async-start(bf16[16,112,128]{2,1,0:T(8,128)(2,1)} %bitcast.128), calls=%async_computation.2 | async-start | bytes 917504 | tf_op jit(solution)/shard_map/all_to_all | solution.py:947
  142.7 16.4 %shard_map.236 = (f32[1,768,3072]{2,1,0:T(8,128)}, f32[1,3072,768]{2,1,0:T(8,128)}) custom-call(bf16[288,768]{1,0:T(8,128)(2,1)} %get-tuple-element.71.rows_ref, bf16[288,768]{1,0:T(8,128)(2,1)} %get-tuple-element.72.grad_ref, bf16[288,3072]{1,0:T(8,128)(2,1)} %get-tuple-element.73.act_ref, bf16[288,3072]{1,0:T(8,128)(2,1)} %get-tuple-element.74.gbef_ref, ...), custom_call_target="tpu_custom_call" | custom-call | flops 18400000000 | tf_op jit(solution)/shard_map/pallas_call | solution.py:827
  159.9 5.3 %shard_map.237 = (f32[256,768]{1,0:T(8,128)}, bf16[256,384]{1,0:T(8,128)(2,1)}, bf16[256,384]{1,0:T(8,128)(2,1)}, bf16[256,384]{1,0:T(8,128)(2,1)}, bf16[256,384]{1,0:T(8,128)(2,1)}, /*index=5*/f32[768,128]{1,0:T(8,128)}) custom-call(s32[1]{0:T(128)} %bitcast.core_ref, bf16[1792,128]{1,0:T(8,128)(2,1)} %bitcast.126, bf16[256,768]{1,0:T(8,128)(2,1)} %bitcast.137, ...), custom_call_target="tpu_custom_call" | custom-call | flops 5750000128 | tf_op jit(solution)/shard_map/pallas_call | solution.py:827
  170.4 3.8 %collective-permute-start.16 = (bf16[512,384]{1,0:T(8,128)(2,1)}, bf16[512,384]{1,0:T(8,128)(2,1)S(1)}, u32[]{:S(2)}, u32[]{:S(2)}) collective-permute-start(bf16[512,384]{1,0:T(8,128)(2,1)} %get-tuple-element.79.gctx_ref), channel_id=1, source_target_pairs={{0,2},{1,3},{2,4},{3,5},{4,6},{5,7},{6,8},{7,9},{8,10},{9,11},{10,... | collective-permute-start | bytes 1179656 | tf_op jit(solution)/shard_map/ppermute | solution.py:770
  175.5 4.5 %collective-permute-start.18 = (f32[8,512]{1,0:T(8,128)}, f32[8,512]{1,0:T(8,128)S(1)}, u32[]{:S(2)}, u32[]{:S(2)}) collective-permute-start(f32[8,512]{1,0:T(8,128)} %get-tuple-element.82), channel_id=1, source_target_pairs={{0,2},{1,3},{2,4},{3,5},{4,6},{5,7},{6,8},{7,9},{8,10},{9,11},{10,... | collective-permute-start | bytes 49160 | tf_op jit(solution)/shard_map/ppermute | solution.py:770
  181.6 15.3 %shard_map.239 = (bf16[512,384]{1,0:T(8,128)(2,1)}, f32[512,384]{1,0:T(8,128)}, f32[512,384]{1,0:T(8,128)}, f32[3,8,128]{2,1,0:T(8,128)}) custom-call(f32[2,6]{1,0:T(2,128)} %maximum_convert_fusion.far_ref, bf16[1536,384]{1,0:T(8,128)(2,1)} %get-tuple-element.57.q_ref.qp_ref.qn_ref, bf16[1536,384]{1,0:T(8,128)(2,1)} %get-tuple-element.58.k_ref, ...), custom_call_target="tpu_custom_call" | custom-call | flops 17250000896 | tf_op jit(solution)/shard_map/pallas_call | solution.py:827
  199.9 9.4 %shard_map.240 = (bf16[512,384]{1,0:T(8,128)(2,1)}, bf16[512,384]{1,0:T(8,128)(2,1)}, f32[3,8,128]{2,1,0:T(8,128)}) custom-call(f32[2,6]{1,0:T(2,128)} %maximum_convert_fusion.far_ref, bf16[1536,384]{1,0:T(8,128)(2,1)} %get-tuple-element.57.q_ref.qp_ref.qn_ref, bf16[1536,384]{1,0:T(8,128)(2,1)} %get-tuple-element.57.q_ref.qp_ref.qn_ref, ...), custom_call_target="tpu_custom_call" | custom-call | flops 10350000128 | tf_op jit(solution)/shard_map/pallas_call | solution.py:827
  210.0 3.0 %collective-permute-start.31 = (f32[6,128]{1,0:T(8,128)S(1)}, f32[6,128]{1,0:T(8,128)S(1)}, u32[]{:S(2)}, u32[]{:S(2)}) collective-permute-start(f32[6,128]{1,0:T(8,128)S(1)} %reshape.154), channel_id=1, source_target_pairs={{0,2},{1,3},{2,0},{3,1},{4,6},{5,7},{6,4},{7,5},{8,10},{9,11},{10,... | collective-permute-start | bytes 9224 | tf_op jit(solution)/shard_map/ppermute | solution.py:759
  214.6 3.5 %collective-permute-start.32 = (f32[6,128]{1,0:T(8,128)S(1)}, f32[6,128]{1,0:T(8,128)S(1)}, u32[]{:S(2)}, u32[]{:S(2)}) collective-permute-start(f32[6,128]{1,0:T(8,128)S(1)} %add.175), channel_id=1, source_target_pairs={{0,4},{1,5},{2,6},{3,7},{4,0},{5,1},{6,2},{7,3},{8,12},{9,13},{10,... | collective-permute-start | bytes 9224 | tf_op jit(solution)/shard_map/ppermute | solution.py:759
  219.6 2.9 %collective-permute-start.33 = (f32[6,128]{1,0:T(8,128)S(1)}, f32[6,128]{1,0:T(8,128)S(1)}, u32[]{:S(2)}, u32[]{:S(2)}) collective-permute-start(f32[6,128]{1,0:T(8,128)S(1)} %add.176), channel_id=1, source_target_pairs={{0,8},{1,9},{2,10},{3,11},{4,12},{5,13},{6,14},{7,15},{8,0},{9,1},... | collective-permute-start | bytes 9224 | tf_op jit(solution)/shard_map/ppermute | solution.py:759
  224.7 4.3 %shard_map.241 = (bf16[384,640]{1,0:T(8,128)(2,1)}, f32[384,640]{1,0:T(8,128)}, bf16[384,640]{1,0:T(8,128)(2,1)}, f32[384,640]{1,0:T(8,128)}) custom-call(s32[2]{0:T(128)} %pad_add_fusion.1.bits_ref, bf16[1536,768]{1,0:T(8,128)(2,1)} %get-tuple-element.66.hid_ref, bf16[512,384]{1,0:T(8,128)(2,1)} %get-tuple-element.81.dq_ref, ...), custom_call_target="tpu_custom_call" | custom-call | flops 4600000000 | tf_op jit(solution)/shard_map/pallas_call | solution.py:827
  233.6 5.7 %all-to-all-start.3 = ((bf16[16,112,128]{2,1,0:T(8,128)(2,1)}), bf16[16,112,128]{2,1,0:T(8,128)(2,1)S(1)}, u32[]{:S(2)}, u32[]{:S(2)}) async-start(bf16[16,112,128]{2,1,0:T(8,128)(2,1)} %bitcast.124), calls=%async_computation.3 | async-start | bytes 917504 | tf_op jit(solution)/shard_map/all_to_all | solution.py:947
  243.8 8.4 %collective-permute-done.22 = bf16[2,2,48,640]{3,2,1,0:T(8,128)(2,1)S(1)} collective-permute-done((bf16[2,2,48,640]{3,2,1,0:T(8,128)(2,1)S(1)}, bf16[2,2,48,640]{3,2,1,0:T(8,128)(2,1)S(1)}, u32[]{:S(2)}, u32[]{:S(2)}) %collective-permute-start.22) | collective-permute-done | bytes 245792 | tf_op jit(solution)/shard_map/ppermute | solution.py:759
  254.0 4.3 %shard_map.244 = (f32[256,768]{1,0:T(8,128)}, f32[256,768]{1,0:T(8,128)}) custom-call(s32[1]{0:T(128)} %bitcast.core_ref, bf16[512,384]{1,0:T(8,128)(2,1)} %get-tuple-element.81.dq_ref, bf16[512,384]{1,0:T(8,128)(2,1)} %get-tuple-element.88.dk_ref, bf16[512,384]{1,0:T(8,128)(2,1)} %get-tuple-element.89.dv_ref, bf16[768,640]{1,0:T(8,128)(2,1)} %bitcast.116, ...), custom_call_target="tpu_custom_call" | custom-call | flops 4600000000 | tf_op jit(solution)/shard_map/pallas_call | solution.py:827
  261.3 3.1 %collective-permute-start.29 = (bf16[48,1664]{1,0:T(8,128)(2,1)S(1)}, bf16[48,1664]{1,0:T(8,128)(2,1)S(1)}, u32[]{:S(2)}, u32[]{:S(2)}) collective-permute-start(bf16[48,1664]{1,0:T(8,128)(2,1)S(1)} %fusion.22), channel_id=1, source_target_pairs={{0,8},{1,9},{2,10},{3,11},{4,12},{5,13},{6,14},{7,15},{8,0},{9,1},... | collective-permute-start | bytes 479240 | tf_op jit(solution)/shard_map/ppermute | solution.py:759
  267.7 3.0 %collective-permute-done.29 = bf16[48,1664]{1,0:T(8,128)(2,1)S(1)} collective-permute-done((bf16[48,1664]{1,0:T(8,128)(2,1)S(1)}, bf16[48,1664]{1,0:T(8,128)(2,1)S(1)}, u32[]{:S(2)}, u32[]{:S(2)}) %collective-permute-start.29) | collective-permute-done | bytes 159776 | tf_op jit(solution)/shard_map/ppermute | solution.py:759
  (225 shorter events, 71.7 us)
Async XLA Ops:
  7.3 92.3 %all-gather.2.cloned.1.call-start = ((), (), s32[]{:S(2)}) async-start(), calls=%async_computation.4 | async-start | bytes 1216512 | tf_op jit(solution)/shard_map/all_gather | solution.py:880
  9.2 34.6 %collective-permute-start = (bf16[256,896]{1,0:T(8,128)(2,1)S(1)}, bf16[256,896]{1,0:T(8,128)(2,1)S(1)}, u32[]{:S(2)}, u32[]{:S(2)}) collective-permute-start(bf16[256,896]{1,0:T(8,128)(2,1)S(1)} %get-tuple-element.171), channel_id=1, source_target_pairs={{0,2},{1,3},{2,4},{3,5},{4,6},{5,7},{6,8},{7,9},{8,10},{9,11},{10,... | collective-permute-start | bytes 1376264 | tf_op jit(solution)/shard_map/ppermute | solution.py:770
  14.1 29.8 %collective-permute-start.1 = (bf16[256,896]{1,0:T(8,128)(2,1)S(1)}, bf16[256,896]{1,0:T(8,128)(2,1)S(1)}, u32[]{:S(2)}, u32[]{:S(2)}) collective-permute-start(bf16[256,896]{1,0:T(8,128)(2,1)S(1)} %get-tuple-element.171), channel_id=1, source_target_pairs={{2,0},{3,1},{4,2},{5,3},{6,4},{7,5},{8,6},{9,7},{10,8},{11,9},{12,... | collective-permute-start | bytes 1376264 | tf_op jit(solution)/shard_map/ppermute | solution.py:770
  17.3 18.4 %collective-permute-start.4 = (bf16[48,1280]{1,0:T(8,128)(2,1)S(1)}, bf16[48,1280]{1,0:T(8,128)(2,1)S(1)}, u32[]{:S(2)}, u32[]{:S(2)}) collective-permute-start(bf16[48,1280]{1,0:T(8,128)(2,1)S(1)} %pad_maximum_fusion.10), channel_id=1, source_target_pairs={{0,8},{1,9},{2,10},{3,11},{4,12},{5,13},{6,14},{7,15},{8,0},{9,1},... | collective-permute-start | bytes 368648 | tf_op jit(solution)/shard_map/ppermute | solution.py:759
  43.8 7.3 %collective-permute-start.6 = (bf16[2,2,48,640]{3,2,0,1:T(8,128)(2,1)S(1)}, bf16[2,2,48,640]{3,2,0,1:T(8,128)(2,1)}, u32[]{:S(2)}, u32[]{:S(2)}) collective-permute-start(bf16[2,2,48,640]{3,2,0,1:T(8,128)(2,1)S(1)} %get-tuple-element.165), channel_id=1, source_target_pairs={{0,2},{1,3},{2,0},{3,1},{4,6},{5,7},{6,4},{7,5},{8,10},{9,11},{10,... | collective-permute-start | bytes 737288 | tf_op jit(solution)/shard_map/ppermute | solution.py:759
  45.1 22.2 %collective-permute-start.2 = (bf16[3,256,896]{2,1,0:T(8,128)(2,1)}, bf16[3,256,896]{2,1,0:T(8,128)(2,1)S(1)}, u32[]{:S(2)}, u32[]{:S(2)}) collective-permute-start(bf16[3,256,896]{2,1,0:T(8,128)(2,1)} %pad_maximum_fusion.1), channel_id=1, source_target_pairs={{0,1},{1,0},{2,3},{3,2},{4,5},{5,4},{6,7},{7,6},{8,9},{9,8},{10,11... | collective-permute-start | bytes 4128776 | tf_op jit(solution)/shard_map/ppermute | solution.py:759
  49.7 11.0 %collective-permute-start.9 = (bf16[2,2,2,48,640]{4,3,1,2,0:T(8,128)(2,1)}, bf16[2,2,2,48,640]{4,3,1,2,0:T(8,128)(2,1)}, u32[]{:S(2)}, u32[]{:S(2)}) collective-permute-start(bf16[2,2,2,48,640]{4,3,1,2,0:T(8,128)(2,1)} %pad_maximum_fusion.6), channel_id=1, source_target_pairs={{0,2},{1,3},{2,0},{3,1},{4,6},{5,7},{6,4},{7,5},{8,10},{9,11},{10,... | collective-permute-start | bytes 1474568 | tf_op jit(solution)/shard_map/ppermute | solution.py:759
  52.2 13.8 %collective-permute-start.7 = (bf16[2,2,2,48,640]{4,3,0,1,2:T(8,128)(2,1)S(1)}, bf16[2,2,2,48,640]{4,3,0,1,2:T(8,128)(2,1)S(1)}, u32[]{:S(2)}, u32[]{:S(2)}) collective-permute-start(bf16[2,2,2,48,640]{4,3,0,1,2:T(8,128)(2,1)S(1)} %pad_maximum_fusion.5), channel_id=1, source_target_pairs={{0,16},{1,17},{2,18},{3,19},{4,20},{5,21},{6,22},{7,23},{8,24},{9,... | collective-permute-start | bytes 1474568 | tf_op jit(solution)/shard_map/ppermute | solution.py:759
  78.2 26.2 %all-to-all-start.1 = ((bf16[16,112,128]{2,1,0:T(8,128)(2,1)}), bf16[16,112,128]{2,1,0:T(8,128)(2,1)S(1)}, u32[]{:S(2)}, u32[]{:S(2)}) async-start(bf16[16,112,128]{2,1,0:T(8,128)(2,1)} %bitcast.127), calls=%async_computation.1 | async-start | bytes 917504 | tf_op jit(solution)/shard_map/all_to_all | solution.py:947
  104.5 19.2 %all-to-all-start = ((bf16[16,112,128]{2,1,0:T(8,128)(2,1)}), bf16[16,112,128]{2,1,0:T(8,128)(2,1)S(1)}, u32[]{:S(2)}, u32[]{:S(2)}) async-start(bf16[16,112,128]{2,1,0:T(8,128)(2,1)} %bitcast.125), calls=%async_computation | async-start | bytes 917504 | tf_op jit(solution)/shard_map/all_to_all | solution.py:947
  111.3 13.0 %collective-permute-start.11 = (f32[3,8,512]{2,1,0:T(8,128)S(1)}, f32[3,8,512]{2,1,0:T(8,128)S(1)}, u32[]{:S(2)}, u32[]{:S(2)}) collective-permute-start(f32[3,8,512]{2,1,0:T(8,128)S(1)} %copy-done.33), channel_id=1, source_target_pairs={{0,2},{1,3},{2,4},{3,5},{4,6},{5,7},{6,8},{7,9},{8,10},{9,11},{10,... | collective-permute-start | bytes 147464 | tf_op jit(solution)/shard_map/ppermute | solution.py:770
  115.1 9.2 %collective-permute-start.12 = (f32[3,8,512]{2,1,0:T(8,128)S(1)}, f32[3,8,512]{2,1,0:T(8,128)S(1)}, u32[]{:S(2)}, u32[]{:S(2)}) collective-permute-start(f32[3,8,512]{2,1,0:T(8,128)S(1)} %copy-done.33), channel_id=1, source_target_pairs={{2,0},{3,1},{4,2},{5,3},{6,4},{7,5},{8,6},{9,7},{10,8},{11,9},{12,... | collective-permute-start | bytes 147464 | tf_op jit(solution)/shard_map/ppermute | solution.py:770
  118.5 23.3 %collective-permute-start.14 = (bf16[288,768]{1,0:T(8,128)(2,1)}, bf16[288,768]{1,0:T(8,128)(2,1)S(1)}, u32[]{:S(2)}, u32[]{:S(2)}) collective-permute-start(bf16[288,768]{1,0:T(8,128)(2,1)} %shard_map.234.cot_ref), channel_id=1, source_target_pairs={{0,16},{1,17},{2,18},{3,19},{4,20},{5,21},{6,22},{7,23},{8,24},{9,... | collective-permute-start | bytes 1327112 | tf_op jit(solution)/shard_map/ppermute | solution.py:759
  123.7 18.1 %collective-permute-start.13 = (bf16[1792,128]{1,0:T(8,128)(2,1)S(1)}, bf16[1792,128]{1,0:T(8,128)(2,1)S(1)}, u32[]{:S(2)}, u32[]{:S(2)}) collective-permute-start(bf16[1792,128]{1,0:T(8,128)(2,1)S(1)} %bitcast.121), channel_id=1, source_target_pairs={{0,16},{1,17},{2,18},{3,19},{4,20},{5,21},{6,22},{7,23},{8,24},{9,... | collective-permute-start | bytes 1376264 | tf_op jit(solution)/shard_map/ppermute | solution.py:759
  137.8 21.4 %all-to-all-start.2 = ((bf16[16,112,128]{2,1,0:T(8,128)(2,1)}), bf16[16,112,128]{2,1,0:T(8,128)(2,1)S(1)}, u32[]{:S(2)}, u32[]{:S(2)}) async-start(bf16[16,112,128]{2,1,0:T(8,128)(2,1)} %bitcast.128), calls=%async_computation.2 | async-start | bytes 917504 | tf_op jit(solution)/shard_map/all_to_all | solution.py:947
  166.2 30.6 %collective-permute-start.25 = (bf16[256,384]{1,0:T(8,128)(2,1)S(1)}, bf16[256,384]{1,0:T(8,128)(2,1)S(1)}, u32[]{:S(2)}, u32[]{:S(2)}) collective-permute-start(bf16[256,384]{1,0:T(8,128)(2,1)S(1)} %copy-done.29), channel_id=1, source_target_pairs={{0,1},{1,0},{2,3},{3,2},{4,5},{5,4},{6,7},{7,6},{8,9},{9,8},{10,11... | collective-permute-start | bytes 589832 | tf_op jit(solution)/shard_map/ppermute | solution.py:759
  170.4 28.7 %collective-permute-start.16 = (bf16[512,384]{1,0:T(8,128)(2,1)}, bf16[512,384]{1,0:T(8,128)(2,1)S(1)}, u32[]{:S(2)}, u32[]{:S(2)}) collective-permute-start(bf16[512,384]{1,0:T(8,128)(2,1)} %get-tuple-element.79.gctx_ref), channel_id=1, source_target_pairs={{0,2},{1,3},{2,4},{3,5},{4,6},{5,7},{6,8},{7,9},{8,10},{9,11},{10,... | collective-permute-start | bytes 1179656 | tf_op jit(solution)/shard_map/ppermute | solution.py:770
  174.2 24.9 %collective-permute-start.17 = (bf16[512,384]{1,0:T(8,128)(2,1)}, bf16[512,384]{1,0:T(8,128)(2,1)S(1)}, u32[]{:S(2)}, u32[]{:S(2)}) collective-permute-start(bf16[512,384]{1,0:T(8,128)(2,1)} %get-tuple-element.79.gctx_ref), channel_id=1, source_target_pairs={{2,0},{3,1},{4,2},{5,3},{6,4},{7,5},{8,6},{9,7},{10,8},{11,9},{12,... | collective-permute-start | bytes 1179656 | tf_op jit(solution)/shard_map/ppermute | solution.py:770
  175.5 23.6 %collective-permute-start.18 = (f32[8,512]{1,0:T(8,128)}, f32[8,512]{1,0:T(8,128)S(1)}, u32[]{:S(2)}, u32[]{:S(2)}) collective-permute-start(f32[8,512]{1,0:T(8,128)} %get-tuple-element.82), channel_id=1, source_target_pairs={{0,2},{1,3},{2,4},{3,5},{4,6},{5,7},{6,8},{7,9},{8,10},{9,11},{10,... | collective-permute-start | bytes 49160 | tf_op jit(solution)/shard_map/ppermute | solution.py:770
  180.0 19.0 %collective-permute-start.19 = (f32[8,512]{1,0:T(8,128)}, f32[8,512]{1,0:T(8,128)S(1)}, u32[]{:S(2)}, u32[]{:S(2)}) collective-permute-start(f32[8,512]{1,0:T(8,128)} %get-tuple-element.82), channel_id=1, source_target_pairs={{2,0},{3,1},{4,2},{5,3},{6,4},{7,5},{8,6},{9,7},{10,8},{11,9},{12,... | collective-permute-start | bytes 49160 | tf_op jit(solution)/shard_map/ppermute | solution.py:770
  197.5 20.5 %collective-permute-start.26 = (bf16[2,2,2,48,384]{4,3,1,0,2:T(8,128)(2,1)S(1)}, bf16[2,2,2,48,384]{4,3,1,0,2:T(8,128)(2,1)S(1)}, u32[]{:S(2)}, u32[]{:S(2)}) collective-permute-start(bf16[2,2,2,48,384]{4,3,1,0,2:T(8,128)(2,1)S(1)} %fusion.18), channel_id=1, source_target_pairs={{0,16},{1,17},{2,18},{3,19},{4,20},{5,21},{6,22},{7,23},{8,24},{9,... | collective-permute-start | bytes 884744 | tf_op jit(solution)/shard_map/ppermute | solution.py:759
  223.2 19.6 %collective-permute-start.27 = (bf16[2,2,48,384]{3,2,1,0:T(8,128)(2,1)}, bf16[2,2,48,384]{3,2,1,0:T(8,128)(2,1)}, u32[]{:S(2)}, u32[]{:S(2)}) collective-permute-start(bf16[2,2,48,384]{3,2,1,0:T(8,128)(2,1)} %fusion.23), channel_id=1, source_target_pairs={{0,2},{1,3},{2,0},{3,1},{4,6},{5,7},{6,4},{7,5},{8,10},{9,11},{10,... | collective-permute-start | bytes 442376 | tf_op jit(solution)/shard_map/ppermute | solution.py:759
  224.1 7.4 %collective-permute-start.34 = (f32[6,128]{1,0:T(8,128)S(1)}, f32[6,128]{1,0:T(8,128)S(1)}, u32[]{:S(2)}, u32[]{:S(2)}) collective-permute-start(f32[6,128]{1,0:T(8,128)S(1)} %add.177), channel_id=1, source_target_pairs={{0,16},{1,17},{2,18},{3,19},{4,20},{5,21},{6,22},{7,23},{8,24},{9,... | collective-permute-start | bytes 9224 | tf_op jit(solution)/shard_map/ppermute | solution.py:759
  229.0 10.9 %collective-permute-start.20 = (bf16[384,640]{1,0:T(8,128)(2,1)}, bf16[384,640]{1,0:T(8,128)(2,1)S(1)}, u32[]{:S(2)}, u32[]{:S(2)}) collective-permute-start(bf16[384,640]{1,0:T(8,128)(2,1)} %get-tuple-element.91.later_ref), channel_id=1, source_target_pairs={{0,16},{1,17},{2,18},{3,19},{4,20},{5,21},{6,22},{7,23},{8,24},{9,... | collective-permute-start | bytes 1474568 | tf_op jit(solution)/shard_map/ppermute | solution.py:759
  230.4 11.6 %collective-permute-start.23 = (bf16[384,640]{1,0:T(8,128)(2,1)}, bf16[384,640]{1,0:T(8,128)(2,1)S(1)}, u32[]{:S(2)}, u32[]{:S(2)}) collective-permute-start(bf16[384,640]{1,0:T(8,128)(2,1)} %get-tuple-element.97), channel_id=1, source_target_pairs={{0,2},{1,3},{2,0},{3,1},{4,6},{5,7},{6,4},{7,5},{8,10},{9,11},{10,... | collective-permute-start | bytes 1474568 | tf_op jit(solution)/shard_map/ppermute | solution.py:759
  231.6 7.7 %collective-permute-start.35 = (f32[6,128]{1,0:T(8,128)S(1)}, f32[6,128]{1,0:T(8,128)S(1)}, u32[]{:S(2)}, u32[]{:S(2)}) collective-permute-start(f32[6,128]{1,0:T(8,128)S(1)} %add.178), channel_id=1, source_target_pairs={{0,1},{1,0},{2,3},{3,2},{4,5},{5,4},{6,7},{7,6},{8,9},{9,8},{10,11... | collective-permute-start | bytes 9224 | tf_op jit(solution)/shard_map/ppermute | solution.py:759
  233.6 30.8 %all-to-all-start.3 = ((bf16[16,112,128]{2,1,0:T(8,128)(2,1)}), bf16[16,112,128]{2,1,0:T(8,128)(2,1)S(1)}, u32[]{:S(2)}, u32[]{:S(2)}) async-start(bf16[16,112,128]{2,1,0:T(8,128)(2,1)} %bitcast.124), calls=%async_computation.3 | async-start | bytes 917504 | tf_op jit(solution)/shard_map/all_to_all | solution.py:947
  240.0 12.1 %collective-permute-start.22 = (bf16[2,2,48,640]{3,2,1,0:T(8,128)(2,1)S(1)}, bf16[2,2,48,640]{3,2,1,0:T(8,128)(2,1)S(1)}, u32[]{:S(2)}, u32[]{:S(2)}) collective-permute-start(bf16[2,2,48,640]{3,2,1,0:T(8,128)(2,1)S(1)} %fusion.19), channel_id=1, source_target_pairs={{0,2},{1,3},{2,0},{3,1},{4,6},{5,7},{6,4},{7,5},{8,10},{9,11},{10,... | collective-permute-start | bytes 737288 | tf_op jit(solution)/shard_map/ppermute | solution.py:759
  242.2 10.1 %collective-permute-start.24 = (bf16[2,2,48,640]{3,2,1,0:T(8,128)(2,1)S(1)}, bf16[2,2,48,640]{3,2,1,0:T(8,128)(2,1)S(1)}, u32[]{:S(2)}, u32[]{:S(2)}) collective-permute-start(bf16[2,2,48,640]{3,2,1,0:T(8,128)(2,1)S(1)} %fusion.20), channel_id=1, source_target_pairs={{0,16},{1,17},{2,18},{3,19},{4,20},{5,21},{6,22},{7,23},{8,24},{9,... | collective-permute-start | bytes 737288 | tf_op jit(solution)/shard_map/ppermute | solution.py:759
  252.4 8.8 %collective-permute-start.28 = (bf16[2,48,1664]{2,1,0:T(8,128)(2,1)S(1)}, bf16[2,48,1664]{2,1,0:T(8,128)(2,1)S(1)}, u32[]{:S(2)}, u32[]{:S(2)}) collective-permute-start(bf16[2,48,1664]{2,1,0:T(8,128)(2,1)S(1)} %fusion.17), channel_id=1, source_target_pairs={{0,4},{1,5},{2,6},{3,7},{4,0},{5,1},{6,2},{7,3},{8,12},{9,13},{10,... | collective-permute-start | bytes 958472 | tf_op jit(solution)/shard_map/ppermute | solution.py:759
  258.4 12.4 %collective-permute-start.21 = (f32[256,768]{1,0:T(8,128)}, f32[256,768]{1,0:T(8,128)S(1)}, u32[]{:S(2)}, u32[]{:S(2)}) collective-permute-start(f32[256,768]{1,0:T(8,128)} %get-tuple-element.95), channel_id=1, source_target_pairs={{0,1},{1,0},{2,3},{3,2},{4,5},{5,4},{6,7},{7,6},{8,9},{9,8},{10,11... | collective-permute-start | bytes 2359304 | tf_op jit(solution)/shard_map/ppermute | solution.py:759
  261.3 9.3 %collective-permute-start.29 = (bf16[48,1664]{1,0:T(8,128)(2,1)S(1)}, bf16[48,1664]{1,0:T(8,128)(2,1)S(1)}, u32[]{:S(2)}, u32[]{:S(2)}) collective-permute-start(bf16[48,1664]{1,0:T(8,128)(2,1)S(1)} %fusion.22), channel_id=1, source_target_pairs={{0,8},{1,9},{2,10},{3,11},{4,12},{5,13},{6,14},{7,15},{8,0},{9,1},... | collective-permute-start | bytes 479240 | tf_op jit(solution)/shard_map/ppermute | solution.py:759
  (45 other events, 224.8 us)
Sparse Core Ops, SparseCore 0:
  16.2 56.9 all-gather.1
where the time goes:
time: 285 us; the launch traced here: 283 us
  Pallas kernels  105 us (37%)
  starting transfers between devices  73.1 us (26%)
  waiting for transfers between devices  57.6 us (20%)
  local copies, waits for them, and re-layouts  15.9 us (6%)
  other arithmetic  15.6 us (5%)
  between operations  14.9 us (5%)
    pallas_call x16, Pallas kernels, call(): pl.pallas_call(kernel, out_shape=shapes, grid=grid if grid is not None el...  105 us
    ppermute x28, waiting for transfers between devices, swap(): return lax.ppermute(value, AXES, pairs)  52.8 us
    ppermute x28, starting transfers between devices, swap(): return lax.ppermute(value, AXES, pairs)  31.3 us
    ppermute x8, starting transfers between devices, shift(): return lax.ppermute(value, AXES, pairs)  22.6 us
    all_to_all x4, starting transfers between devices, exchange(): lax.all_to_all(message, 'ctx', split_axis=0, concat_axis=0, tiled=True)  19.2 us
    unnamed x76, local copies, waits for them, and re-layouts  8.09 us
  transfers between devices with their start and end apart: 41, of which 15 were waited for; matrix products, arithmetic and copies ran while one was open for 7% of the time, Pallas kernels for 35%

commit v1 on v0

--- a/solution.py
+++ b/solution.py
@@ -14,6 +14,9 @@
 BLK = 256
 LANES = 128
 FAR = 91
+CHUNK = 32
+TABLE = 32
+CODE_ROWS = 16
 GELU_A = 0.7978845608028654
 GELU_B = 0.044715
 
@@ -70,7 +73,7 @@
     return high, middle, (rest - middle.astype(F32)).astype(BF16)
 
 
-def fill_message(out_ref, flat_ref, msg_ref, cap, depth, values=None):
+def fill_message(out_ref, flat_ref, msg_ref, cap, depth, values=None, turn=0, turns=1):
     groups = flat_ref.shape[0] // cap
     parts = flat_ref.shape[1] // LANES
     for group in range(groups):
@@ -86,13 +89,24 @@
         if values is not None:
             for part, piece in enumerate(values):
                 msg_ref[first + part : first + part + 1, :] = piece[group : group + 1, :]
-    out_ref[...] = msg_ref[...].astype(BF16)
-
-
-def read_message(message, flat_ref, msg_ref, cap, depth):
+    if turns == 1:
+        out_ref[...] = msg_ref[...].astype(BF16)
+        return
+    for group in range(groups):
+        first = (group * turns + turn) * depth
+        out_ref[first : first + depth, :] = msg_ref[
+            group * depth : (group + 1) * depth, :
+        ].astype(BF16)
+
+
+def read_message(message_ref, flat_ref, msg_ref, cap, depth, turn=0, turns=1, start=0):
     groups = flat_ref.shape[0] // cap
     parts = flat_ref.shape[1] // LANES
-    msg_ref[...] = message.astype(F32)
+    for group in range(groups):
+        first = start + (group * turns + turn) * depth
+        msg_ref[group * depth : (group + 1) * depth, :] = message_ref[
+            first : first + depth, :
+        ].astype(F32)
     values = []
     for group in range(groups):
         for part in range(parts):
@@ -138,7 +152,7 @@
 
 
 def rows_kernel(cap, depth, message_ref, out_ref, flat, msg):
-    read_message(message_ref[...], flat, msg, cap, depth)
+    read_message(message_ref, flat, msg, cap, depth)
     out_ref[...] = flat[...].astype(BF16)
 
 
@@ -147,29 +161,84 @@
     return nt(pick, columns)
 
 
-def qkv_kernel(experts, x_ref, wa_ref, wb_ref, hid_ref, q_ref, k_ref, v_ref, gain_ref):
-    half = q_ref.shape[1]
-    split = wa_ref.shape[1]
-    cut = split - half
-    gains = picked_rows(wb_ref[:, split - LANES :], experts)
-    gain_ref[...] = gains
-    tokens = x_ref[...].astype(F32)
-    scale = lax.rsqrt(jnp.mean(tokens * tokens, axis=-1, keepdims=True) + EPSILON)
-    hidden = (tokens * scale * gains[0:1, :]).astype(BF16)
-    hid_ref[...] = hidden
-    first = nn(hidden, wa_ref[...]).astype(BF16)
-    second = nn(hidden, wb_ref[:, : split - LANES]).astype(BF16)
-    q_ref[...] = first[:, :half]
-    k_ref[:, :cut] = first[:, half:]
-    k_ref[:, cut:] = second[:, : half - cut]
-    v_ref[...] = second[:, half - cut :]
-
-
-def bias_kernel(table_ref, later_ref, bias_ref, prev_ref, next_ref):
-    del later_ref
+def extend_kernel(x_ref, seg_ref, out_ref):
+    tok, width = x_ref.shape
+    out_ref[:tok, :] = x_ref[...]
+    code = (seg_ref[...] + 1).astype(F32)
+    code = jnp.concatenate([code, jnp.zeros((1, width - tok), F32)], axis=1)
+    out_ref[tok:, :] = jnp.broadcast_to(code, (CODE_ROWS, width)).astype(BF16)
+
+
+def arrange_kernel(where_ref, *refs):
+    count = len(refs) - 8
+    pieces, (before_ref, own_ref, after_ref) = refs[:count], refs[count : count + 3]
+    a_ref, b_ref, o_ref, three_ref = refs[count + 4 :]
+    rows, split = pieces[0].shape[0], a_ref.shape[1]
+    for other, ref in enumerate(pieces):
+        place = pl.ds(pl.multiple_of((where_ref[5] ^ other) * rows, 16), rows)
+        a_ref[place, :] = ref[:, :split]
+        b_ref[place, :] = ref[:, split : 2 * split]
+        o_ref[place, :] = ref[:, 2 * split :]
+    tok = own_ref.shape[0]
+    for place, ref in enumerate((before_ref, own_ref, after_ref)):
+        three_ref[place * tok : (place + 1) * tok, :] = ref[...]
+
+
+def stack_kernel(before_ref, own_ref, after_ref, out_ref):
+    tok = own_ref.shape[0]
+    for place, ref in enumerate((before_ref, own_ref, after_ref)):
+        out_ref[place * tok : (place + 1) * tok, :] = ref[...]
+
+
+def prepare_kernel(
+    cap,
+    experts,
+    where_ref,
+    table_ref,
+    route_col_ref,
+    route_row_ref,
+    bias_ref,
+    prev_ref,
+    next_ref,
+    far_ref,
+    col_ref,
+    row_ref,
+):
+    own_heads = bias_ref.shape[0]
+    pick = iota((8, 2 * own_heads), 1) == iota((8, 2 * own_heads), 0) + where_ref[0] * own_heads
+    table = nt(pick.astype(BF16), table_ref[...])
+    far_ref[...] = jnp.concatenate(
+        [table, jnp.zeros((8, LANES - table.shape[1]), F32)], axis=1
+    )
+    fill_bias(table.astype(BF16), bias_ref, prev_ref, next_ref)
+    tok = route_col_ref.shape[0]
+    route_col = route_col_ref[...]
+    route_row = route_row_ref[...]
+    hot_col = route_col == iota((tok, LANES), 1)
+    earlier = (iota((tok, tok), 1) < iota((tok, tok), 0)).astype(BF16)
+    count = nn(earlier, hot_col.astype(F32).astype(BF16))
+    slot_col = jnp.sum(jnp.where(hot_col, count, 0.0), axis=1, keepdims=True).astype(jnp.int32)
+    lane = iota((tok, LANES), 1)
+    col_ref[...] = jnp.where(
+        lane == 0,
+        route_col * cap + slot_col,
+        jnp.where(lane == 1, route_col, jnp.where(lane == 2, slot_col, 0)),
+    )
+    hot_row = iota((experts, tok), 0) == route_row
+    later = (iota((tok, tok), 0) < iota((tok, tok), 1)).astype(BF16)
+    count = nn(hot_row.astype(F32).astype(BF16), later)
+    slot_row = jnp.sum(jnp.where(hot_row, count, 0.0), axis=0, keepdims=True).astype(jnp.int32)
+    line = iota((8, tok), 0)
+    row_ref[...] = jnp.where(
+        line == 0,
+        route_row * cap + slot_row,
+        jnp.where(line == 1, route_row, jnp.where(line == 2, slot_row, 0)),
+    )
+
+
+def fill_bias(table, bias_ref, prev_ref, next_ref):
     heads, near = bias_ref.shape[0], bias_ref.shape[2]
     wide = near + BLK
-    table = table_ref[...]
     buckets = table.shape[1]
     apart = iota((buckets, wide), 1) - (wide // 2)
     ahead = nn(table, (bucket_of(apart) == iota((buckets, wide), 0)).astype(BF16))
@@ -193,11 +262,10 @@
     return jnp.where(keep, value, jnp.zeros_like(value))
 
 
-def scores_of(query, keys, bias, left, right, mask):
-    raw = nt(query, keys)
+def masked_scores(raw, bias, left, right, mask):
     near = bias.shape[1]
-    edge = (keys.shape[0] - near) // 2
-    raw = jnp.concatenate(
+    edge = (raw.shape[1] - near) // 2
+    added = jnp.concatenate(
         [
             raw[:, :edge] + left,
             raw[:, edge : edge + near] + bias.astype(F32),
@@ -205,43 +273,159 @@
         ],
         axis=1,
     )
-    return jnp.where(mask, raw, NEGATIVE)
-
-
-def attend_kernel(
-    far_ref, q_ref, k_ref, v_ref, bias_ref, code_ref, ctx_ref, low_ref, lse_ref, lse_row_ref
+    return jnp.where(mask, added, NEGATIVE)
+
+
+def join_weights(chip_rows, bits_ref, pieces, wa_ref, wb_ref):
+    if len(pieces) == 2:
+        wa_ref[...] = pieces[0][...]
+        wb_ref[...] = pieces[1][...]
+        return
+    rows = pieces[0].shape[0]
+    for turn in range(2):
+        place = bits_ref[1] if turn == 0 else 1 - bits_ref[1]
+        wa_ref[pl.ds(pl.multiple_of(place * rows, rows), rows), :] = pieces[turn][...]
+        place = bits_ref[2] if turn == 0 else 1 - bits_ref[2]
+        for group in range(rows // chip_rows):
+            first = pl.multiple_of(group * 2 * chip_rows + place * chip_rows, 16)
+            wb_ref[pl.ds(first, chip_rows), :] = pieces[2 + turn][
+                group * chip_rows : (group + 1) * chip_rows, :
+            ]
+
+
+def forward_kernel(experts, chip_rows, count, far_ref, where_ref, *refs):
+    forward_body(experts, chip_rows, far_ref, where_ref, refs[:count], *refs[count:])
+
+
+def forward_body(
+    experts,
+    chip_rows,
+    far_ref,
+    where_ref,
+    pieces,
+    x_ref,
+    came_ref,
+    code_own_ref,
+    code_came_ref,
+    bias_ref,
+    earlier_ref,
+    hid_ref,
+    q_ref,
+    k_ref,
+    v_ref,
+    gain_ref,
+    low_ref,
+    lse_ref,
+    wa_ref,
+    wb_ref,
+    code_ref,
+    q_all,
+    k_all,
+    v_all,
+    code_row,
+    raw,
+    prob,
 ):
-    pair = pl.program_id(0)
-    own = q_ref.shape[0]
-    window = 5 * BLK
-    lane = iota((BLK, LANES), 1)
-    code_row = picked_rows(code_ref[...], 0)
-    lse_row_ref[...] = jnp.zeros_like(lse_row_ref)
-    for block in range(own // BLK):
-        rows = slice(block * BLK, (block + 1) * BLK)
-        cols = slice(block * BLK, block * BLK + window)
-        query = q_ref[rows, :]
-        keys = k_ref[cols, :]
-        values = v_ref[cols, :]
-        code_col = code_ref[own + block * BLK : own + (block + 1) * BLK, 0:1].astype(F32)
-        mask = code_col == code_row[0:1, cols]
-        outs = []
-        logs = jnp.zeros((BLK, LANES), F32)
-        for turn in range(2):
-            head = pair * 2 + turn
-            scores = scores_of(
-                own_half(query, turn), keys, bias_ref[turn], far_ref[0, head], far_ref[1, head], mask
-            )
-            top = jnp.max(scores, axis=1, keepdims=True)
-            weight = jnp.exp(scores - top)
-            total = jnp.sum(weight, axis=1, keepdims=True)
-            outs.append(nn((weight * (1.0 / total)).astype(BF16), values))
-            logs = jnp.where(lane == turn, top + jnp.log(total), logs)
-        context = jnp.where(lane < LANES // 2, outs[0], outs[1])
-        ctx_ref[rows, :] = context
-        low_ref[rows, :] = context.astype(BF16)
-        lse_ref[rows, :] = logs
-        lse_row_ref[0, 0:2, rows] = jnp.transpose(logs)[0:2, :]
+    del earlier_ref
+    step = pl.program_id(0)
+    own, half = q_ref.shape
+    split = wa_ref.shape[1]
+    cut = split - half
+    core = where_ref[0]
+    tok = x_ref.shape[0] - CODE_ROWS
+
+    @pl.when(step == 0)
+    def _():
+        join_weights(chip_rows, where_ref, pieces, wa_ref, wb_ref)
+        for chip in range(3):
+            for ref, which in ((code_own_ref, core), (code_came_ref, 1 - core)):
+                first = pl.multiple_of(chip * own + which * tok, tok)
+                row = chip * (tok + CODE_ROWS) + tok
+                pick = (iota((CODE_ROWS, LANES), 0) == 0).astype(BF16)
+                code_ref[pl.ds(first, tok), :] = tn(ref[row : row + CODE_ROWS, :], pick).astype(BF16)
+        gain_ref[...] = picked_rows(wb_ref[:, split - LANES :], experts)
+        code_row[...] = picked_rows(code_ref[...], 0)
+
+    @pl.when(step < 3)
+    def _():
+        for ref, which in ((x_ref, core), (came_ref, 1 - core)):
+            tokens = ref[:tok, :].astype(F32)
+            scale = lax.rsqrt(jnp.mean(tokens * tokens, axis=-1, keepdims=True) + EPSILON)
+            hid_ref[pl.ds(pl.multiple_of(which * tok, tok), tok), :] = (
+                tokens * scale * gain_ref[0:1, :]
+            ).astype(BF16)
+        hidden = hid_ref[...]
+        second = nn(hidden, wb_ref[:, : split - LANES]).astype(BF16)
+        k_ref[:, :cut] = nn(hidden, wa_ref[:, half:]).astype(BF16)
+        k_ref[:, cut:] = second[:, : half - cut]
+        v_ref[...] = second[:, half - cut :]
+        rows = pl.ds(pl.multiple_of(step * own, own), own)
+        k_all[rows, :] = k_ref[...]
+        v_all[rows, :] = v_ref[...]
+
+        @pl.when(step == 1)
+        def _():
+            query = nn(hidden, wa_ref[:, :half]).astype(BF16)
+            q_ref[...] = query
+            q_all[...] = query
+
+    @pl.when(step >= 3)
+    def _():
+        pair = step - 3
+        lanes = pl.ds(pl.multiple_of(pair * LANES, LANES), LANES)
+        window = 5 * BLK
+        lane = iota((BLK, LANES), 1)
+        lse_ref[...] = jnp.zeros_like(lse_ref)
+        for block in range(own // BLK):
+            rows = slice(block * BLK, (block + 1) * BLK)
+            cols = slice(block * BLK, block * BLK + window)
+            query = q_all[rows, lanes]
+            keys = k_all[cols, lanes]
+            values = v_all[cols, lanes]
+            outs = []
+            for turn in range(2):
+                raw[turn] = nt(own_half(query, turn), keys)
+            logs = jnp.zeros((BLK, LANES), F32)
+            for turn in range(2):
+                head = pair * 2 + turn
+                found = []
+                for first in range(0, BLK, CHUNK):
+                    part = slice(first, first + CHUNK)
+                    here = own + block * BLK + first
+                    mask = code_ref[here : here + CHUNK, 0:1].astype(F32) == code_row[0:1, cols]
+                    scores = masked_scores(
+                        raw[turn, part, :],
+                        bias_ref[turn, part, :],
+                        far_ref[pl.ds(head, 1), 15:16],
+                        far_ref[pl.ds(head, 1), 31:32],
+                        mask,
+                    )
+                    top = jnp.max(scores, axis=1, keepdims=True)
+                    weight = jnp.exp(scores - top)
+                    total = jnp.sum(weight, axis=1, keepdims=True)
+                    prob[turn, part, :] = (weight * (1.0 / total)).astype(BF16)
+                    found.append(top + jnp.log(total))
+                outs.append(nn(prob[turn], values))
+                logs = jnp.where(lane == turn, jnp.concatenate(found, axis=0), logs)
+            low_ref[rows, :] = jnp.where(lane < LANES // 2, outs[0], outs[1]).astype(BF16)
+            lse_ref[0, 0:2, rows] = jnp.transpose(logs)[0:2, :]
+
+
+def halo_query_kernel(hid_ref, wa_ref, q_ref):
+    q_ref[...] = nn(hid_ref[...], wa_ref[:, : q_ref.shape[1]]).astype(BF16)
+
+
+def turned(rows):
+    parts = jnp.concatenate([piece.astype(F32) for piece in three_parts(rows)], axis=0)
+    pick = iota((3 * rows.shape[0], LANES), 0) % rows.shape[0] == iota(
+        (3 * rows.shape[0], LANES), 1
+    )
+    return tn(parts.astype(BF16), pick.astype(BF16))
+
+
+def delta_rows(parts):
+    parts = parts.astype(F32)
+    return parts[0:8] + parts[8:16] + parts[16:24]
 
 
 def rolled_left(value, steps):
@@ -263,8 +447,7 @@
     q_ref,
     k_ref,
     v_ref,
-    gctx_ref,
-    ctx_ref,
+    msg_ref,
     lse_ref,
     bias_ref,
     code_ref,
@@ -272,57 +455,84 @@
     dk_ref,
     dv_ref,
     tab_ref,
+    raw,
+    grown,
+    prob,
+    grads,
+    near_sum,
 ):
     pair = pl.program_id(0)
-    blocks = q_ref.shape[0] // BLK
+    own = q_ref.shape[0]
+    blocks = own // BLK
+    deep = msg_ref.shape[0] // blocks
     window = 5 * BLK
     near = bias_ref.shape[2]
     edge = (window - near) // 2
+    lanes = pl.ds(pl.multiple_of(pair * LANES, LANES), LANES)
     lane = iota((BLK, LANES), 1)
-    own = q_ref.shape[0]
     code_row = picked_rows(code_ref[...], 0)
     dk_ref[...] = jnp.zeros_like(dk_ref)
     dv_ref[...] = jnp.zeros_like(dv_ref)
-    near_sum = [jnp.zeros((BLK, near), F32), jnp.zeros((BLK, near), F32)]
-    left_sum = [jnp.zeros((BLK, edge), F32), jnp.zeros((BLK, edge), F32)]
-    right_sum = [jnp.zeros((BLK, edge), F32), jnp.zeros((BLK, edge), F32)]
+    side = iota((window, LANES), 0)
+    side_lane = iota((window, LANES), 1)
+    ends = ((side < edge) & (side_lane == 0)) | ((side >= edge + near) & (side_lane == 1))
+    ends = ends.astype(BF16)
+    end_sums = [jnp.zeros((1, LANES), F32), jnp.zeros((1, LANES), F32)]
     for block in range(blocks):
         rows = slice(block * BLK, (block + 1) * BLK)
         cols = slice(block * BLK, block * BLK + window)
         keys = k_ref[cols, :]
         values = v_ref[cols, :]
-        code_col = code_ref[own + block * BLK : own + (block + 1) * BLK, 0:1].astype(F32)
-        mask = code_col == code_row[0:1, cols]
+        keys_ends = jnp.concatenate([keys, ends], axis=1)
         mine = slice((blocks - block) * BLK, (2 * blocks - block) * BLK)
-        gctx_all = gctx_ref[rows, :]
-        product = gctx_all.astype(F32) * ctx_ref[rows, :]
-        logs = lse_ref[rows, :]
+        first = block * deep
+        gctx_all = msg_ref[first : first + BLK, lanes]
+        deltas = turned(delta_rows(msg_ref[first + BLK : first + BLK + 24, :BLK]))
+        logs = turned(lse_ref[0, :, rows])
         outs = []
         for turn in range(2):
+            raw[turn] = nt(own_half(q_ref[rows, :], turn), keys)
+            grown[turn] = nt(own_half(gctx_all, turn), values)
+        for turn in range(2):
             head = pair * 2 + turn
+            delta = jnp.sum(jnp.where(lane == head, deltas, 0.0), axis=1, keepdims=True)
+            log = logs[:, turn : turn + 1]
+            for start in range(0, BLK, CHUNK):
+                part = slice(start, start + CHUNK)
+                here = own + block * BLK + start
+                mask = code_ref[here : here + CHUNK, 0:1].astype(F32) == code_row[0:1, cols]
+                scores = masked_scores(
+                    raw[turn, part, :],
+                    bias_ref[turn, part, :],
+                    far_ref[pl.ds(head, 1), 15:16],
+                    far_ref[pl.ds(head, 1), 31:32],
+                    mask,
+                )
+                probs = jnp.exp(scores - log[part])
+                low = (probs * (grown[turn, part, :] - delta[part])).astype(BF16)
+                prob[turn, part, :] = probs.astype(BF16)
+                grads[turn, part, :] = low
+                wide = low[:, edge : edge + near].astype(F32)
+                if block == 0:
+                    near_sum[turn, part, :] = wide
+                else:
+                    near_sum[turn, part, :] += wide
+        for turn in range(2):
             query = own_half(q_ref[rows, :], turn)
             gctx = own_half(gctx_all, turn)
-            scores = scores_of(
-                query, keys, bias_ref[turn], far_ref[0, head], far_ref[1, head], mask
-            )
-            probs = jnp.exp(scores - logs[:, turn : turn + 1])
-            delta = jnp.sum(own_half(product, turn), axis=1, keepdims=True)
-            grads = (probs * (nt(gctx, values) - delta)).astype(BF16)
-            outs.append(nn(grads, keys))
-            dk_ref[...] += tn(grads[:, mine], query)
-            dv_ref[...] += tn(probs[:, mine].astype(BF16), gctx)
-            wide = grads.astype(F32)
-            left_sum[turn] = left_sum[turn] + wide[:, :edge]
-            near_sum[turn] = near_sum[turn] + wide[:, edge : edge + near]
-            right_sum[turn] = right_sum[turn] + wide[:, edge + near :]
+            both = nn(grads[turn], keys_ends)
+            outs.append(both[:, :LANES])
+            end_sums[turn] = end_sums[turn] + jnp.sum(both[:, LANES:], axis=0, keepdims=True)
+            dk_ref[...] += tn(grads[turn, :, mine], query)
+            dv_ref[...] += tn(prob[turn, :, mine], gctx)
         dq_ref[rows, :] = jnp.where(lane < LANES // 2, outs[0], outs[1]).astype(BF16)
     apart = iota((BLK, near), 1) - (2 * BLK - edge) - iota((BLK, near), 0)
     tab_lane = iota((1, LANES), 1)
     hot = (bucket_of(iota((near, LANES), 0) - LANES) == iota((near, LANES), 1)).astype(F32)
     for turn in range(2):
         total = near_sum[turn]
-        left = jnp.sum(left_sum[turn]) + jnp.sum(jnp.where(apart <= -FAR, total, 0.0))
-        right = jnp.sum(right_sum[turn]) + jnp.sum(jnp.where(apart >= FAR, total, 0.0))
+        left = end_sums[turn][:, 0:1] + jnp.sum(jnp.where(apart <= -FAR, total, 0.0))
+        right = end_sums[turn][:, 1:2] + jnp.sum(jnp.where(apart >= FAR, total, 0.0))
         close = jnp.where(jnp.abs(apart) < FAR, total, 0.0)
         diagonal = diagonal_sums(close)
         sums = lax.dot_general(
@@ -346,23 +556,27 @@
     gn_ref,
     lp_ref,
     ln_ref,
-    deltap_ref,
-    deltan_ref,
     biasp_ref,
     biasn_ref,
     code_ref,
     dka_ref,
     dva_ref,
-    tab_in_ref,
     dk_ref,
     dv_ref,
-    tab_ref,
+    delta_ref,
 ):
     pair = pl.program_id(0)
     own = k_ref.shape[0]
     half = LANES
     code_row = picked_rows(code_ref[...], 0)
-    tab_ref[...] = tab_in_ref[...]
+    lanes = pl.ds(pl.multiple_of(pair * LANES, LANES), LANES)
+    deep = gp_ref.shape[0] // 2
+    for side, g_side in enumerate((gp_ref, gn_ref)):
+        for block in range(2):
+            first = block * deep + BLK
+            delta_ref[side, :, block * BLK : (block + 1) * BLK] = delta_rows(
+                g_side[first : first + 24, :BLK]
+            )
     total_k = dka_ref[...]
     total_v = dva_ref[...]
     parts = []
@@ -384,16 +598,16 @@
         values = v_ref[cols, :]
         count = cols.stop - cols.start
         lse_ref = lp_ref if side == 0 else ln_ref
-        delta_ref = deltap_ref if side == 0 else deltan_ref
+        places = slice(rows.start // BLK * deep, rows.start // BLK * deep + BLK)
         code_col = code_ref[own + cols.start : own + cols.stop, 0:1].astype(F32)
         first = 2 * own * side + rows.start
         mask = code_col == code_row[0:1, first : first + BLK]
         for turn in range(2):
             head = pair * 2 + turn
             query = own_half(q_side[rows, :], turn)
-            gctx = own_half(g_side[rows, :], turn)
+            gctx = own_half(g_side[places, lanes], turn)
             raw = nt(keys, query)
-            far = far_ref[1 - side, head]
+            far = far_ref[pl.ds(head, 1), 15:16] if side else far_ref[pl.ds(head, 1), 31:32]
             if far_block:
                 raw = raw + far
             elif side == 0:
@@ -407,7 +621,7 @@
                 )
             scores = jnp.where(mask, raw, NEGATIVE)
             logs = lse_ref[0, turn : turn + 1, rows]
-            delta = delta_ref[pl.ds(head, 1), rows]
+            delta = delta_ref[side, pl.ds(head, 1), rows]
             probs = jnp.exp(scores - logs)
             grads = (probs * (nt(values, gctx) - delta)).astype(BF16)
             got_k = nn(grads, query)
@@ -421,24 +635,6 @@
     dv_ref[...] = (total_v + jnp.concatenate(add_v, axis=0)).astype(BF16)
 
 
-def delta_kernel(core_ref, mine_ref, came_ref, ctx_ref, gctx_ref, delta_ref):
-    core = core_ref[0]
-    tok = mine_ref.shape[0]
-    width = mine_ref.shape[1]
-    gctx_ref[pl.ds(pl.multiple_of(core * tok, tok), tok), :] = mine_ref[...]
-    gctx_ref[pl.ds(pl.multiple_of((1 - core) * tok, tok), tok), :] = came_ref[...]
-    product = gctx_ref[...].astype(F32) * ctx_ref[...]
-    head_rows = delta_ref.shape[0]
-    pick = (iota((head_rows, width), 1) // (LANES // 2) == iota((head_rows, width), 0)).astype(F32)
-    delta_ref[...] = lax.dot_general(
-        pick,
-        product,
-        (((1,), (1,)), ((), ())),
-        precision=lax.Precision.HIGHEST,
-        preferred_element_type=F32,
-    )
-
-
 def token_columns(meta_ref, probs):
     route_hot = iota(probs.shape, 1) == meta_ref[:, 1:2]
     slot_hot = iota((probs.shape[0], LANES), 1) == meta_ref[:, 2:3]
@@ -454,7 +650,8 @@
     x_ref,
     own_ref,
     came_ref,
-    wo_ref,
+    wonear_ref,
+    wofar_ref,
     small_ref,
     gain_ref,
     meta_col_ref,
@@ -463,6 +660,7 @@
     hid_ref,
     prob_ref,
     msg_out_ref,
+    wo_ref,
     flat,
     msg,
 ):
@@ -470,11 +668,15 @@
     tok = x_ref.shape[0]
     width = own_ref.shape[1]
     rows = pl.ds(pl.multiple_of(core * tok, tok), tok)
+    side = core_ref[1]
+    wo_ref[pl.ds(pl.multiple_of(side * width, width), width), :] = wonear_ref[...]
+    wo_ref[pl.ds(pl.multiple_of((1 - side) * width, width), width), :] = wofar_ref[...]
     own_w = wo_ref[pl.ds(pl.multiple_of(core * width, width), width), :]
     other_w = wo_ref[pl.ds(pl.multiple_of((1 - core) * width, width), width), :]
-    attended = nn(own_ref[rows, :], own_w) + nn(came_ref[rows, :], other_w)
-    middle = x_ref[...].astype(F32) + attended
-    mid_ref[...] = middle
+    mid_ref[...] = (
+        x_ref[...].astype(F32) + nn(own_ref[rows, :], own_w) + nn(came_ref[rows, :], other_w)
+    )
+    middle = mid_ref[...]
     scale = lax.rsqrt(jnp.mean(middle * middle, axis=-1, keepdims=True) + EPSILON)
     hidden = (middle * scale * gain_ref[1:2, :]).astype(BF16)
     hid_ref[...] = hidden
@@ -511,24 +713,24 @@
     wout_ref,
     earlier_a_ref,
     earlier_b_ref,
+    earlier_c_ref,
     rows_ref,
     grad_ref,
     act_ref,
     gbef_ref,
-    made_ref,
     back_msg_ref,
     made_acc,
     back_acc,
     msg,
 ):
-    del earlier_a_ref, earlier_b_ref
+    del earlier_a_ref, earlier_b_ref, earlier_c_ref
     step = pl.program_id(0)
     count = rows_ref.shape[0]
     groups = count // cap
 
     @pl.when(step == 0)
     def _():
-        values = read_message(msg_ref[...], made_acc, msg, cap, depth)
+        values = read_message(msg_ref, made_acc, msg, cap, depth)
         rows_ref[...] = made_acc[...].astype(BF16)
         by_row, _, slot_hot = slot_places(count, groups, cap)
         gate = values_out(by_row, slot_hot, values)
@@ -551,19 +753,14 @@
     @pl.when(step == pl.num_programs(0) - 1)
     def _():
         produced = made_acc[...].astype(BF16)
-        made_ref[...] = produced
         grad_gate = jnp.sum(
             cot_ref[...].astype(F32) * produced.astype(F32), axis=1, keepdims=True
         )
         _, by_col, slot_hot = slot_places(count, groups, cap)
         values = values_in(by_col, slot_hot, grad_gate)
-        fill_message(back_msg_ref, back_acc, msg, cap, depth, values)
-
-
-def spread_kernel(cap, depth, rows_ref, later_ref, out_ref, flat, msg):
-    del later_ref
-    flat[...] = rows_ref[...].astype(F32)
-    fill_message(out_ref, flat, msg, cap, depth)
+        fill_message(back_msg_ref, back_acc, msg, cap, depth, values, 0, 2)
+        made_acc[...] = produced.astype(F32)
+        fill_message(back_msg_ref, made_acc, msg, cap, depth, None, 1, 2)
 
 
 def expert_grads_kernel(
@@ -593,8 +790,7 @@
         all_grad[:count, :] = grad_ref[...]
         by_row, _, slot_hot = slot_places(count, count // cap, cap)
         for other in range(msgs_ref.shape[0] // size):
-            message = msgs_ref[other * size : (other + 1) * size, :]
-            values = read_message(message, flat, msg, cap, depth)
+            values = read_message(msgs_ref, flat, msg, cap, depth, start=other * size)
             gate = values_out(by_row, slot_hot, values)
             first = (other + 1) * count
             all_rows[first : first + count, :] = flat[...].astype(BF16)
@@ -619,6 +815,7 @@
     dk_ref,
     dv_ref,
     extra_ref,
+    tab_ref,
     senda_ref,
     keepa_ref,
     sendb_ref,
@@ -630,8 +827,8 @@
     split = keepa_ref.shape[1]
     cut = split - half
     hidden = hid_ref[...]
-    bit_a = bits_ref[0]
-    bit_b = bits_ref[1]
+    bit_a = bits_ref[3]
+    bit_b = bits_ref[4]
     chunk = keepa_ref.shape[0]
     total[:, :half] = tn(hidden, dq_ref[...])
     total[:, half:] = tn(hidden, dk_ref[:, :cut])
@@ -641,12 +838,35 @@
     total[:, half - cut : split - LANES] = tn(hidden, dv_ref[...])
     total[:, split - LANES :] = extra_ref[...]
     chunk = chip_rows
+    table = jnp.concatenate([tab_ref[pair, 0:2, :] for pair in range(tab_ref.shape[0])], axis=0)
+    table = jnp.where(iota(table.shape, 1) < TABLE, table, 0.0)
+    table = pltpu.roll(table, LANES - TABLE, 1)
+    for index in range(2 * rows // chunk):
+        first = index * chunk // 2
+        total[first : first + table.shape[0], split - LANES :] += table
     for index in range(rows // (2 * chunk)):
         first = index * 2 * chunk
         out = slice(index * chunk, (index + 1) * chunk)
         keepb_ref[out, :] = total[pl.ds(pl.multiple_of(first + bit_b * chunk, 8), chunk), :]
         gone = total[pl.ds(pl.multiple_of(first + (1 - bit_b) * chunk, 8), chunk), :]
         sendb_ref[out, :] = gone.astype(BF16)
+
+
+def join_kernel(
+    chip_rows, where_ref, keepa_ref, camea_ref, keepb_ref, cameb_ref, keepo_ref, cameo_ref, later_ref, *refs
+):
+    del later_ref
+    kept_ref, total = refs[0], refs[-1]
+    first = 0
+    for kept, came in ((keepa_ref, camea_ref), (keepb_ref, cameb_ref), (keepo_ref, cameo_ref)):
+        last = first + kept.shape[1]
+        total[:, first:last] = kept[...] + came[...].astype(F32)
+        first = last
+    mine = where_ref[5]
+    kept_ref[...] = total[pl.ds(pl.multiple_of(mine * chip_rows, 8), chip_rows), :]
+    for other, ref in enumerate(refs[1:-1]):
+        place = mine ^ (other + 1)
+        ref[...] = total[pl.ds(pl.multiple_of(place * chip_rows, 8), chip_rows), :].astype(BF16)
 
 
 def input_kernel(core_ref, dq_ref, dk_ref, dv_ref, wa_ref, wb_ref, later_ref, keep_ref, send_ref):
@@ -680,6 +900,8 @@
     gain_ref,
     wo_ref,
     meta_ref,
+    own_ref,
+    came_ref,
     earlier_ref,
     gmid_ref,
     gmine_ref,
@@ -695,7 +917,7 @@
     core = core_ref[0]
     width = mine_ref.shape[1]
     tok = cot_ref.shape[0]
-    values = read_message(msg_in_ref[...], flat, msg, cap, depth)
+    values = read_message(msg_in_ref, flat, msg, cap, depth, 0, 2)
     hot = (iota((tok, flat.shape[0]), 1) == meta_ref[:, 0:1]).astype(BF16)
     came = nn(hot, flat[...].astype(BF16))
     probs = prob_ref[...]
@@ -714,12 +936,29 @@
     gmid_ref[...] = grad_middle
     low = grad_middle.astype(BF16)
     low_scr[...] = low
-    gmine_ref[...] = low_scr[:, pl.ds(pl.multiple_of(core * width, width), width)]
-    gtheirs_ref[...] = low_scr[:, pl.ds(pl.multiple_of((1 - core) * width, width), width)]
-    own_w = wo_ref[pl.ds(pl.multiple_of(core * width, width), width), :]
-    other_w = wo_ref[pl.ds(pl.multiple_of((1 - core) * width, width), width), :]
-    theirs_ref[...] = nt(low, other_w).astype(BF16)
-    mine_ref[...] = nt(low, own_w).astype(BF16)
+    own_heads = pl.ds(pl.multiple_of(core * width, width), width)
+    other_heads = pl.ds(pl.multiple_of((1 - core) * width, width), width)
+    gmine_ref[...] = low_scr[:, own_heads]
+    gtheirs_ref[...] = low_scr[:, other_heads]
+    rows = pl.ds(pl.multiple_of(core * tok, tok), tok)
+    pick = (iota((8, width), 1) // (LANES // 2) == iota((8, width), 0)).astype(F32)
+    for out_ref, heads, context in (
+        (theirs_ref, other_heads, came_ref[rows, :]),
+        (mine_ref, own_heads, own_ref[rows, :]),
+    ):
+        gctx = nt(low, wo_ref[heads, :]).astype(BF16)
+        delta = lax.dot_general(
+            pick,
+            gctx.astype(F32) * context.astype(F32),
+            (((1,), (1,)), ((), ())),
+            precision=lax.Precision.HIGHEST,
+            preferred_element_type=F32,
+        )
+        out_ref[:tok, :] = gctx
+        parts = [piece.astype(F32) for piece in three_parts(delta)]
+        parts = jnp.concatenate(parts + [jnp.zeros((8, tok), F32)], axis=0)
+        parts = jnp.concatenate([parts, jnp.zeros((32, width - tok), F32)], axis=1)
+        out_ref[tok:, :] = parts.astype(BF16)
     router = tn(hid_ref[...], grad_logits)
     gain = lax.dot_general(
         grad_hidden * normed,
@@ -734,7 +973,7 @@
 
 def output_kernel(cap, depth, msg_in_ref, mid_ref, prob_ref, meta_ref, out_ref, flat, msg):
     tok = out_ref.shape[0]
-    read_message(msg_in_ref[...], flat, msg, cap, depth)
+    read_message(msg_in_ref, flat, msg, cap, depth, 1, 2)
     hot = (iota((tok, flat.shape[0]), 1) == meta_ref[:, 0:1]).astype(BF16)
     combined = nn(hot, flat[...].astype(BF16))
     _, _, gate = token_columns(meta_ref, prob_ref[...])
@@ -777,15 +1016,33 @@
         axis = sum(1 for other in done if other > bit)
         return self.ordered(block, self.swap(block, bit), bit, axis, jnp.stack), done + [bit]
 
+    def several(self, bits):
+        index = 0
+        for bit in bits:
+            index = index * 2 + self.bit(bit)
+        masks = []
+        for other in range(1, 1 << len(bits)):
+            mask = sum(((other >> (len(bits) - 1 - at)) & 1) << bit for at, bit in enumerate(bits))
+            masks.append((other, mask))
+        return index, masks
+
+    def swap_mask(self, value, mask):
+        return lax.ppermute(value, AXES, [(i, i ^ mask) for i in range(self.count)])
+
     def gather(self, block, order, done=()):
         done = list(done)
         for bit in order:
             block, done = self.stage(block, bit, done)
         return block.reshape((-1,) + block.shape[len(done) + 1 :])
 
-    def scatter_on(self, gone, kept, order, first, keep):
-        value = kept + self.swap(gone, first).astype(F32)
-        return value, self.scatter(value, order, keep)
+    def halves(self, value, bit, order):
+        left = sorted(order, reverse=True)
+        axis = left.index(bit)
+        value = value.reshape((2,) * len(left) + (-1, value.shape[-1]))
+        gone = lax.dynamic_index_in_dim(value, 1 - self.bit(bit), axis, keepdims=False)
+        kept = lax.dynamic_index_in_dim(value, self.bit(bit), axis, keepdims=False)
+        flat = (-1, value.shape[-1])
+        return gone.astype(BF16).reshape(flat), kept.reshape(flat)
 
     def scatter(self, value, order, keep=()):
         left = sorted(list(order) + list(keep), reverse=True)
@@ -856,7 +1113,6 @@
 ):
     place = Place()
     core = place.core
-    core_arg = core.reshape(1).astype(jnp.int32)
     x = inputs[0]
     cot = cotangent[0]
     tok, width = x.shape
@@ -877,7 +1133,17 @@
     rows_all = 6 * tok
     own_rows = 2 * tok
 
-    wo = lax.all_gather(w_output, AXES, axis=0, tiled=True)
+    where = jnp.stack(
+        [
+            core,
+            place.bit(seq_bits[-1]),
+            place.bit(near_bits[-1]),
+            place.bit(seq_bits[0]),
+            place.bit(near_bits[0]),
+            place.several(far)[0],
+        ]
+    ).astype(jnp.int32)
+
     small_w = jnp.concatenate(
         [
             w_router,
@@ -889,7 +1155,8 @@
     )
     both = [
         jnp.concatenate(
-            [w[:, side * half : (side + 1) * half] for w in (w_query, w_key, w_value)] + [small_w],
+            [w[:, side * half : (side + 1) * half] for w in (w_query, w_key, w_value)]
+            + [small_w, w_output[:, side * half : (side + 1) * half]],
             axis=1,
         )
         for side in range(2)
@@ -897,86 +1164,173 @@
     ours = jnp.where(core == 0, both[0], both[1])
     theirs = jnp.where(core == 0, both[1], both[0])
     block = place.ordered(ours, place.swap(theirs, 0), 0, 0, jnp.concatenate)
-    done = []
-    for bit in far:
-        block, done = place.stage(block, bit, done)
-    split = block.shape[-1] // 2
-    later_a, done_a = block[..., :split], done
-    for bit in near_bits:
-        later_a, done_a = place.stage(later_a, bit, done_a)
-    w_a = place.gather(later_a, seq_bits, done_a)
-    w_b = place.gather(block[..., split:], seq_bits + near_bits, done)
-
-    code = (segments[0] + 1).astype(BF16)
-    x_ext = jnp.concatenate([x, jnp.broadcast_to(code[:, None], (tok, LANES))], axis=1)
-    before_x = place.shift(x_ext, 2)
-    after_x = place.shift(x_ext, -2)
-    three = jnp.stack([before_x, x_ext, after_x])
-    three_came = place.swap(three, 0)
-    x_all = place.ordered(three, three_came, 0, 1, jnp.concatenate).reshape(
-        rows_all, width + LANES
-    )
-    code_block = pl.BlockSpec((rows_all, LANES), lambda *_: (0, parts))
-
+    chip_rows = 2 * rows_dev
+    halved = chip_rows % 16 == 0
+    split = (block.shape[-1] - half) // 2
+    long = tok + CODE_ROWS
+    x_ext = call(extend_kernel, [((long, width), BF16)], x, segments)[0]
+    around = (place.shift(x_ext, 2), x_ext, place.shift(x_ext, -2))
     near = 2 * BLK
-    table_mine = lax.dynamic_slice_in_dim(bias_table, core * mine_heads, mine_heads, 1)
-    far_bias = jnp.stack([table_mine[15], table_mine[31]]).astype(F32)
-    bias, bias_prev, bias_next = call(
-        bias_kernel,
+    bias, bias_prev, bias_next, far_bias, meta_col, meta_row = call(
+        functools.partial(prepare_kernel, cap, experts),
         [
             ((mine_heads, BLK, near), BF16),
             ((mine_heads, LANES, BLK), BF16),
             ((mine_heads, LANES, BLK), BF16),
+            ((8, LANES), F32),
+            ((tok, LANES), jnp.int32),
+            ((8, tok), jnp.int32),
         ],
-        jnp.pad(table_mine.T, ((0, 8 - mine_heads), (0, 0))),
-        x_all,
+        where,
+        bias_table,
+        routes[0],
+        routes[0].reshape(1, tok),
         us=3.0,
-        in_specs=[whole((8, buckets)), anywhere()],
-    )
-
-    route = routes[0, :, 0]
-    route_hot = (route[:, None] == iota((tok, experts), 1)).astype(F32)
-    earlier = (iota((tok, tok), 1) < iota((tok, tok), 0)).astype(F32)
-    slot = jnp.sum(jnp.dot(earlier, route_hot) * route_hot, axis=1).astype(jnp.int32)
-    meta = jnp.stack([route * cap + slot, route, slot])
-    meta_row = jnp.pad(meta, ((0, 5), (0, 0)))
-    meta_col = jnp.pad(meta.T, ((0, 0), (0, LANES - 3)))
+        smem_first=True,
+    )
+
+    if halved and len(far) == 2:
+        came = [place.swap_mask(block, mask) for _, mask in place.several(far)[1]]
+        group = 4 * chip_rows
+        after_a, after_b, after_o, three = call(
+            arrange_kernel,
+            [
+                ((group, split), BF16),
+                ((group, split), BF16),
+                ((group, half), BF16),
+                ((3 * long, width), BF16),
+            ],
+            where,
+            block,
+            *came,
+            *around,
+            meta_row,
+            in_specs=[smem()]
+            + [whole(v.shape) for v in (block, *came, *around)]
+            + [anywhere()],
+        )
+        done = list(far)
+        after_a = after_a.reshape(2, 2, chip_rows, split)
+        after_b = after_b.reshape(2, 2, chip_rows, split)
+        after_o = after_o.reshape(2, 2, chip_rows, half)
+    else:
+        after_far, done = block, []
+        for bit in far:
+            after_far, done = place.stage(after_far, bit, done)
+        after_a, after_b = after_far[..., :split], after_far[..., split : 2 * split]
+        after_o = after_far[..., 2 * split :]
+        three = call(stack_kernel, [((3 * long, width), BF16)], *around)[0]
+    three_came = place.swap(three, 0)
+    later_a, done_a = after_a, done
+    for bit in near_bits:
+        later_a, done_a = place.stage(later_a, bit, done_a)
+    later_b, done_b = after_b, done
+    for bit in seq_bits:
+        later_b, done_b = place.stage(later_b, bit, done_b)
+    later_o, done_o = after_o, done
+    for bit in near_bits:
+        later_o, done_o = place.stage(later_o, bit, done_o)
+    later_o = place.ordered(
+        later_o, place.swap(later_o, 0), 0, len(later_o.shape) - 1, jnp.concatenate
+    )
+    for bit in seq_bits[:-1]:
+        later_o, done_o = place.stage(later_o, bit, done_o)
+    wo_near = later_o.reshape(width // 2, width)
+    wo_far = place.swap(wo_near, seq_bits[-1])
+    if halved:
+        part_rows = width // 2
+        pieces_a = (later_a, place.swap(later_a, seq_bits[-1]))
+        pieces_b = (later_b, place.swap(later_b, near_bits[-1]))
+        pieces = [piece.reshape(part_rows, split) for piece in pieces_a + pieces_b]
+    else:
+        pieces = [
+            place.gather(later_a, seq_bits, done_a),
+            place.gather(later_b, near_bits, done_b),
+        ]
 
     def exchange(message):
-        message = message.reshape(n_ctx, depth, LANES)
+        shape = message.shape
+        message = message.reshape(n_ctx, -1, LANES)
         message = lax.all_to_all(message, "ctx", split_axis=0, concat_axis=0, tiled=True)
-        return message.reshape(n_ctx * depth, LANES)
+        return message.reshape(shape)
 
     msg_shape = (n_ctx * depth, LANES)
     msg_scratch = [VMEM((slots, width), F32), VMEM(msg_shape, F32)]
-
-    hid_all, q_all, k_all, v_all, gains = call(
-        functools.partial(qkv_kernel, experts),
-        [((rows_all, width), BF16)] + [((rows_all, half), BF16)] * 3 + [((8, width), F32)],
-        x_all,
-        w_a,
-        w_b,
-        us=6.0,
-        grid=(rows_all // own_rows,),
-        in_specs=[
-            pl.BlockSpec((own_rows, width), lambda i: (i, 0)),
-            whole((width, split)),
-            whole((width, split)),
-        ],
-        out_specs=[pl.BlockSpec((own_rows, width), lambda i: (i, 0))]
-        + [pl.BlockSpec((own_rows, half), lambda i: (i, 0))] * 3
-        + [whole((8, width))],
-    )
 
     cot_msg = call(
         functools.partial(message_kernel, cap, depth),
         [(msg_shape, BF16)],
         cot,
         meta_row,
-        gains,
+        later_a,
         in_specs=[whole((tok, width)), whole((8, tok)), anywhere()],
         scratch=msg_scratch,
     )[0]
+
+    def chip_step(i):
+        return jnp.minimum(i, 2)
+
+    def pair_step(i):
+        return jnp.maximum(i - 3, 0)
+
+    small_block = pl.BlockSpec((width, LANES), lambda *_: (0, split // LANES - 1))
+    hid_all, q_own, k_all, v_all, gains, ctx_low, lse_rows, w_a, w_b, codes = call(
+        functools.partial(forward_kernel, experts, chip_rows, len(pieces)),
+        [
+            ((rows_all, width), BF16),
+            ((own_rows, half), BF16),
+            ((rows_all, half), BF16),
+            ((rows_all, half), BF16),
+            ((8, width), F32),
+            ((own_rows, half), BF16),
+            ((pairs, 8, own_rows), F32),
+            ((width, split), BF16),
+            ((width, split), BF16),
+            ((rows_all, LANES), BF16),
+        ],
+        far_bias,
+        where,
+        *pieces,
+        three,
+        three_came,
+        three,
+        three_came,
+        bias,
+        cot_msg,
+        us=1.0,
+        grid=(3 + pairs,),
+        in_specs=[whole((8, LANES)), smem()]
+        + [whole(piece.shape) for piece in pieces]
+        + [
+            pl.BlockSpec((long, width), lambda i: (chip_step(i), 0)),
+            pl.BlockSpec((long, width), lambda i: (chip_step(i), 0)),
+            pl.BlockSpec((3 * long, tok), lambda *_: (0, 0)),
+            pl.BlockSpec((3 * long, tok), lambda *_: (0, 0)),
+            pl.BlockSpec((2, BLK, near), lambda i: (pair_step(i), 0, 0)),
+            anywhere(),
+        ],
+        out_specs=[
+            pl.BlockSpec((own_rows, width), lambda i: (chip_step(i), 0)),
+            whole((own_rows, half)),
+            pl.BlockSpec((own_rows, half), lambda i: (chip_step(i), 0)),
+            pl.BlockSpec((own_rows, half), lambda i: (chip_step(i), 0)),
+            whole((8, width)),
+            pl.BlockSpec((own_rows, LANES), lambda i: (0, pair_step(i))),
+            pl.BlockSpec((1, 8, own_rows), lambda i: (pair_step(i), 0, 0)),
+            whole((width, split)),
+            whole((width, split)),
+            whole((rows_all, LANES)),
+        ],
+        scratch=[
+            VMEM((own_rows, half), BF16),
+            VMEM((rows_all, half), BF16),
+            VMEM((rows_all, half), BF16),
+            VMEM((8, rows_all), F32),
+            VMEM((2, BLK, 5 * BLK), F32),
+            VMEM((2, BLK, 5 * BLK), BF16),
+        ],
+    )
+
     cot_in = exchange(cot_msg)
     cot_rows = call(
         functools.partial(rows_kernel, cap, depth),
@@ -986,47 +1340,30 @@
     )[0]
 
     hid_block = pl.BlockSpec((own_rows, width), lambda *_: (1, 0))
-    small_block = pl.BlockSpec((width, LANES), lambda *_: (0, split // LANES - 1))
-
+    code_block = whole((rows_all, LANES))
+    far_block = whole((8, LANES))
     own_block = pl.BlockSpec((own_rows, LANES), lambda p: (1, p))
     all_block = pl.BlockSpec((rows_all, LANES), lambda p: (0, p))
     out_block = pl.BlockSpec((own_rows, LANES), lambda p: (0, p))
     bias_block = pl.BlockSpec((2, BLK, near), lambda p: (p, 0, 0))
     lse_block = pl.BlockSpec((1, 8, own_rows), lambda p: (p, 0, 0))
-    ctx_f, ctx_low, lse, lse_rows = call(
-        attend_kernel,
-        [
-            ((own_rows, half), F32),
-            ((own_rows, half), BF16),
-            ((own_rows, half), F32),
-            ((pairs, 8, own_rows), F32),
-        ],
-        far_bias,
-        q_all,
-        k_all,
-        v_all,
-        bias,
-        x_all,
-        us=12.0,
-        grid=(pairs,),
-        in_specs=[smem(), own_block, all_block, all_block, bias_block, code_block],
-        out_specs=[out_block] * 3 + [lse_block],
-    )
 
     ctx_came = place.swap(ctx_low, 0)
-    mid, hid_two, probs, msg = call(
+    mid, hid_two, probs, msg, wo = call(
         functools.partial(before_kernel, cap, depth, experts),
         [
             ((tok, width), F32),
             ((tok, width), BF16),
             ((tok, LANES), F32),
             (msg_shape, BF16),
+            ((width, width), BF16),
         ],
-        core_arg,
+        where,
         x,
         ctx_low,
         ctx_came,
-        wo,
+        wo_near,
+        wo_far,
         w_b,
         gains,
         meta_col,
@@ -1037,7 +1374,8 @@
             whole((tok, width)),
             whole((own_rows, half)),
             whole((own_rows, half)),
-            whole((width, width)),
+            whole((width // 2, width)),
+            whole((width // 2, width)),
             small_block,
             whole((8, width)),
             whole((tok, LANES)),
@@ -1048,22 +1386,36 @@
     msg_in = exchange(msg)
     lse_prev = place.shift(lse_rows, 2)
     lse_next = place.shift(lse_rows, -2)
+    q_halo = call(
+        halo_query_kernel,
+        [((2 * own_rows, half), BF16)],
+        hid_all,
+        w_a,
+        us=2.0,
+        grid=(2,),
+        in_specs=[
+            pl.BlockSpec((own_rows, width), lambda i: (2 * i, 0)),
+            whole((width, split)),
+        ],
+        out_specs=[pl.BlockSpec((own_rows, half), lambda i: (i, 0))],
+    )[0]
 
     fblk = 512
     win_block = pl.BlockSpec((1, width, fblk), lambda i: (0, 0, i))
     wout_block = pl.BlockSpec((1, fblk, width), lambda i: (0, i, 0))
     act_block = pl.BlockSpec((slots, fblk), lambda i: (0, i))
-    e_rows, e_grad, e_act, e_gbef, made, back_msg = call(
+    e_rows, e_grad, e_act, e_gbef, back_msg = call(
         functools.partial(expert_kernel, cap, depth),
         [((slots, width), BF16)] * 2
         + [((slots, hidden_units), BF16)] * 2
-        + [((slots, width), BF16), (msg_shape, BF16)],
+        + [((2 * msg_shape[0], LANES), BF16)],
         msg_in,
         cot_rows,
         w_in,
         w_out,
         lse_prev,
         lse_next,
+        q_halo,
         us=12.0,
         grid=(hidden_units // fblk,),
         in_specs=[
@@ -1073,10 +1425,11 @@
             wout_block,
             anywhere(),
             anywhere(),
+            anywhere(),
         ],
         out_specs=[whole((slots, width))] * 2
         + [act_block] * 2
-        + [whole((slots, width)), whole(msg_shape)],
+        + [whole((2 * msg_shape[0], LANES))],
         scratch=[VMEM((slots, width), F32)] + msg_scratch,
     )
     back_in = exchange(back_msg)
@@ -1123,8 +1476,11 @@
 
     grad_mid, gattn_mine, gattn_theirs, gctx_mine, gctx_theirs, extra = call(
         functools.partial(after_kernel, cap, depth, experts),
-        [((tok, width), F32)] + [((tok, half), BF16)] * 4 + [((width, LANES), F32)],
-        core_arg,
+        [((tok, width), F32)]
+        + [((tok, half), BF16)] * 2
+        + [((tok + 32, half), BF16)] * 2
+        + [((width, LANES), F32)],
+        where,
         back_in,
         cot,
         mid,
@@ -1134,11 +1490,13 @@
         gains,
         wo,
         meta_col,
+        ctx_low,
+        ctx_came,
         grad_w_out,
         us=5.0,
         in_specs=[
             smem(),
-            whole(msg_shape),
+            whole(back_in.shape),
             whole((tok, width)),
             whole((tok, width)),
             whole((tok, width)),
@@ -1147,26 +1505,26 @@
             whole((8, width)),
             whole((width, width)),
             whole((tok, LANES)),
+            whole((own_rows, half)),
+            whole((own_rows, half)),
             anywhere(),
         ],
         scratch=msg_scratch + [VMEM((tok, width), BF16)],
     )
 
-    gctx_came = place.swap(gctx_theirs, 0)
-    gctx, delta = call(
-        delta_kernel,
-        [((own_rows, half), BF16), ((8, own_rows), F32)],
-        core_arg,
-        gctx_mine,
-        gctx_came,
-        ctx_f,
-        us=2.0,
-        smem_first=True,
-    )
+    gctx = place.ordered(gctx_mine, place.swap(gctx_theirs, 0), 0, 0, jnp.concatenate)
     gctx_prev = place.shift(gctx, 2)
     gctx_next = place.shift(gctx, -2)
-    delta_prev = place.shift(delta, 2)
-    delta_next = place.shift(delta, -2)
+
+    output = call(
+        functools.partial(output_kernel, cap, depth),
+        [((tok, width), BF16)],
+        back_in,
+        mid,
+        probs,
+        meta_col,
+        scratch=msg_scratch,
+    )[0]
 
     dq, dk_own, dv_own, tab = call(
         own_backward_kernel,
@@ -1177,87 +1535,88 @@
             ((pairs, 8, LANES), F32),
         ],
         far_bias,
-        q_all,
+        q_own,
         k_all,
         v_all,
         gctx,
-        ctx_f,
-        lse,
+        lse_rows,
         bias,
-        x_all,
-        us=15.0,
+        codes,
+        us=14.0,
         grid=(pairs,),
         in_specs=[
-            smem(),
-            own_block,
+            far_block,
+            out_block,
             all_block,
             all_block,
-            out_block,
-            out_block,
-            out_block,
+            whole(gctx.shape),
+            lse_block,
             bias_block,
             code_block,
         ],
         out_specs=[out_block] * 3 + [pl.BlockSpec((1, 8, LANES), lambda p: (p, 0, 0))],
-    )
-
-    delta_block = whole((8, own_rows))
+        scratch=[
+            VMEM((2, BLK, 5 * BLK), F32),
+            VMEM((2, BLK, 5 * BLK), F32),
+            VMEM((2, BLK, 5 * BLK), BF16),
+            VMEM((2, BLK, 5 * BLK), BF16),
+            VMEM((2, BLK, near), F32),
+        ],
+    )
+
     halo_bias = pl.BlockSpec((2, LANES, BLK), lambda p: (p, 0, 0))
-    tab_block = pl.BlockSpec((1, 8, LANES), lambda p: (p, 0, 0))
-    dk, dv, tab = call(
+    dk, dv = call(
         halo_backward_kernel,
-        [((own_rows, half), BF16)] * 2 + [((pairs, 8, LANES), F32)],
+        [((own_rows, half), BF16)] * 2,
         far_bias,
-        q_all,
-        q_all,
+        q_halo,
+        q_halo,
         k_all,
         v_all,
         gctx_prev,
         gctx_next,
         lse_prev,
         lse_next,
-        delta_prev,
-        delta_next,
         bias_prev,
         bias_next,
-        x_all,
+        codes,
         dk_own,
         dv_own,
-        tab,
         us=9.0,
         grid=(pairs,),
         in_specs=[
-            smem(),
-            pl.BlockSpec((own_rows, LANES), lambda p: (0, p)),
-            pl.BlockSpec((own_rows, LANES), lambda p: (2, p)),
+            far_block,
+            out_block,
             own_block,
             own_block,
-            out_block,
-            out_block,
+            own_block,
+            whole(gctx.shape),
+            whole(gctx.shape),
             lse_block,
             lse_block,
-            delta_block,
-            delta_block,
             halo_bias,
             halo_bias,
             code_block,
             out_block,
             out_block,
-            tab_block,
         ],
-        out_specs=[out_block] * 2 + [tab_block],
+        out_specs=[out_block] * 2,
+        scratch=[VMEM((2, 8, own_rows), F32)],
     )
 
     ga_cols = place.ordered(gattn_mine, place.swap(gattn_theirs, 0), 0, 0, jnp.concatenate)
     ctx_full = place.ordered(ctx_low, ctx_came, 0, 1, jnp.concatenate)
     back_far = far[::-1]
-    head_bits = seq_bits + near_bits
-    sum_o = place.scatter(tn(ctx_full, ga_cols), head_bits, back_far)
-    chip_rows = 2 * rows_dev
+    total_o = tn(ctx_full, ga_cols)
     order_a = seq_bits + near_bits
     order_b = near_bits + seq_bits
-    if chip_rows % 16 == 0:
-        bits = jnp.stack([place.bit(order_a[0]), place.bit(order_b[0])]).astype(jnp.int32)
+    joined = halved and len(seq_bits) == 1 and len(far) == 2
+    if joined:
+        chip_bits = seq_bits + near_bits + far
+        gone_o, kept_o = place.halves(total_o, order_a[0], chip_bits)
+        half_o = kept_o + place.swap(gone_o, order_a[0]).astype(F32)
+        gone_o, kept_o = place.halves(half_o, order_a[1], order_a[1:] + far)
+        came_o = place.swap(gone_o, order_a[1])
         gone_a, kept_a, gone_b, kept_b = call(
             functools.partial(sums_kernel, chip_rows),
             [
@@ -1266,12 +1625,13 @@
                 ((width // 2, split), BF16),
                 ((width // 2, split), F32),
             ],
-            bits,
+            where,
             hid_all,
             dq,
             dk,
             dv,
             extra,
+            tab,
             us=4.0,
             in_specs=[
                 smem(),
@@ -1280,45 +1640,30 @@
                 whole((own_rows, half)),
                 whole((own_rows, half)),
                 whole((width, LANES)),
+                whole((pairs, 8, LANES)),
             ],
             scratch=[VMEM((width, split), F32)],
         )
-        soon = gone_a
-        later, sum_a = place.scatter_on(gone_a, kept_a, order_a[1:], order_a[0], back_far)
-        _, sum_b = place.scatter_on(gone_b, kept_b, order_b[1:], order_b[0], back_far)
+        later = half_a = kept_a + place.swap(gone_a, order_a[0]).astype(F32)
+        half_b = kept_b + place.swap(gone_b, order_b[0]).astype(F32)
+        gone_a, kept_a = place.halves(half_a, order_a[1], order_a[1:] + far)
+        gone_b, kept_b = place.halves(half_b, order_b[1], order_b[1:] + far)
+        came_a = place.swap(gone_a, order_a[1])
+        came_b = place.swap(gone_b, order_b[1])
     else:
         hid_one = hid_all[own_rows : 2 * own_rows]
         cut = split - half
         total_a = tn(hid_one, jnp.concatenate([dq, dk[:, :cut]], axis=1))
         total_b = tn(hid_one, jnp.concatenate([dk[:, cut:], dv], axis=1))
-        soon = later = total_a
-        sum_a = place.scatter(total_a, order_a, back_far)
-        sum_b = place.scatter(jnp.concatenate([total_b, extra], axis=1), order_b, back_far)
-    sums = place.scatter(jnp.concatenate([sum_a, sum_b, sum_o], axis=1), back_far)
-    sums = sums.reshape(2, rows_dev, sums.shape[1])
-    gone = lax.dynamic_index_in_dim(sums, 1 - core, 0, keepdims=False)
-    kept = lax.dynamic_index_in_dim(sums, core, 0, keepdims=False)
-    came = place.swap(gone, 0)
-
-    def columns(first):
-        return place.ordered(
-            kept[:, first : first + half], came[:, first : first + half], 0, 1, jnp.concatenate
-        )
-
-    sum_q, sum_k, sum_v = columns(0), columns(half), columns(2 * half)
-    sum_out = columns(3 * half + LANES)
-    extra_sum = kept[:, 3 * half : 3 * half + LANES] + came[:, 3 * half : 3 * half + LANES]
-    grad_router = extra_sum[:, :experts]
-    grad_gain_two = extra_sum[:, experts]
-    weighted = (
-        sum_q * w_query.astype(F32) + sum_k * w_key.astype(F32) + sum_v * w_value.astype(F32)
-    )
-    grad_gain_one = jnp.sum(weighted, axis=1) / gain_attn.astype(F32)
+        later = total_a
+        total_b = jnp.concatenate([total_b, extra], axis=1)
+        sums = jnp.concatenate([total_a, total_b, total_o], axis=1)
+        sums = place.scatter(sums, seq_bits + near_bits + far[::-1])
 
     part, part_gone = call(
         input_kernel,
         [((tok, width), F32), ((tok, width), F32)],
-        core_arg,
+        where,
         dq,
         dk,
         dv,
@@ -1331,6 +1676,47 @@
         + [whole((width, split))] * 2
         + [anywhere()],
     )
+    if joined:
+        columns_all = 2 * split + half
+        parts_z = call(
+            functools.partial(join_kernel, chip_rows),
+            [((chip_rows, columns_all), F32)] + [((chip_rows, columns_all), BF16)] * 3,
+            where,
+            kept_a,
+            came_a,
+            kept_b,
+            came_b,
+            kept_o,
+            came_o,
+            part_gone,
+            in_specs=[smem()]
+            + [whole(v.shape) for v in (kept_a, came_a, kept_b, came_b, kept_o, came_o)]
+            + [anywhere()],
+            scratch=[VMEM((kept_a.shape[0], columns_all), F32)],
+        )
+        sums = parts_z[0]
+        for (_, mask), piece in zip(place.several(far)[1], parts_z[1:]):
+            sums = sums + place.swap_mask(piece, mask).astype(F32)
+    sums = sums.reshape(2, rows_dev, sums.shape[1])
+    gone = lax.dynamic_index_in_dim(sums, 1 - core, 0, keepdims=False)
+    kept = lax.dynamic_index_in_dim(sums, core, 0, keepdims=False)
+    came = place.swap(gone, 0)
+
+    def columns(first):
+        return place.ordered(
+            kept[:, first : first + half], came[:, first : first + half], 0, 1, jnp.concatenate
+        )
+
+    sum_q, sum_k, sum_v = columns(0), columns(half), columns(2 * half)
+    sum_out = columns(3 * half + LANES)
+    extra_sum = kept[:, 3 * half : 3 * half + LANES] + came[:, 3 * half : 3 * half + LANES]
+    grad_router = extra_sum[:, :experts]
+    grad_gain_two = extra_sum[:, experts]
+    weighted = (
+        sum_q * w_query.astype(F32) + sum_k * w_key.astype(F32) + sum_v * w_value.astype(F32)
+    )
+    grad_gain_one = jnp.sum(weighted, axis=1) / gain_attn.astype(F32)
+
     grad_hidden = part + place.swap(part_gone, 0)
     tokens = x.astype(F32)
     scale_one = lax.rsqrt(jnp.mean(tokens * tokens, axis=-1, keepdims=True) + EPSILON)
@@ -1340,28 +1726,15 @@
         grad_normed - normed_one * jnp.mean(grad_normed * normed_one, axis=-1, keepdims=True)
     )
 
-    made_msg = call(
-        functools.partial(spread_kernel, cap, depth),
-        [(msg_shape, BF16)],
-        made,
-        soon,
-        in_specs=[whole((slots, width)), anywhere()],
-        scratch=msg_scratch,
-    )[0]
-    made_in = exchange(made_msg)
-    output = call(
-        functools.partial(output_kernel, cap, depth),
-        [((tok, width), BF16)],
-        made_in,
-        mid,
-        probs,
-        meta_col,
-        scratch=msg_scratch,
-    )[0]
-
-    table = place.total(tab[:, :2].reshape(mine_heads, LANES))
-    table = place.ordered(table, place.swap(table, 0), 0, 0, jnp.concatenate)
-    table_sum = table[:, :buckets].T
+    if joined:
+        first = 3 * half + LANES - buckets
+        table = kept[:mine_heads, first : first + buckets]
+        other = came[:mine_heads, first : first + buckets]
+        table_sum = place.ordered(table, other, 0, 0, jnp.concatenate).T
+    else:
+        table = place.total(tab[:, :2].reshape(mine_heads, LANES))
+        table = place.ordered(table, place.swap(table, 0), 0, 0, jnp.concatenate)
+        table_sum = table[:, :buckets].T
 
     return (
         output[None],

time: 285 us -> 262 us (0.919)
  between operations: 14.9 us -> 1.26 us
  starting transfers between devices: 73.1 us -> 62.3 us
  Pallas kernels: 105 us -> 113 us
  other arithmetic: 15.6 us -> 8.01 us
  local copies, waits for them, and re-layouts: 15.9 us -> 18.8 us
    ppermute x28 -> x22, waiting for transfers between devices: 52.8 us -> 26.1 us  [swap(): return lax.ppermute(value, AXES, pairs)]
    ppermute x0 -> x6, waiting for transfers between devices: none -> 23.4 us  [swap_mask(): return lax.ppermute(value, AXES, [(i, i ^ mask) for i in range(self.count)])]
    ppermute x0 -> x6, starting transfers between devices: none -> 12.7 us  [swap_mask(): return lax.ppermute(value, AXES, [(i, i ^ mask) for i in range(self.count)])]
    ppermute x28 -> x22, starting transfers between devices: 31.3 us -> 19.8 us  [swap(): return lax.ppermute(value, AXES, pairs)]
    pallas_call x16 -> x17, Pallas kernels: 105 us -> 113 us  [call(): pl.pallas_call(kernel, out_shape=shapes, grid=grid if grid is not None el...]
    ppermute x8 -> x6, starting transfers between devices: 22.6 us -> 16.2 us  [shift(): return lax.ppermute(value, AXES, pairs)]
    all_to_all x4 -> x3, starting transfers between devices: 19.2 us -> 13.6 us  [exchange(): lax.all_to_all(message, 'ctx', split_axis=0, concat_axis=0, tiled=True)]
    another operation x4 -> x0, other arithmetic: 2.92 us -> none  [the longest x2 2.32 us: local(): three = jnp.stack([before_x, x_ext, after_x])]
  transfers between devices with their start and end apart: 41 -> 37, of which waited for: 15 -> 16; matrix products, arithmetic and copies ran while one was open for 7% -> 5% of each run, Pallas kernels for 35% -> 39%
where the time goes in v1:
time: 262 us; the launch traced here: 260 us
  Pallas kernels  113 us (43%)
  starting transfers between devices  62.3 us (24%)
  waiting for transfers between devices  56.7 us (22%)
  local copies, waits for them, and re-layouts  18.8 us (7%)
  other arithmetic  8.01 us (3%)
    pallas_call x17, Pallas kernels, call(): pl.pallas_call(kernel, out_shape=shapes, grid=grid if grid is not None el...  113 us
    ppermute x22, waiting for transfers between devices, swap(): return lax.ppermute(value, AXES, pairs)  26.1 us
    ppermute x6, waiting for transfers between devices, swap_mask(): return lax.ppermute(value, AXES, [(i, i ^ mask) for i in range(self.count)])  23.4 us
    ppermute x22, starting transfers between devices, swap(): return lax.ppermute(value, AXES, pairs)  19.8 us
    ppermute x6, starting transfers between devices, shift(): return lax.ppermute(value, AXES, pairs)  16.2 us
    all_to_all x3, starting transfers between devices, exchange(): lax.all_to_all(message, 'ctx', split_axis=0, concat_axis=0, tiled=True)  13.6 us
    ppermute x6, starting transfers between devices, swap_mask(): return lax.ppermute(value, AXES, [(i, i ^ mask) for i in range(self.count)])  12.7 us
    unnamed x93, local copies, waits for them, and re-layouts  10 us
  transfers between devices with their start and end apart: 37, of which 16 were waited for; matrix products, arithmetic and copies ran while one was open for 5% of the time, Pallas kernels for 39%

profile of v1, /device:TPU:0, one launch (start us, length us, event | category | flops | bytes accessed | tf_op | source)
XLA Modules:
  0.0 260.3 jit_solution(13032511349112718138)
XLA Ops:
  7.1 4.4 %collective-permute-start.4 = (bf16[272,768]{1,0:T(8,128)(2,1)}, bf16[272,768]{1,0:T(8,128)(2,1)S(1)}, u32[]{:S(2)}, u32[]{:S(2)}) collective-permute-start(bf16[272,768]{1,0:T(8,128)(2,1)} %shard_map.230.refs_5_), channel_id=1, source_target_pairs={{0,2},{1,3},{2,4},{3,5},{4,6},{5,7},{6,8},{7,9},{8,10},{9,11},{10,... | collective-permute-start | bytes 1253384 | tf_op jit(solution)/shard_map/ppermute | solution.py:1009
  15.0 3.7 %collective-permute-start.1 = (bf16[48,1664]{1,0:T(8,128)(2,1)S(1)}, bf16[48,1664]{1,0:T(8,128)(2,1)S(1)}, u32[]{:S(2)}, u32[]{:S(2)}) collective-permute-start(bf16[48,1664]{1,0:T(8,128)(2,1)S(1)} %pad_maximum_fusion.5.refs_0_), channel_id=1, source_target_pairs={{0,4},{1,5},{2,6},{3,7},{4,0},{5,1},{6,2},{7,3},{8,12},{9,13},{10,... | collective-permute-start | bytes 479240 | tf_op jit(solution)/shard_map/ppermute | solution.py:1030
  18.7 2.6 collective-permute-start.2
  21.3 3.3 %shard_map.229 = (bf16[6,256,512]{2,1,0:T(8,128)(2,1)}, bf16[6,128,256]{2,1,0:T(8,128)(2,1)}, bf16[6,128,256]{2,1,0:T(8,128)(2,1)}, f32[8,128]{1,0:T(8,128)}, s32[256,128]{1,0:T(8,128)}, /*index=5*/s32[8,256]{1,0:T(8,128)}) custom-call(s32[6]{0:T(128)} %stack.48.where_ref.core_ref.bits_ref, bf16[32,12]{1,0:T(8,128)(2,1)} %copy.82.table_ref, ...), custom_call_target="tpu_custom_call" | custom-call | flops 3449999872 | tf_op jit(solution)/shard_map/pallas_call | solution.py:1084
  24.6 8.7 %collective-permute-done.1.refs_1_ = bf16[48,1664]{1,0:T(8,128)(2,1)S(1)} collective-permute-done((bf16[48,1664]{1,0:T(8,128)(2,1)S(1)}, bf16[48,1664]{1,0:T(8,128)(2,1)S(1)}, u32[]{:S(2)}, u32[]{:S(2)}) %collective-permute-start.1) | collective-permute-done | bytes 159776 | tf_op jit(solution)/shard_map/ppermute | solution.py:1030
  33.2 5.5 %collective-permute-done.3.refs_3_ = bf16[48,1664]{1,0:T(8,128)(2,1)S(1)} collective-permute-done((bf16[48,1664]{1,0:T(8,128)(2,1)S(1)}, bf16[48,1664]{1,0:T(8,128)(2,1)S(1)}, u32[]{:S(2)}, u32[]{:S(2)}) %collective-permute-start.3) | collective-permute-done | bytes 159776 | tf_op jit(solution)/shard_map/ppermute | solution.py:1030
  39.7 2.8 %shard_map.231 = (bf16[192,640]{1,0:T(8,128)(2,1)}, bf16[192,640]{1,0:T(8,128)(2,1)}, bf16[192,384]{1,0:T(8,128)(2,1)}, bf16[816,768]{1,0:T(8,128)(2,1)}) custom-call(s32[6]{0:T(128)} %stack.48.where_ref.core_ref.bits_ref, bf16[48,1664]{1,0:T(8,128)(2,1)} %copy-done.20, bf16[48,1664]{1,0:T(8,128)(2,1)} %copy-done.38, bf16[48,1664]{1,0:T(8,128)(2,1)} %copy-done.39, ...), custom_call_target="tpu_custom_call" | custom-call | flops 2300000000 | tf_op jit(solution)/shard_map/pallas_call | solution.py:1084
  46.1 3.4 %collective-permute-done.12 = bf16[2,2,48,384]{3,2,1,0:T(8,128)(2,1)S(1)} collective-permute-done((bf16[2,2,48,384]{3,2,1,0:T(8,128)(2,1)}, bf16[2,2,48,384]{3,2,1,0:T(8,128)(2,1)S(1)}, u32[]{:S(2)}, u32[]{:S(2)}) %collective-permute-start.12) | collective-permute-done | bytes 147488 | tf_op jit(solution)/shard_map/ppermute | solution.py:998
  57.7 4.4 %all-to-all-start.1 = ((bf16[16,112,128]{2,1,0:T(8,128)(2,1)}), bf16[16,112,128]{2,1,0:T(8,128)(2,1)}, u32[]{:S(2)}, u32[]{:S(2)}) async-start(bf16[16,112,128]{2,1,0:T(8,128)(2,1)} %bitcast.79), calls=%async_computation.1 | async-start | bytes 917504 | tf_op jit(solution)/shard_map/all_to_all | solution.py:1254
  64.6 3.0 %collective-permute-done.7 = bf16[2,2,2,48,640]{4,3,2,1,0:T(8,128)(2,1)} collective-permute-done((bf16[2,2,2,48,640]{4,3,2,1,0:T(8,128)(2,1)S(1)}, bf16[2,2,2,48,640]{4,3,2,1,0:T(8,128)(2,1)}, u32[]{:S(2)}, u32[]{:S(2)}) %collective-permute-start.7) | collective-permute-done | bytes 491552 | tf_op jit(solution)/shard_map/ppermute | solution.py:998
  68.6 18.8 %shard_map.233 = (bf16[1536,768]{1,0:T(8,128)(2,1)}, bf16[512,384]{1,0:T(8,128)(2,1)}, bf16[1536,384]{1,0:T(8,128)(2,1)}, bf16[1536,384]{1,0:T(8,128)(2,1)}, f32...) custom-call(f32[8,128]{1,0:T(8,128)} %get-tuple-element.66.far_ref, ...), custom_call_target="tpu_custom_call" | custom-call | flops 1150000000 | tf_op jit(solution)/shard_map/pallas_call | solution.py:1084
  90.2 4.6 %shard_map.234 = (f32[256,768]{1,0:T(8,128)}, bf16[256,768]{1,0:T(8,128)(2,1)}, f32[256,128]{1,0:T(8,128)}, bf16[1792,128]{1,0:T(8,128)(2,1)}, bf16[768,768]{1,0:T(8,128)(2,1)}) custom-call(s32[6]{0:T(128)} %stack.48.where_ref.core_ref.bits_ref, bf16[256,768]{1,0:T(8,128)(2,1)} %bitcast.72, bf16[512,384]{1,0:T(8,128)(2,1)} %get-tuple-element.72.own_ref, ...), custom_call_target="tpu_custom_call" | custom-call | flops 4600000000 | tf_op jit(solution)/shard_map/pallas_call | solution.py:1084
  94.8 4.4 %all-to-all-start = ((bf16[16,112,128]{2,1,0:T(8,128)(2,1)}), bf16[16,112,128]{2,1,0:T(8,128)(2,1)S(1)}, u32[]{:S(2)}, u32[]{:S(2)}) async-start(bf16[16,112,128]{2,1,0:T(8,128)(2,1)} %bitcast.94), calls=%async_computation | async-start | bytes 917504 | tf_op jit(solution)/shard_map/all_to_all | solution.py:1254
  102.9 3.8 %collective-permute-start.15 = (f32[3,8,512]{2,1,0:T(8,128)S(1)}, f32[3,8,512]{2,1,0:T(8,128)S(1)}, u32[]{:S(2)}, u32[]{:S(2)}) collective-permute-start(f32[3,8,512]{2,1,0:T(8,128)S(1)} %copy-done.42), channel_id=1, source_target_pairs={{0,2},{1,3},{2,4},{3,5},{4,6},{5,7},{6,8},{7,9},{8,10},{9,11},{10,... | collective-permute-start | bytes 147464 | tf_op jit(solution)/shard_map/ppermute | solution.py:1009
  108.2 3.4 %shard_map.236.earlier_c_ref.qp_ref.qn_ref = bf16[1024,384]{1,0:T(8,128)(2,1)} custom-call(bf16[1536,768]{1,0:T(8,128)(2,1)} %get-tuple-element.79.hid_ref, bf16[768,640]{1,0:T(8,128)(2,1)} %get-tuple-element.80.wa_ref), custom_call_target="tpu_custom_call" | custom-call | flops 2300000000 | tf_op jit(solution)/shard_map/pallas_call | solution.py:1084
  115.2 12.4 %shard_map.237 = (bf16[288,768]{1,0:T(8,128)(2,1)}, bf16[288,768]{1,0:T(8,128)(2,1)}, bf16[288,3072]{1,0:T(8,128)(2,1)}, bf16[288,3072]{1,0:T(8,128)(2,1)}, bf16[3584,128]{1,0:T(8,128)(2,1)}) custom-call(bf16[1792,128]{1,0:T(8,128)(2,1)} %bitcast.93, bf16[288,768]{1,0:T(8,128)(2,1)} %shard_map.235.cot_ref, bf16[1,768,3072]{2,1,0:T(8,128)(2,1)} %win_ref.3, ...), custom_call_target="tpu_custom_call" | custom-call | flops 13799999488 | tf_op jit(solution)/shard_map/pallas_call | solution.py:1084
  127.6 4.8 %all-to-all-start.2 = ((bf16[16,224,128]{2,1,0:T(8,128)(2,1)}), bf16[16,224,128]{2,1,0:T(8,128)(2,1)S(1)}, u32[]{:S(2)}, u32[]{:S(2)}) async-start(bf16[16,224,128]{2,1,0:T(8,128)(2,1)} %bitcast.85), calls=%async_computation.2 | async-start | bytes 1835008 | tf_op jit(solution)/shard_map/all_to_all | solution.py:1254
  133.4 16.4 %shard_map.239 = (f32[1,768,3072]{2,1,0:T(8,128)}, f32[1,3072,768]{2,1,0:T(8,128)}) custom-call(bf16[288,768]{1,0:T(8,128)(2,1)} %get-tuple-element.86.rows_ref, bf16[288,768]{1,0:T(8,128)(2,1)} %get-tuple-element.87.grad_ref, bf16[288,3072]{1,0:T(8,128)(2,1)} %get-tuple-element.88.act_ref, bf16[288,3072]{1,0:T(8,128)(2,1)} %get-tuple-element.89.gbef_ref, ...), custom_call_target="tpu_custom_call" | custom-call | flops 18400000000 | tf_op jit(solution)/shard_map/pallas_call | solution.py:1084
  149.7 3.5 %all-to-all-done.2 = bf16[16,224,128]{2,1,0:T(8,128)(2,1)S(1)} async-done(((bf16[16,224,128]{2,1,0:T(8,128)(2,1)}), bf16[16,224,128]{2,1,0:T(8,128)(2,1)S(1)}, u32[]{:S(2)}, u32[]{:S(2)}) %all-to-all-start.2) | async-done | bytes 917536 | tf_op jit(solution)/shard_map/all_to_all | solution.py:1254
  154.2 6.6 %shard_map.240 = (f32[256,768]{1,0:T(8,128)}, bf16[256,384]{1,0:T(8,128)(2,1)}, bf16[256,384]{1,0:T(8,128)(2,1)}, bf16[288,384]{1,0:T(8,128)(2,1)}, bf16[288,384]{1,0:T(8,128)(2,1)}, /*index=5*/f32[768,128]{1,0:T(8,128)}) custom-call(s32[6]{0:T(128)} %stack.48.where_ref.core_ref.bits_ref, bf16[3584,128]{1,0:T(8,128)(2,1)} %bitcast.83, ...), custom_call_target="tpu_custom_call" | custom-call | flops 5750000128 | tf_op jit(solution)/shard_map/pallas_call | solution.py:1084
  165.1 3.7 %collective-permute-start.20 = (bf16[576,384]{1,0:T(8,128)(2,1)S(1)}, bf16[576,384]{1,0:T(8,128)(2,1)S(1)}, u32[]{:S(2)}, u32[]{:S(2)}) collective-permute-start(bf16[576,384]{1,0:T(8,128)(2,1)S(1)} %pad_maximum_fusion.3.msg_ref), channel_id=1, source_target_pairs={{0,2},{1,3},{2,4},{3,5},{4,6},{5,7},{6,8},{7,9},{8,10},{9,11},{10,... | collective-permute-start | bytes 1327112 | tf_op jit(solution)/shard_map/ppermute | solution.py:1009
  170.3 14.7 %shard_map.241 = (bf16[512,384]{1,0:T(8,128)(2,1)}, f32[512,384]{1,0:T(8,128)}, f32[512,384]{1,0:T(8,128)}, f32[3,8,128]{2,1,0:T(8,128)}) custom-call(f32[8,128]{1,0:T(8,128)} %get-tuple-element.66.far_ref, bf16[512,384]{1,0:T(8,128)(2,1)} %get-tuple-element.92.q_ref, bf16[1536,384]{1,0:T(8,128)(2,1)} %get-tuple-element.93.k_ref, ...), custom_call_target="tpu_custom_call" | custom-call | flops 16099999744 | tf_op jit(solution)/shard_map/pallas_call | solution.py:1084
  185.0 2.9 %collective-permute-done.20.gp_ref = bf16[576,384]{1,0:T(8,128)(2,1)S(1)} collective-permute-done((bf16[576,384]{1,0:T(8,128)(2,1)S(1)}, bf16[576,384]{1,0:T(8,128)(2,1)S(1)}, u32[]{:S(2)}, u32[]{:S(2)}) %collective-permute-start.20) | collective-permute-done | bytes 442400 | tf_op jit(solution)/shard_map/ppermute | solution.py:1009
  188.8 9.7 %shard_map.242 = (bf16[512,384]{1,0:T(8,128)(2,1)}, bf16[512,384]{1,0:T(8,128)(2,1)}) custom-call(f32[8,128]{1,0:T(8,128)} %get-tuple-element.66.far_ref, bf16[1024,384]{1,0:T(8,128)(2,1)} %shard_map.236.earlier_c_ref.qp_ref.qn_ref, bf16[1024,384]{1,0:T(8,128)(2,1)} %shard_map.236.earlier_c_ref.qp_ref.qn_ref, bf16[1536,384]{1,0:T(8,128)(2,1)} %get-tuple-element.93.k_ref, ...), custom_call_target="tpu_custom_call" | custom-call | flops 10350000128 | tf_op jit(solution)/shard_map/pallas_call | solution.py:1084
  198.5 4.3 %shard_map.243 = (bf16[384,640]{1,0:T(8,128)(2,1)}, f32[384,640]{1,0:T(8,128)}, bf16[384,640]{1,0:T(8,128)(2,1)}, f32[384,640]{1,0:T(8,128)}) custom-call(s32[6]{0:T(128)} %stack.48.where_ref.core_ref.bits_ref, bf16[1536,768]{1,0:T(8,128)(2,1)} %get-tuple-element.79.hid_ref, bf16[512,384]{1,0:T(8,128)(2,1)} %get-tuple-element.98.dq_ref, ...), custom_call_target="tpu_custom_call" | custom-call | flops 4600000000 | tf_op jit(solution)/shard_map/pallas_call | solution.py:1084
  202.9 2.5 collective-permute-start.25
  207.4 10.3 %collective-permute-done.25 = bf16[384,640]{1,0:T(8,128)(2,1)S(1)} collective-permute-done((bf16[384,640]{1,0:T(8,128)(2,1)}, bf16[384,640]{1,0:T(8,128)(2,1)S(1)}, u32[]{:S(2)}, u32[]{:S(2)}) %collective-permute-start.25) | collective-permute-done | bytes 491552 | tf_op jit(solution)/shard_map/ppermute | solution.py:998
  220.0 4.4 %shard_map.244 = (f32[256,768]{1,0:T(8,128)}, f32[256,768]{1,0:T(8,128)}) custom-call(s32[6]{0:T(128)} %stack.48.where_ref.core_ref.bits_ref, bf16[512,384]{1,0:T(8,128)(2,1)} %get-tuple-element.98.dq_ref, bf16[512,384]{1,0:T(8,128)(2,1)} %get-tuple-element.103.dk_ref, bf16[512,384]{1,0:T(8,128)(2,1)} %get-tuple-element.104.dv_ref, ...), custom_call_target="tpu_custom_call" | custom-call | flops 4600000000 | tf_op jit(solution)/shard_map/pallas_call | solution.py:1084
  231.4 2.6 shard_map.245
  234.0 3.9 %collective-permute-start.30 = (bf16[48,1664]{1,0:T(8,128)(2,1)}, bf16[48,1664]{1,0:T(8,128)(2,1)S(1)}, u32[]{:S(2)}, u32[]{:S(2)}) collective-permute-start(bf16[48,1664]{1,0:T(8,128)(2,1)} %get-tuple-element.116), channel_id=1, source_target_pairs={{0,4},{1,5},{2,6},{3,7},{4,0},{5,1},{6,2},{7,3},{8,12},{9,13},{10,... | collective-permute-start | bytes 479240 | tf_op jit(solution)/shard_map/ppermute | solution.py:1030
  242.3 8.1 %collective-permute-done.31 = bf16[48,1664]{1,0:T(8,128)(2,1)S(1)} collective-permute-done((bf16[48,1664]{1,0:T(8,128)(2,1)}, bf16[48,1664]{1,0:T(8,128)(2,1)S(1)}, u32[]{:S(2)}, u32[]{:S(2)}) %collective-permute-start.31) | collective-permute-done | bytes 159776 | tf_op jit(solution)/shard_map/ppermute | solution.py:1030
  251.6 2.7 %shard_map.238 = bf16[256,768]{1,0:T(8,128)(2,1)} custom-call(bf16[3584,128]{1,0:T(8,128)(2,1)} %bitcast.84, f32[256,768]{1,0:T(8,128)} %get-tuple-element.82.mid_ref, f32[256,128]{1,0:T(8,128)} %get-tuple-element.83.prob_ref, s32[256,128]{1,0:T(8,128)} %get-tuple-element.76.meta_col_ref.meta_ref), custom_call_target="tpu_custom_call" | custom-call | flops 2300000000 | tf_op jit(solution)/shard_map/pallas_call | solution.py:1084
  (204 shorter events, 68.6 us)
Async XLA Ops:
  4.7 10.2 %collective-permute-start = (bf16[24,1664]{1,0:T(8,128)(2,1)S(1)}, bf16[24,1664]{1,0:T(8,128)(2,1)S(1)}, u32[]{:S(2)}, u32[]{:S(2)}) collective-permute-start(bf16[24,1664]{1,0:T(8,128)(2,1)S(1)} %broadcast_select_fusion.9), channel_id=1, source_target_pairs={{0,1},{1,0},{2,3},{3,2},{4,5},{5,4},{6,7},{7,6},{8,9},{9,8},{10,11... | collective-permute-start | bytes 239624 | tf_op jit(solution)/shard_map/ppermute | solution.py:998
  7.1 31.7 %collective-permute-start.4 = (bf16[272,768]{1,0:T(8,128)(2,1)}, bf16[272,768]{1,0:T(8,128)(2,1)S(1)}, u32[]{:S(2)}, u32[]{:S(2)}) collective-permute-start(bf16[272,768]{1,0:T(8,128)(2,1)} %shard_map.230.refs_5_), channel_id=1, source_target_pairs={{0,2},{1,3},{2,4},{3,5},{4,6},{5,7},{6,8},{7,9},{8,10},{9,11},{10,... | collective-permute-start | bytes 1253384 | tf_op jit(solution)/shard_map/ppermute | solution.py:1009
  11.5 27.3 %collective-permute-start.5 = (bf16[272,768]{1,0:T(8,128)(2,1)}, bf16[272,768]{1,0:T(8,128)(2,1)S(1)}, u32[]{:S(2)}, u32[]{:S(2)}) collective-permute-start(bf16[272,768]{1,0:T(8,128)(2,1)} %shard_map.230.refs_5_), channel_id=1, source_target_pairs={{2,0},{3,1},{4,2},{5,3},{6,4},{7,5},{8,6},{9,7},{10,8},{11,9},{12,... | collective-permute-start | bytes 1253384 | tf_op jit(solution)/shard_map/ppermute | solution.py:1009
  15.0 18.2 %collective-permute-start.1 = (bf16[48,1664]{1,0:T(8,128)(2,1)S(1)}, bf16[48,1664]{1,0:T(8,128)(2,1)S(1)}, u32[]{:S(2)}, u32[]{:S(2)}) collective-permute-start(bf16[48,1664]{1,0:T(8,128)(2,1)S(1)} %pad_maximum_fusion.5.refs_0_), channel_id=1, source_target_pairs={{0,4},{1,5},{2,6},{3,7},{4,0},{5,1},{6,2},{7,3},{8,12},{9,13},{10,... | collective-permute-start | bytes 479240 | tf_op jit(solution)/shard_map/ppermute | solution.py:1030
  18.7 14.6 %collective-permute-start.2 = (bf16[48,1664]{1,0:T(8,128)(2,1)S(1)}, bf16[48,1664]{1,0:T(8,128)(2,1)S(1)}, u32[]{:S(2)}, u32[]{:S(2)}) collective-permute-start(bf16[48,1664]{1,0:T(8,128)(2,1)S(1)} %pad_maximum_fusion.5.refs_0_), channel_id=1, source_target_pairs={{0,8},{1,9},{2,10},{3,11},{4,12},{5,13},{6,14},{7,15},{8,0},{9,1},... | collective-permute-start | bytes 479240 | tf_op jit(solution)/shard_map/ppermute | solution.py:1030
  21.2 17.5 %collective-permute-start.3 = (bf16[48,1664]{1,0:T(8,128)(2,1)S(1)}, bf16[48,1664]{1,0:T(8,128)(2,1)S(1)}, u32[]{:S(2)}, u32[]{:S(2)}) collective-permute-start(bf16[48,1664]{1,0:T(8,128)(2,1)S(1)} %pad_maximum_fusion.5.refs_0_), channel_id=1, source_target_pairs={{0,12},{1,13},{2,14},{3,15},{4,8},{5,9},{6,10},{7,11},{8,4},{9,5},... | collective-permute-start | bytes 479240 | tf_op jit(solution)/shard_map/ppermute | solution.py:1030
  42.6 7.0 %collective-permute-start.12 = (bf16[2,2,48,384]{3,2,1,0:T(8,128)(2,1)}, bf16[2,2,48,384]{3,2,1,0:T(8,128)(2,1)S(1)}, u32[]{:S(2)}, u32[]{:S(2)}) collective-permute-start(bf16[2,2,48,384]{3,2,1,0:T(8,128)(2,1)} %bitcast.104), channel_id=1, source_target_pairs={{0,2},{1,3},{2,0},{3,1},{4,6},{5,7},{6,4},{7,5},{8,10},{9,11},{10,... | collective-permute-start | bytes 442376 | tf_op jit(solution)/shard_map/ppermute | solution.py:998
  42.6 10.6 %collective-permute-start.6 = (bf16[2,2,48,640]{3,2,1,0:T(8,128)(2,1)}, bf16[2,2,48,640]{3,2,1,0:T(8,128)(2,1)S(1)}, u32[]{:S(2)}, u32[]{:S(2)}) collective-permute-start(bf16[2,2,48,640]{3,2,1,0:T(8,128)(2,1)} %bitcast.99), channel_id=1, source_target_pairs={{0,2},{1,3},{2,0},{3,1},{4,6},{5,7},{6,4},{7,5},{8,10},{9,11},{10,... | collective-permute-start | bytes 737288 | tf_op jit(solution)/shard_map/ppermute | solution.py:998
  44.6 6.8 %collective-permute-start.8 = (bf16[2,2,48,640]{3,2,1,0:T(8,128)(2,1)}, bf16[2,2,48,640]{3,2,1,0:T(8,128)(2,1)S(1)}, u32[]{:S(2)}, u32[]{:S(2)}) collective-permute-start(bf16[2,2,48,640]{3,2,1,0:T(8,128)(2,1)} %bitcast.101), channel_id=1, source_target_pairs={{0,16},{1,17},{2,18},{3,19},{4,20},{5,21},{6,22},{7,23},{8,24},{9,... | collective-permute-start | bytes 737288 | tf_op jit(solution)/shard_map/ppermute | solution.py:998
  46.1 21.5 %collective-permute-start.10 = (bf16[816,768]{1,0:T(8,128)(2,1)}, bf16[816,768]{1,0:T(8,128)(2,1)S(1)}, u32[]{:S(2)}, u32[]{:S(2)}) collective-permute-start(bf16[816,768]{1,0:T(8,128)(2,1)} %get-tuple-element.70.refs_4_.refs_6_), channel_id=1, source_target_pairs={{0,1},{1,0},{2,3},{3,2},{4,5},{5,4},{6,7},{7,6},{8,9},{9,8},{10,11... | collective-permute-start | bytes 3760136 | tf_op jit(solution)/shard_map/ppermute | solution.py:998
  51.6 13.0 %collective-permute-start.9 = (bf16[2,2,2,48,640]{4,3,2,1,0:T(8,128)(2,1)S(1)}, bf16[2,2,2,48,640]{4,3,2,1,0:T(8,128)(2,1)}, u32[]{:S(2)}, u32[]{:S(2)}) collective-permute-start(bf16[2,2,2,48,640]{4,3,2,1,0:T(8,128)(2,1)S(1)} %pad_maximum_fusion.2), channel_id=1, source_target_pairs={{0,2},{1,3},{2,0},{3,1},{4,6},{5,7},{6,4},{7,5},{8,10},{9,11},{10,... | collective-permute-start | bytes 1474568 | tf_op jit(solution)/shard_map/ppermute | solution.py:998
  53.3 14.3 %collective-permute-start.7 = (bf16[2,2,2,48,640]{4,3,2,1,0:T(8,128)(2,1)S(1)}, bf16[2,2,2,48,640]{4,3,2,1,0:T(8,128)(2,1)}, u32[]{:S(2)}, u32[]{:S(2)}) collective-permute-start(bf16[2,2,2,48,640]{4,3,2,1,0:T(8,128)(2,1)S(1)} %pad_maximum_fusion.1.later_ref), channel_id=1, source_target_pairs={{0,16},{1,17},{2,18},{3,19},{4,20},{5,21},{6,22},{7,23},{8,24},{9,... | collective-permute-start | bytes 1474568 | tf_op jit(solution)/shard_map/ppermute | solution.py:998
  55.0 32.5 %collective-permute-start.14 = (bf16[384,768]{1,0:T(8,128)(2,1)S(1)}, bf16[384,768]{1,0:T(8,128)(2,1)}, u32[]{:S(2)}, u32[]{:S(2)}) collective-permute-start(bf16[384,768]{1,0:T(8,128)(2,1)S(1)} %bitcast.88), channel_id=1, source_target_pairs={{0,16},{1,17},{2,18},{3,19},{4,20},{5,21},{6,22},{7,23},{8,24},{9,... | collective-permute-start | bytes 1769480 | tf_op jit(solution)/shard_map/ppermute | solution.py:998
  57.7 37.1 %all-to-all-start.1 = ((bf16[16,112,128]{2,1,0:T(8,128)(2,1)}), bf16[16,112,128]{2,1,0:T(8,128)(2,1)}, u32[]{:S(2)}, u32[]{:S(2)}) async-start(bf16[16,112,128]{2,1,0:T(8,128)(2,1)} %bitcast.79), calls=%async_computation.1 | async-start | bytes 917504 | tf_op jit(solution)/shard_map/all_to_all | solution.py:1254
  94.8 17.6 %all-to-all-start = ((bf16[16,112,128]{2,1,0:T(8,128)(2,1)}), bf16[16,112,128]{2,1,0:T(8,128)(2,1)S(1)}, u32[]{:S(2)}, u32[]{:S(2)}) async-start(bf16[16,112,128]{2,1,0:T(8,128)(2,1)} %bitcast.94), calls=%async_computation | async-start | bytes 917504 | tf_op jit(solution)/shard_map/all_to_all | solution.py:1254
  101.3 31.1 %collective-permute-start.18 = (bf16[288,768]{1,0:T(8,128)(2,1)}, bf16[288,768]{1,0:T(8,128)(2,1)S(1)}, u32[]{:S(2)}, u32[]{:S(2)}) collective-permute-start(bf16[288,768]{1,0:T(8,128)(2,1)} %shard_map.235.cot_ref), channel_id=1, source_target_pairs={{0,16},{1,17},{2,18},{3,19},{4,20},{5,21},{6,22},{7,23},{8,24},{9,... | collective-permute-start | bytes 1327112 | tf_op jit(solution)/shard_map/ppermute | solution.py:998
  102.9 11.1 %collective-permute-start.15 = (f32[3,8,512]{2,1,0:T(8,128)S(1)}, f32[3,8,512]{2,1,0:T(8,128)S(1)}, u32[]{:S(2)}, u32[]{:S(2)}) collective-permute-start(f32[3,8,512]{2,1,0:T(8,128)S(1)} %copy-done.42), channel_id=1, source_target_pairs={{0,2},{1,3},{2,4},{3,5},{4,6},{5,7},{6,8},{7,9},{8,10},{9,11},{10,... | collective-permute-start | bytes 147464 | tf_op jit(solution)/shard_map/ppermute | solution.py:1009
  106.7 7.3 %collective-permute-start.16 = (f32[3,8,512]{2,1,0:T(8,128)S(1)}, f32[3,8,512]{2,1,0:T(8,128)S(1)}, u32[]{:S(2)}, u32[]{:S(2)}) collective-permute-start(f32[3,8,512]{2,1,0:T(8,128)S(1)} %copy-done.42), channel_id=1, source_target_pairs={{2,0},{3,1},{4,2},{5,3},{6,4},{7,5},{8,6},{9,7},{10,8},{11,9},{12,... | collective-permute-start | bytes 147464 | tf_op jit(solution)/shard_map/ppermute | solution.py:1009
  112.5 20.0 %collective-permute-start.17 = (bf16[1792,128]{1,0:T(8,128)(2,1)S(1)}, bf16[1792,128]{1,0:T(8,128)(2,1)S(1)}, u32[]{:S(2)}, u32[]{:S(2)}) collective-permute-start(bf16[1792,128]{1,0:T(8,128)(2,1)S(1)} %bitcast.92), channel_id=1, source_target_pairs={{0,16},{1,17},{2,18},{3,19},{4,20},{5,21},{6,22},{7,23},{8,24},{9,... | collective-permute-start | bytes 1376264 | tf_op jit(solution)/shard_map/ppermute | solution.py:998
  127.6 25.6 %all-to-all-start.2 = ((bf16[16,224,128]{2,1,0:T(8,128)(2,1)}), bf16[16,224,128]{2,1,0:T(8,128)(2,1)S(1)}, u32[]{:S(2)}, u32[]{:S(2)}) async-start(bf16[16,224,128]{2,1,0:T(8,128)(2,1)} %bitcast.85), calls=%async_computation.2 | async-start | bytes 1835008 | tf_op jit(solution)/shard_map/all_to_all | solution.py:1254
  163.3 42.1 %collective-permute-start.28 = (bf16[384,384]{1,0:T(8,128)(2,1)S(1)}, bf16[384,384]{1,0:T(8,128)(2,1)S(1)}, u32[]{:S(2)}, u32[]{:S(2)}) collective-permute-start(bf16[384,384]{1,0:T(8,128)(2,1)S(1)} %bitcast.95), channel_id=1, source_target_pairs={{0,16},{1,17},{2,18},{3,19},{4,20},{5,21},{6,22},{7,23},{8,24},{9,... | collective-permute-start | bytes 884744 | tf_op jit(solution)/shard_map/ppermute | solution.py:998
  165.1 22.8 %collective-permute-start.20 = (bf16[576,384]{1,0:T(8,128)(2,1)S(1)}, bf16[576,384]{1,0:T(8,128)(2,1)S(1)}, u32[]{:S(2)}, u32[]{:S(2)}) collective-permute-start(bf16[576,384]{1,0:T(8,128)(2,1)S(1)} %pad_maximum_fusion.3.msg_ref), channel_id=1, source_target_pairs={{0,2},{1,3},{2,4},{3,5},{4,6},{5,7},{6,8},{7,9},{8,10},{9,11},{10,... | collective-permute-start | bytes 1327112 | tf_op jit(solution)/shard_map/ppermute | solution.py:1009
  168.8 19.1 %collective-permute-start.21 = (bf16[576,384]{1,0:T(8,128)(2,1)S(1)}, bf16[576,384]{1,0:T(8,128)(2,1)S(1)}, u32[]{:S(2)}, u32[]{:S(2)}) collective-permute-start(bf16[576,384]{1,0:T(8,128)(2,1)S(1)} %pad_maximum_fusion.3.msg_ref), channel_id=1, source_target_pairs={{2,0},{3,1},{4,2},{5,3},{6,4},{7,5},{8,6},{9,7},{10,8},{11,9},{12,... | collective-permute-start | bytes 1327112 | tf_op jit(solution)/shard_map/ppermute | solution.py:1009
  202.9 14.9 %collective-permute-start.25 = (bf16[384,640]{1,0:T(8,128)(2,1)}, bf16[384,640]{1,0:T(8,128)(2,1)S(1)}, u32[]{:S(2)}, u32[]{:S(2)}) collective-permute-start(bf16[384,640]{1,0:T(8,128)(2,1)} %get-tuple-element.112), channel_id=1, source_target_pairs={{0,2},{1,3},{2,0},{3,1},{4,6},{5,7},{6,4},{7,5},{8,10},{9,11},{10,... | collective-permute-start | bytes 1474568 | tf_op jit(solution)/shard_map/ppermute | solution.py:998
  205.5 22.7 %collective-permute-start.29 = (bf16[192,384]{1,0:T(8,128)(2,1)S(1)}, bf16[192,384]{1,0:T(8,128)(2,1)S(1)}, u32[]{:S(2)}, u32[]{:S(2)}) collective-permute-start(bf16[192,384]{1,0:T(8,128)(2,1)S(1)} %bitcast.103), channel_id=1, source_target_pairs={{0,2},{1,3},{2,0},{3,1},{4,6},{5,7},{6,4},{7,5},{8,10},{9,11},{10,... | collective-permute-start | bytes 442376 | tf_op jit(solution)/shard_map/ppermute | solution.py:998
  205.6 13.3 %collective-permute-start.22 = (bf16[384,640]{1,0:T(8,128)(2,1)S(1)}, bf16[384,640]{1,0:T(8,128)(2,1)S(1)}, u32[]{:S(2)}, u32[]{:S(2)}) collective-permute-start(bf16[384,640]{1,0:T(8,128)(2,1)S(1)} %copy-done.28), channel_id=1, source_target_pairs={{0,16},{1,17},{2,18},{3,19},{4,20},{5,21},{6,22},{7,23},{8,24},{9,... | collective-permute-start | bytes 1474568 | tf_op jit(solution)/shard_map/ppermute | solution.py:998
  217.9 10.3 %collective-permute-start.26 = (bf16[192,640]{1,0:T(8,128)(2,1)S(1)}, bf16[192,640]{1,0:T(8,128)(2,1)S(1)}, u32[]{:S(2)}, u32[]{:S(2)}) collective-permute-start(bf16[192,640]{1,0:T(8,128)(2,1)S(1)} %bitcast.97), channel_id=1, source_target_pairs={{0,16},{1,17},{2,18},{3,19},{4,20},{5,21},{6,22},{7,23},{8,24},{9,... | collective-permute-start | bytes 737288 | tf_op jit(solution)/shard_map/ppermute | solution.py:998
  224.4 6.3 %collective-permute-start.24 = (bf16[192,640]{1,0:T(8,128)(2,1)S(1)}, bf16[192,640]{1,0:T(8,128)(2,1)S(1)}, u32[]{:S(2)}, u32[]{:S(2)}) collective-permute-start(bf16[192,640]{1,0:T(8,128)(2,1)S(1)} %bitcast.98), channel_id=1, source_target_pairs={{0,2},{1,3},{2,0},{3,1},{4,6},{5,7},{6,4},{7,5},{8,10},{9,11},{10,... | collective-permute-start | bytes 737288 | tf_op jit(solution)/shard_map/ppermute | solution.py:998
  234.0 8.3 %collective-permute-start.30 = (bf16[48,1664]{1,0:T(8,128)(2,1)}, bf16[48,1664]{1,0:T(8,128)(2,1)S(1)}, u32[]{:S(2)}, u32[]{:S(2)}) collective-permute-start(bf16[48,1664]{1,0:T(8,128)(2,1)} %get-tuple-element.116), channel_id=1, source_target_pairs={{0,4},{1,5},{2,6},{3,7},{4,0},{5,1},{6,2},{7,3},{8,12},{9,13},{10,... | collective-permute-start | bytes 479240 | tf_op jit(solution)/shard_map/ppermute | solution.py:1030
  237.9 12.5 %collective-permute-start.31 = (bf16[48,1664]{1,0:T(8,128)(2,1)}, bf16[48,1664]{1,0:T(8,128)(2,1)S(1)}, u32[]{:S(2)}, u32[]{:S(2)}) collective-permute-start(bf16[48,1664]{1,0:T(8,128)(2,1)} %get-tuple-element.117), channel_id=1, source_target_pairs={{0,8},{1,9},{2,10},{3,11},{4,12},{5,13},{6,14},{7,15},{8,0},{9,1},... | collective-permute-start | bytes 479240 | tf_op jit(solution)/shard_map/ppermute | solution.py:1030
  239.0 11.4 %collective-permute-start.32 = (bf16[48,1664]{1,0:T(8,128)(2,1)}, bf16[48,1664]{1,0:T(8,128)(2,1)S(1)}, u32[]{:S(2)}, u32[]{:S(2)}) collective-permute-start(bf16[48,1664]{1,0:T(8,128)(2,1)} %get-tuple-element.118), channel_id=1, source_target_pairs={{0,12},{1,13},{2,14},{3,15},{4,8},{5,9},{6,10},{7,11},{8,4},{9,5},... | collective-permute-start | bytes 479240 | tf_op jit(solution)/shard_map/ppermute | solution.py:1030
  254.3 4.6 %collective-permute-start.23 = (f32[256,768]{1,0:T(8,128)S(1)}, f32[256,768]{1,0:T(8,128)S(1)}, u32[]{:S(2)}, u32[]{:S(2)}) collective-permute-start(f32[256,768]{1,0:T(8,128)S(1)} %copy-done.27), channel_id=1, source_target_pairs={{0,1},{1,0},{2,3},{3,2},{4,5},{5,4},{6,7},{7,6},{8,9},{9,8},{10,11... | collective-permute-start | bytes 2359304 | tf_op jit(solution)/shard_map/ppermute | solution.py:998
  (50 other events, 179.2 us)

commit v2 on v1

--- a/solution.py
+++ b/solution.py
@@ -15,6 +15,22 @@
 LANES = 128
 FAR = 91
 CHUNK = 32
+FULL = 58
+GRANTS = {
+    "extend_kernel": 58,
+    "arrange_kernel": 24,
+    "prepare_kernel": 58,
+    "own_backward_kernel": 24,
+    "halo_backward_kernel": 24,
+    "sums_kernel": 16,
+    "input_kernel": 16,
+    "finish_input_kernel": 16,
+    "join_kernel": 16,
+    "stage_kernel": 16,
+    "finish_kernel": 16,
+    "output_kernel": 16,
+    "output_weight_kernel": 16,
+}
 TABLE = 32
 CODE_ROWS = 16
 GELU_A = 0.7978845608028654
@@ -25,7 +41,7 @@
 VMEM = pltpu.VMEM
 
 
-def params(mib=48):
+def params(mib):
     return pltpu.CompilerParams(vmem_limit_bytes=mib * 1024 * 1024)
 
 
@@ -51,6 +67,16 @@
 
 def tn(a, b):
     return lax.dot_general(a, b, (((0,), (0,)), ((), ())), preferred_element_type=F32)
+
+
+def exact_nt(a, b):
+    return lax.dot_general(
+        a,
+        b,
+        (((1,), (1,)), ((), ())),
+        precision=lax.Precision.HIGHEST,
+        preferred_element_type=F32,
+    )
 
 
 def iota(shape, dim):
@@ -293,6 +319,12 @@
             ]
 
 
+def code_columns(code_ref, first, count):
+    rows = code_ref[:, first : first + count].astype(BF16)
+    pick = (iota((8, LANES), 0) == 0).astype(BF16)
+    return tn(rows, pick)
+
+
 def forward_kernel(experts, chip_rows, count, far_ref, where_ref, *refs):
     forward_body(experts, chip_rows, far_ref, where_ref, refs[:count], *refs[count:])
 
@@ -305,8 +337,6 @@
     pieces,
     x_ref,
     came_ref,
-    code_own_ref,
-    code_came_ref,
     bias_ref,
     earlier_ref,
     hid_ref,
@@ -314,17 +344,19 @@
     k_ref,
     v_ref,
     gain_ref,
+    small_ref,
+    code_ref,
     low_ref,
     lse_ref,
-    wa_ref,
-    wb_ref,
-    code_ref,
     q_all,
     k_all,
     v_all,
-    code_row,
     raw,
     prob,
+    wa_ref,
+    wb_ref,
+    hid_scr,
+    code_col,
 ):
     del earlier_ref
     step = pl.program_id(0)
@@ -337,24 +369,21 @@
     @pl.when(step == 0)
     def _():
         join_weights(chip_rows, where_ref, pieces, wa_ref, wb_ref)
-        for chip in range(3):
-            for ref, which in ((code_own_ref, core), (code_came_ref, 1 - core)):
-                first = pl.multiple_of(chip * own + which * tok, tok)
-                row = chip * (tok + CODE_ROWS) + tok
-                pick = (iota((CODE_ROWS, LANES), 0) == 0).astype(BF16)
-                code_ref[pl.ds(first, tok), :] = tn(ref[row : row + CODE_ROWS, :], pick).astype(BF16)
+        small_ref[...] = wb_ref[:, split - LANES :]
         gain_ref[...] = picked_rows(wb_ref[:, split - LANES :], experts)
-        code_row[...] = picked_rows(code_ref[...], 0)
+        code_ref[...] = jnp.zeros_like(code_ref)
 
     @pl.when(step < 3)
     def _():
         for ref, which in ((x_ref, core), (came_ref, 1 - core)):
             tokens = ref[:tok, :].astype(F32)
             scale = lax.rsqrt(jnp.mean(tokens * tokens, axis=-1, keepdims=True) + EPSILON)
-            hid_ref[pl.ds(pl.multiple_of(which * tok, tok), tok), :] = (
+            hid_scr[pl.ds(pl.multiple_of(which * tok, tok), tok), :] = (
                 tokens * scale * gain_ref[0:1, :]
             ).astype(BF16)
-        hidden = hid_ref[...]
+            first = pl.multiple_of(step * own + which * tok, tok)
+            code_ref[:, pl.ds(first, tok)] = ref[tok : tok + 8, :tok].astype(F32)
+        hidden = hid_scr[...]
         second = nn(hidden, wb_ref[:, : split - LANES]).astype(BF16)
         k_ref[:, :cut] = nn(hidden, wa_ref[:, half:]).astype(BF16)
         k_ref[:, cut:] = second[:, : half - cut]
@@ -368,6 +397,8 @@
             query = nn(hidden, wa_ref[:, :half]).astype(BF16)
             q_ref[...] = query
             q_all[...] = query
+            hid_ref[...] = hidden
+            code_col[...] = code_columns(code_ref, own, own)
 
     @pl.when(step >= 3)
     def _():
@@ -391,8 +422,8 @@
                 found = []
                 for first in range(0, BLK, CHUNK):
                     part = slice(first, first + CHUNK)
-                    here = own + block * BLK + first
-                    mask = code_ref[here : here + CHUNK, 0:1].astype(F32) == code_row[0:1, cols]
+                    here = block * BLK + first
+                    mask = code_col[here : here + CHUNK, 0:1] == code_ref[0:1, cols]
                     scores = masked_scores(
                         raw[turn, part, :],
                         bias_ref[turn, part, :],
@@ -411,8 +442,29 @@
             lse_ref[0, 0:2, rows] = jnp.transpose(logs)[0:2, :]
 
 
-def halo_query_kernel(hid_ref, wa_ref, q_ref):
-    q_ref[...] = nn(hid_ref[...], wa_ref[:, : q_ref.shape[1]]).astype(BF16)
+def halo_query_kernel(chip_rows, where_ref, x_ref, came_ref, gain_ref, *refs):
+    pieces, (q_ref, hid_scr, wa_ref) = refs[:-3], refs[-3:]
+    half = q_ref.shape[1]
+    core = where_ref[0]
+    tok = x_ref.shape[0] - CODE_ROWS
+
+    @pl.when(pl.program_id(0) == 0)
+    def _():
+        rows = pieces[0].shape[0]
+        if len(pieces) == 1:
+            wa_ref[...] = pieces[0][...]
+        else:
+            for turn in range(2):
+                place = where_ref[1] if turn == 0 else 1 - where_ref[1]
+                wa_ref[pl.ds(pl.multiple_of(place * rows, rows), rows), :] = pieces[turn][...]
+
+    for ref, which in ((x_ref, core), (came_ref, 1 - core)):
+        tokens = ref[:tok, :].astype(F32)
+        scale = lax.rsqrt(jnp.mean(tokens * tokens, axis=-1, keepdims=True) + EPSILON)
+        hid_scr[pl.ds(pl.multiple_of(which * tok, tok), tok), :] = (
+            tokens * scale * gain_ref[0:1, :]
+        ).astype(BF16)
+    q_ref[...] = nn(hid_scr[...], wa_ref[:, :half]).astype(BF16)
 
 
 def turned(rows):
@@ -423,9 +475,19 @@
     return tn(parts.astype(BF16), pick.astype(BF16))
 
 
-def delta_rows(parts):
-    parts = parts.astype(F32)
-    return parts[0:8] + parts[8:16] + parts[16:24]
+def packed_rows(rows):
+    parts = [piece.astype(F32) for piece in three_parts(rows)]
+    halves = [
+        jnp.concatenate([part[:, first : first + LANES] for part in parts], axis=1)
+        for first in (0, LANES)
+    ]
+    return jnp.concatenate(halves, axis=0).astype(BF16)
+
+
+def unpacked_rows(packed):
+    packed = packed.astype(F32)
+    total = sum(packed[:, first : first + LANES] for first in range(0, 3 * LANES, LANES))
+    return jnp.concatenate([total[:8], total[8:]], axis=1)
 
 
 def rolled_left(value, steps):
@@ -470,7 +532,7 @@
     edge = (window - near) // 2
     lanes = pl.ds(pl.multiple_of(pair * LANES, LANES), LANES)
     lane = iota((BLK, LANES), 1)
-    code_row = picked_rows(code_ref[...], 0)
+    codes = code_columns(code_ref, own, own)
     dk_ref[...] = jnp.zeros_like(dk_ref)
     dv_ref[...] = jnp.zeros_like(dv_ref)
     side = iota((window, LANES), 0)
@@ -487,7 +549,7 @@
         mine = slice((blocks - block) * BLK, (2 * blocks - block) * BLK)
         first = block * deep
         gctx_all = msg_ref[first : first + BLK, lanes]
-        deltas = turned(delta_rows(msg_ref[first + BLK : first + BLK + 24, :BLK]))
+        deltas = turned(unpacked_rows(msg_ref[first + BLK : first + BLK + 16, :]))
         logs = turned(lse_ref[0, :, rows])
         outs = []
         for turn in range(2):
@@ -499,8 +561,8 @@
             log = logs[:, turn : turn + 1]
             for start in range(0, BLK, CHUNK):
                 part = slice(start, start + CHUNK)
-                here = own + block * BLK + start
-                mask = code_ref[here : here + CHUNK, 0:1].astype(F32) == code_row[0:1, cols]
+                here = block * BLK + start
+                mask = codes[here : here + CHUNK, 0:1] == code_ref[0:1, cols]
                 scores = masked_scores(
                     raw[turn, part, :],
                     bias_ref[turn, part, :],
@@ -561,21 +623,23 @@
     code_ref,
     dka_ref,
     dva_ref,
+    earlier_ref,
     dk_ref,
     dv_ref,
     delta_ref,
 ):
+    del earlier_ref
     pair = pl.program_id(0)
     own = k_ref.shape[0]
     half = LANES
-    code_row = picked_rows(code_ref[...], 0)
+    codes = code_columns(code_ref, own, own)
     lanes = pl.ds(pl.multiple_of(pair * LANES, LANES), LANES)
     deep = gp_ref.shape[0] // 2
     for side, g_side in enumerate((gp_ref, gn_ref)):
         for block in range(2):
             first = block * deep + BLK
-            delta_ref[side, :, block * BLK : (block + 1) * BLK] = delta_rows(
-                g_side[first : first + 24, :BLK]
+            delta_ref[side, :, block * BLK : (block + 1) * BLK] = unpacked_rows(
+                g_side[first : first + 16, :]
             )
     total_k = dka_ref[...]
     total_v = dva_ref[...]
@@ -599,9 +663,8 @@
         count = cols.stop - cols.start
         lse_ref = lp_ref if side == 0 else ln_ref
         places = slice(rows.start // BLK * deep, rows.start // BLK * deep + BLK)
-        code_col = code_ref[own + cols.start : own + cols.stop, 0:1].astype(F32)
         first = 2 * own * side + rows.start
-        mask = code_col == code_row[0:1, first : first + BLK]
+        mask = codes[cols, 0:1] == code_ref[0:1, first : first + BLK]
         for turn in range(2):
             head = pair * 2 + turn
             query = own_half(q_side[rows, :], turn)
@@ -642,6 +705,13 @@
     return route_hot, slot_hot, gate
 
 
+def join_halves(where_ref, near_ref, far_ref, out_ref):
+    half = near_ref.shape[0]
+    side = where_ref[1]
+    out_ref[pl.ds(pl.multiple_of(side * half, half), half), :] = near_ref[...]
+    out_ref[pl.ds(pl.multiple_of((1 - side) * half, half), half), :] = far_ref[...]
+
+
 def before_kernel(
     cap,
     depth,
@@ -660,17 +730,15 @@
     hid_ref,
     prob_ref,
     msg_out_ref,
-    wo_ref,
     flat,
     msg,
+    wo_ref,
 ):
     core = core_ref[0]
     tok = x_ref.shape[0]
     width = own_ref.shape[1]
     rows = pl.ds(pl.multiple_of(core * tok, tok), tok)
-    side = core_ref[1]
-    wo_ref[pl.ds(pl.multiple_of(side * width, width), width), :] = wonear_ref[...]
-    wo_ref[pl.ds(pl.multiple_of((1 - side) * width, width), width), :] = wofar_ref[...]
+    join_halves(core_ref, wonear_ref, wofar_ref, wo_ref)
     own_w = wo_ref[pl.ds(pl.multiple_of(core * width, width), width), :]
     other_w = wo_ref[pl.ds(pl.multiple_of((1 - core) * width, width), width), :]
     mid_ref[...] = (
@@ -816,12 +884,14 @@
     dv_ref,
     extra_ref,
     tab_ref,
+    earlier_ref,
     senda_ref,
     keepa_ref,
     sendb_ref,
     keepb_ref,
     total,
 ):
+    del earlier_ref
     rows = hid_ref.shape[1]
     half = dq_ref.shape[1]
     split = keepa_ref.shape[1]
@@ -852,26 +922,49 @@
         sendb_ref[out, :] = gone.astype(BF16)
 
 
-def join_kernel(
-    chip_rows, where_ref, keepa_ref, camea_ref, keepb_ref, cameb_ref, keepo_ref, cameo_ref, later_ref, *refs
-):
+def add_blocks(counts, refs, total):
+    first, at = 0, 0
+    for count in counts:
+        value = refs[at][...]
+        for ref in refs[at + 1 : at + count]:
+            value = value + ref[...].astype(F32)
+        last = first + value.shape[1]
+        total[:, first:last] = value
+        first, at = last, at + count
+
+
+def stage_kernel(counts, groups, rows, where_at, where_ref, later_ref, *refs):
     del later_ref
-    kept_ref, total = refs[0], refs[-1]
-    first = 0
-    for kept, came in ((keepa_ref, camea_ref), (keepb_ref, cameb_ref), (keepo_ref, cameo_ref)):
-        last = first + kept.shape[1]
-        total[:, first:last] = kept[...] + came[...].astype(F32)
-        first = last
-    mine = where_ref[5]
-    kept_ref[...] = total[pl.ds(pl.multiple_of(mine * chip_rows, 8), chip_rows), :]
-    for other, ref in enumerate(refs[1:-1]):
-        place = mine ^ (other + 1)
-        ref[...] = total[pl.ds(pl.multiple_of(place * chip_rows, 8), chip_rows), :].astype(BF16)
-
-
-def input_kernel(core_ref, dq_ref, dk_ref, dv_ref, wa_ref, wb_ref, later_ref, keep_ref, send_ref):
+    blocks, (gone_ref, kept_ref, total) = refs[:-3], refs[-3:]
+    add_blocks(counts, blocks, total)
+    mine = where_ref[where_at]
+    for group in range(groups):
+        out = slice(group * rows, (group + 1) * rows)
+        base = group * 2 * rows
+        kept_ref[out, :] = total[pl.ds(pl.multiple_of(base + mine * rows, 8), rows), :]
+        gone = total[pl.ds(pl.multiple_of(base + (1 - mine) * rows, 8), rows), :]
+        gone_ref[out, :] = gone.astype(gone_ref.dtype)
+
+
+def join_kernel(counts, groups, rows, where_ref, later_ref, *refs):
     del later_ref
-    core = core_ref[0]
+    blocks, outs, total = refs[: sum(counts)], refs[sum(counts) : -1], refs[-1]
+    add_blocks(counts, blocks, total)
+    for other, ref in enumerate(outs):
+        place = where_ref[5] ^ other
+        for group in range(groups):
+            first = pl.multiple_of((group * len(outs) + place) * rows, 8)
+            ref[group * rows : (group + 1) * rows, :] = total[pl.ds(first, rows), :].astype(
+                ref.dtype
+            )
+
+
+def input_kernel(chip_rows, where_ref, dq_ref, dk_ref, dv_ref, later_ref, *refs):
+    del later_ref
+    pieces, (keep_ref, send_ref, token_ref, wa_ref, wb_ref) = refs[:-5], refs[-5:]
+    token_ref[...] = jnp.zeros_like(token_ref)
+    join_weights(chip_rows, where_ref, pieces, wa_ref, wb_ref)
+    core = where_ref[0]
     half = dq_ref.shape[1]
     split = wa_ref.shape[1]
     cut = split - half
@@ -886,6 +979,91 @@
         )
 
 
+def finish_input_kernel(part_ref, came_ref, x_ref, gain_ref, mid_ref, out_ref, token_ref):
+    token_ref[...] = jnp.zeros_like(token_ref)
+    grad_hidden = part_ref[...] + came_ref[...]
+    tokens = x_ref[...].astype(F32)
+    scale = lax.rsqrt(jnp.mean(tokens * tokens, axis=-1, keepdims=True) + EPSILON)
+    normed = tokens * scale
+    grad_normed = grad_hidden * gain_ref[0:1, :]
+    out_ref[...] = (
+        mid_ref[...]
+        + scale
+        * (grad_normed - normed * jnp.mean(grad_normed * normed, axis=-1, keepdims=True))
+    ).astype(BF16)
+
+
+def output_weight_kernel(
+    where_ref, ctx_ref, ctx_came_ref, ga_ref, ga_came_ref, later_ref, gone_ref, kept_ref, token_ref, ga, total
+):
+    del later_ref
+    token_ref[...] = jnp.zeros_like(token_ref)
+    core = where_ref[0]
+    tok = ga_ref.shape[0]
+    half = ctx_ref.shape[1]
+    ga[pl.ds(pl.multiple_of(core * tok, tok), tok), :] = ga_ref[...]
+    ga[pl.ds(pl.multiple_of((1 - core) * tok, tok), tok), :] = ga_came_ref[...]
+    cols = ga[...]
+    total[pl.ds(pl.multiple_of(core * half, half), half), :] = tn(ctx_ref[...], cols)
+    total[pl.ds(pl.multiple_of((1 - core) * half, half), half), :] = tn(ctx_came_ref[...], cols)
+    mine = where_ref[3]
+    gone_ref[...] = total[pl.ds(pl.multiple_of((1 - mine) * half, half), half), :].astype(BF16)
+    kept_ref[...] = total[pl.ds(pl.multiple_of(mine * half, half), half), :]
+
+
+def finish_kernel(
+    experts,
+    buckets,
+    where_ref,
+    kept_ref,
+    came_ref,
+    wq_ref,
+    wk_ref,
+    wv_ref,
+    gain_ref,
+    q_ref,
+    k_ref,
+    v_ref,
+    o_ref,
+    router_ref,
+    gains_ref,
+    table_ref,
+):
+    core = where_ref[0]
+    half = q_ref.shape[1] // 2
+    split = (kept_ref.shape[1] - half) // 2
+    cut = split - half
+    last = kept_ref.shape[1] - LANES
+    for source, which in ((kept_ref, core), (came_ref, 1 - core)):
+        cols = pl.ds(pl.multiple_of(which * half, half), half)
+        q_ref[:, cols] = source[:, :half]
+        k_ref[:, cols] = jnp.concatenate(
+            [source[:, half:split], source[:, split + half : split + 2 * half - cut]], axis=1
+        )
+        o_ref[:, cols] = source[:, split : split + half]
+        v_ref[:, cols] = source[:, last - half : last]
+    kept = kept_ref[:, last:]
+    came = came_ref[:, last:]
+    both = kept + came
+    router_ref[...] = both[:, :experts]
+    weighted = (
+        q_ref[...] * wq_ref[...].astype(F32)
+        + k_ref[...] * wk_ref[...].astype(F32)
+        + v_ref[...] * wv_ref[...].astype(F32)
+    )
+    gain_one = jnp.sum(weighted, axis=1, keepdims=True) / gain_ref[...].astype(F32)
+    lane = iota(both.shape, 1)
+    cols = jnp.where(lane == 0, gain_one, jnp.where(lane == 1, both[:, experts : experts + 1], 0.0))
+    gains_ref[...] = exact_nt((iota((8, LANES), 0) == iota((8, LANES), 1)).astype(F32), cols)
+    heads = table_ref.shape[1] // 2
+    own = kept[:heads, LANES - buckets :]
+    other = came[:heads, LANES - buckets :]
+    first = jnp.where(core == 0, own, other)
+    second = jnp.where(core == 0, other, own)
+    eye = (iota((buckets, buckets), 0) == iota((buckets, buckets), 1)).astype(F32)
+    table_ref[...] = exact_nt(eye, jnp.concatenate([first, second], axis=0))
+
+
 def after_kernel(
     cap,
     depth,
@@ -898,7 +1076,8 @@
     prob_ref,
     small_ref,
     gain_ref,
-    wo_ref,
+    wonear_ref,
+    wofar_ref,
     meta_ref,
     own_ref,
     came_ref,
@@ -912,6 +1091,7 @@
     flat,
     msg,
     low_scr,
+    wo_ref,
 ):
     del earlier_ref
     core = core_ref[0]
@@ -936,6 +1116,7 @@
     gmid_ref[...] = grad_middle
     low = grad_middle.astype(BF16)
     low_scr[...] = low
+    join_halves(core_ref, wonear_ref, wofar_ref, wo_ref)
     own_heads = pl.ds(pl.multiple_of(core * width, width), width)
     other_heads = pl.ds(pl.multiple_of((1 - core) * width, width), width)
     gmine_ref[...] = low_scr[:, own_heads]
@@ -955,10 +1136,7 @@
             preferred_element_type=F32,
         )
         out_ref[:tok, :] = gctx
-        parts = [piece.astype(F32) for piece in three_parts(delta)]
-        parts = jnp.concatenate(parts + [jnp.zeros((8, tok), F32)], axis=0)
-        parts = jnp.concatenate([parts, jnp.zeros((32, width - tok), F32)], axis=1)
-        out_ref[tok:, :] = parts.astype(BF16)
+        out_ref[tok:, :] = packed_rows(delta)
     router = tn(hid_ref[...], grad_logits)
     gain = lax.dot_general(
         grad_hidden * normed,
@@ -971,7 +1149,8 @@
     sums_ref[...] = jnp.where(lane < experts, router, jnp.where(lane == experts, gain, 0.0))
 
 
-def output_kernel(cap, depth, msg_in_ref, mid_ref, prob_ref, meta_ref, out_ref, flat, msg):
+def output_kernel(cap, depth, msg_in_ref, mid_ref, prob_ref, meta_ref, out_ref, token_ref, flat, msg):
+    token_ref[...] = jnp.zeros_like(token_ref)
     tok = out_ref.shape[0]
     read_message(msg_in_ref, flat, msg, cap, depth, 1, 2)
     hot = (iota((tok, flat.shape[0]), 1) == meta_ref[:, 0:1]).astype(BF16)
@@ -1066,13 +1245,12 @@
     kernel,
     outs,
     *args,
-    us=2.0,
+    us=0.3,
     grid=None,
     in_specs=None,
     out_specs=None,
     scratch=(),
     smem_first=False,
-    mib=58,
 ):
     if in_specs is None:
         in_specs = [whole(a.shape) for a in args]
@@ -1081,6 +1259,10 @@
     if out_specs is None:
         out_specs = [whole(o[0]) for o in outs]
     shapes = [jax.ShapeDtypeStruct(*o) for o in outs]
+    inner = kernel
+    while isinstance(inner, functools.partial):
+        inner = inner.func
+    mib = GRANTS.get(inner.__name__, FULL)
     return pl.pallas_call(
         kernel,
         out_shape=shapes,
@@ -1185,7 +1367,7 @@
         bias_table,
         routes[0],
         routes[0].reshape(1, tok),
-        us=3.0,
+        us=0.3,
         smem_first=True,
     )
 
@@ -1273,26 +1455,23 @@
     def pair_step(i):
         return jnp.maximum(i - 3, 0)
 
-    small_block = pl.BlockSpec((width, LANES), lambda *_: (0, split // LANES - 1))
-    hid_all, q_own, k_all, v_all, gains, ctx_low, lse_rows, w_a, w_b, codes = call(
+    small_block = whole((width, LANES))
+    hid_own, q_own, k_all, v_all, gains, small, codes, ctx_low, lse_rows = call(
         functools.partial(forward_kernel, experts, chip_rows, len(pieces)),
         [
-            ((rows_all, width), BF16),
+            ((own_rows, width), BF16),
             ((own_rows, half), BF16),
             ((rows_all, half), BF16),
             ((rows_all, half), BF16),
             ((8, width), F32),
+            ((width, LANES), BF16),
+            ((8, rows_all), F32),
             ((own_rows, half), BF16),
             ((pairs, 8, own_rows), F32),
-            ((width, split), BF16),
-            ((width, split), BF16),
-            ((rows_all, LANES), BF16),
         ],
         far_bias,
         where,
         *pieces,
-        three,
-        three_came,
         three,
         three_came,
         bias,
@@ -1304,30 +1483,30 @@
         + [
             pl.BlockSpec((long, width), lambda i: (chip_step(i), 0)),
             pl.BlockSpec((long, width), lambda i: (chip_step(i), 0)),
-            pl.BlockSpec((3 * long, tok), lambda *_: (0, 0)),
-            pl.BlockSpec((3 * long, tok), lambda *_: (0, 0)),
             pl.BlockSpec((2, BLK, near), lambda i: (pair_step(i), 0, 0)),
             anywhere(),
         ],
         out_specs=[
-            pl.BlockSpec((own_rows, width), lambda i: (chip_step(i), 0)),
+            whole((own_rows, width)),
             whole((own_rows, half)),
             pl.BlockSpec((own_rows, half), lambda i: (chip_step(i), 0)),
             pl.BlockSpec((own_rows, half), lambda i: (chip_step(i), 0)),
             whole((8, width)),
+            whole((width, LANES)),
+            whole((8, rows_all)),
             pl.BlockSpec((own_rows, LANES), lambda i: (0, pair_step(i))),
             pl.BlockSpec((1, 8, own_rows), lambda i: (pair_step(i), 0, 0)),
-            whole((width, split)),
-            whole((width, split)),
-            whole((rows_all, LANES)),
         ],
         scratch=[
             VMEM((own_rows, half), BF16),
             VMEM((rows_all, half), BF16),
             VMEM((rows_all, half), BF16),
-            VMEM((8, rows_all), F32),
             VMEM((2, BLK, 5 * BLK), F32),
             VMEM((2, BLK, 5 * BLK), BF16),
+            VMEM((width, split), BF16),
+            VMEM((width, split), BF16),
+            VMEM((own_rows, width), BF16),
+            VMEM((own_rows, LANES), F32),
         ],
     )
 
@@ -1339,8 +1518,7 @@
         scratch=msg_scratch,
     )[0]
 
-    hid_block = pl.BlockSpec((own_rows, width), lambda *_: (1, 0))
-    code_block = whole((rows_all, LANES))
+    code_block = whole((8, rows_all))
     far_block = whole((8, LANES))
     own_block = pl.BlockSpec((own_rows, LANES), lambda p: (1, p))
     all_block = pl.BlockSpec((rows_all, LANES), lambda p: (0, p))
@@ -1349,14 +1527,13 @@
     lse_block = pl.BlockSpec((1, 8, own_rows), lambda p: (p, 0, 0))
 
     ctx_came = place.swap(ctx_low, 0)
-    mid, hid_two, probs, msg, wo = call(
+    mid, hid_two, probs, msg = call(
         functools.partial(before_kernel, cap, depth, experts),
         [
             ((tok, width), F32),
             ((tok, width), BF16),
             ((tok, LANES), F32),
             (msg_shape, BF16),
-            ((width, width), BF16),
         ],
         where,
         x,
@@ -1364,7 +1541,7 @@
         ctx_came,
         wo_near,
         wo_far,
-        w_b,
+        small,
         gains,
         meta_col,
         meta_row,
@@ -1381,23 +1558,31 @@
             whole((tok, LANES)),
             whole((8, tok)),
         ],
-        scratch=msg_scratch,
+        scratch=msg_scratch + [VMEM((width, width), BF16)],
     )
     msg_in = exchange(msg)
     lse_prev = place.shift(lse_rows, 2)
     lse_next = place.shift(lse_rows, -2)
+    pieces_q = pieces[: len(pieces) // 2]
     q_halo = call(
-        halo_query_kernel,
+        functools.partial(halo_query_kernel, chip_rows),
         [((2 * own_rows, half), BF16)],
-        hid_all,
-        w_a,
-        us=2.0,
+        where,
+        three,
+        three_came,
+        gains,
+        *pieces_q,
+        us=0.3,
         grid=(2,),
         in_specs=[
-            pl.BlockSpec((own_rows, width), lambda i: (2 * i, 0)),
-            whole((width, split)),
-        ],
+            smem(),
+            pl.BlockSpec((long, width), lambda i: (2 * i, 0)),
+            pl.BlockSpec((long, width), lambda i: (2 * i, 0)),
+            whole((8, width)),
+        ]
+        + [whole(piece.shape) for piece in pieces_q],
         out_specs=[pl.BlockSpec((own_rows, half), lambda i: (i, 0))],
+        scratch=[VMEM((own_rows, width), BF16), VMEM((width, split), BF16)],
     )[0]
 
     fblk = 512
@@ -1413,9 +1598,9 @@
         cot_rows,
         w_in,
         w_out,
+        q_halo,
         lse_prev,
         lse_next,
-        q_halo,
         us=12.0,
         grid=(hidden_units // fblk,),
         in_specs=[
@@ -1478,7 +1663,7 @@
         functools.partial(after_kernel, cap, depth, experts),
         [((tok, width), F32)]
         + [((tok, half), BF16)] * 2
-        + [((tok + 32, half), BF16)] * 2
+        + [((tok + 16, half), BF16)] * 2
         + [((width, LANES), F32)],
         where,
         back_in,
@@ -1486,9 +1671,10 @@
         mid,
         hid_two,
         probs,
-        w_b,
+        small,
         gains,
-        wo,
+        wo_near,
+        wo_far,
         meta_col,
         ctx_low,
         ctx_came,
@@ -1503,28 +1689,30 @@
             whole((tok, LANES)),
             small_block,
             whole((8, width)),
-            whole((width, width)),
+            whole((width // 2, width)),
+            whole((width // 2, width)),
             whole((tok, LANES)),
             whole((own_rows, half)),
             whole((own_rows, half)),
             anywhere(),
         ],
-        scratch=msg_scratch + [VMEM((tok, width), BF16)],
+        scratch=msg_scratch + [VMEM((tok, width), BF16), VMEM((width, width), BF16)],
     )
 
     gctx = place.ordered(gctx_mine, place.swap(gctx_theirs, 0), 0, 0, jnp.concatenate)
     gctx_prev = place.shift(gctx, 2)
     gctx_next = place.shift(gctx, -2)
 
-    output = call(
+    token = ((8, LANES), F32)
+    output, output_made = call(
         functools.partial(output_kernel, cap, depth),
-        [((tok, width), BF16)],
+        [((tok, width), BF16), token],
         back_in,
         mid,
         probs,
         meta_col,
         scratch=msg_scratch,
-    )[0]
+    )
 
     dq, dk_own, dv_own, tab = call(
         own_backward_kernel,
@@ -1564,6 +1752,28 @@
         ],
     )
 
+    order_a = seq_bits + near_bits
+    order_b = near_bits + seq_bits
+    joined = halved and len(seq_bits) == 1 and len(far) == 2
+    ga_came = place.swap(gattn_theirs, 0)
+    if joined:
+        gone_o, kept_o, sooner = call(
+            output_weight_kernel,
+            [((width // 2, half), BF16), ((width // 2, half), F32), token],
+            where,
+            ctx_low,
+            ctx_came,
+            gattn_mine,
+            ga_came,
+            tab,
+            in_specs=[smem()]
+            + [whole((own_rows, half))] * 2
+            + [whole((tok, half))] * 2
+            + [anywhere()],
+            scratch=[VMEM((own_rows, half), BF16), VMEM((width, half), F32)],
+        )
+    else:
+        sooner = tab
     halo_bias = pl.BlockSpec((2, LANES, BLK), lambda p: (p, 0, 0))
     dk, dv = call(
         halo_backward_kernel,
@@ -1582,7 +1792,8 @@
         codes,
         dk_own,
         dv_own,
-        us=9.0,
+        sooner,
+        us=7.0,
         grid=(pairs,),
         in_specs=[
             far_block,
@@ -1599,24 +1810,44 @@
             code_block,
             out_block,
             out_block,
+            anywhere(),
         ],
         out_specs=[out_block] * 2,
         scratch=[VMEM((2, 8, own_rows), F32)],
     )
 
-    ga_cols = place.ordered(gattn_mine, place.swap(gattn_theirs, 0), 0, 0, jnp.concatenate)
-    ctx_full = place.ordered(ctx_low, ctx_came, 0, 1, jnp.concatenate)
-    back_far = far[::-1]
-    total_o = tn(ctx_full, ga_cols)
-    order_a = seq_bits + near_bits
-    order_b = near_bits + seq_bits
-    joined = halved and len(seq_bits) == 1 and len(far) == 2
+
+    def input_parts(later):
+        return call(
+            functools.partial(input_kernel, chip_rows),
+            [((tok, width), F32), ((tok, width), F32), token],
+            where,
+            dq,
+            dk,
+            dv,
+            later,
+            *pieces,
+            us=0.3,
+            in_specs=[smem()]
+            + [whole((own_rows, half))] * 3
+            + [anywhere()]
+            + [whole(piece.shape) for piece in pieces],
+            scratch=[VMEM((width, split), BF16), VMEM((width, split), BF16)],
+        )
+
+    def input_gradient(part, part_gone):
+        return call(
+            finish_input_kernel,
+            [((tok, width), BF16), token],
+            part,
+            place.swap(part_gone, 0),
+            x,
+            gains,
+            grad_mid,
+        )
+
     if joined:
-        chip_bits = seq_bits + near_bits + far
-        gone_o, kept_o = place.halves(total_o, order_a[0], chip_bits)
-        half_o = kept_o + place.swap(gone_o, order_a[0]).astype(F32)
-        gone_o, kept_o = place.halves(half_o, order_a[1], order_a[1:] + far)
-        came_o = place.swap(gone_o, order_a[1])
+        came_o = place.swap(gone_o, order_a[0])
         gone_a, kept_a, gone_b, kept_b = call(
             functools.partial(sums_kernel, chip_rows),
             [
@@ -1626,119 +1857,136 @@
                 ((width // 2, split), F32),
             ],
             where,
-            hid_all,
+            hid_own,
             dq,
             dk,
             dv,
             extra,
             tab,
-            us=4.0,
+            came_o,
+            us=0.3,
             in_specs=[
                 smem(),
-                hid_block,
+                whole((own_rows, width)),
                 whole((own_rows, half)),
                 whole((own_rows, half)),
                 whole((own_rows, half)),
                 whole((width, LANES)),
                 whole((pairs, 8, LANES)),
+                anywhere(),
             ],
             scratch=[VMEM((width, split), F32)],
         )
-        later = half_a = kept_a + place.swap(gone_a, order_a[0]).astype(F32)
-        half_b = kept_b + place.swap(gone_b, order_b[0]).astype(F32)
-        gone_a, kept_a = place.halves(half_a, order_a[1], order_a[1:] + far)
-        gone_b, kept_b = place.halves(half_b, order_b[1], order_b[1:] + far)
+        came_a = place.swap(gone_a, order_a[0])
+        came_b = place.swap(gone_b, order_b[0])
+
+        masks = [mask for _, mask in place.several(far)[1]]
+        far_count = len(masks) + 1
+
+        def added(kernel, later, counts, blocks, outs, *how):
+            columns_all = sum(blocks[sum(counts[:at])].shape[1] for at in range(len(counts)))
+            height = blocks[0].shape[0]
+            return call(
+                functools.partial(kernel, counts, *how),
+                [((height // out, columns_all), dtype) for out, dtype in outs],
+                where,
+                later,
+                *blocks,
+                us=0.3,
+                in_specs=[smem(), anywhere()] + [whole(block.shape) for block in blocks],
+                scratch=[VMEM((height, columns_all), F32)],
+            )
+
+        def swapped(pieces):
+            return [place.swap_mask(piece, mask) for piece, mask in zip(pieces, masks)]
+
+        two = [(2, BF16), (2, F32)]
+        four = [(far_count, F32)] + [(far_count, BF16)] * len(masks)
+        gone_a, kept_a = added(
+            stage_kernel,
+            came_b,
+            (2, 2),
+            (kept_a, came_a, kept_o, came_o),
+            two,
+            far_count,
+            chip_rows,
+            4,
+        )
+        part, part_gone, part_made = input_parts(output_made)
+        pieces_z = added(
+            join_kernel, far_bias, (2,), (kept_b, came_b), four, 2, chip_rows
+        )
         came_a = place.swap(gone_a, order_a[1])
-        came_b = place.swap(gone_b, order_b[1])
+        came_z = swapped(pieces_z[1:])
+        grad_tokens, ended = input_gradient(part, part_gone)
+        pieces_a = added(join_kernel, part_made, (2,), (kept_a, came_a), four, 1, chip_rows)
+        gone_b, kept_b = added(
+            stage_kernel, ended, (far_count,), (pieces_z[0], *came_z), two, 1, chip_rows, 3
+        )
+        came_b = place.swap(gone_b, seq_bits[0])
+        came_z = swapped(pieces_a[1:])
+        gone, kept = added(
+            stage_kernel,
+            ended,
+            (far_count, 2),
+            (pieces_a[0], *came_z, kept_b, came_b),
+            [(2, F32), (2, F32)],
+            1,
+            rows_dev,
+            0,
+        )
     else:
-        hid_one = hid_all[own_rows : 2 * own_rows]
+        ga_cols = place.ordered(gattn_mine, ga_came, 0, 0, jnp.concatenate)
+        ctx_full = place.ordered(ctx_low, ctx_came, 0, 1, jnp.concatenate)
         cut = split - half
-        total_a = tn(hid_one, jnp.concatenate([dq, dk[:, :cut]], axis=1))
-        total_b = tn(hid_one, jnp.concatenate([dk[:, cut:], dv], axis=1))
-        later = total_a
+        total_a = tn(hid_own, jnp.concatenate([dq, dk[:, :cut]], axis=1))
+        total_b = tn(hid_own, jnp.concatenate([dk[:, cut:], dv], axis=1))
+        grad_tokens, _ = input_gradient(*input_parts(total_a)[:2])
         total_b = jnp.concatenate([total_b, extra], axis=1)
-        sums = jnp.concatenate([total_a, total_b, total_o], axis=1)
+        sums = jnp.concatenate([total_a, total_b, tn(ctx_full, ga_cols)], axis=1)
         sums = place.scatter(sums, seq_bits + near_bits + far[::-1])
-
-    part, part_gone = call(
-        input_kernel,
-        [((tok, width), F32), ((tok, width), F32)],
-        where,
-        dq,
-        dk,
-        dv,
-        w_a,
-        w_b,
-        later,
-        us=4.0,
-        in_specs=[smem()]
-        + [whole((own_rows, half))] * 3
-        + [whole((width, split))] * 2
-        + [anywhere()],
-    )
+        sums = sums.reshape(2, rows_dev, sums.shape[1])
+        gone = lax.dynamic_index_in_dim(sums, 1 - core, 0, keepdims=False)
+        kept = lax.dynamic_index_in_dim(sums, core, 0, keepdims=False)
+    came = place.swap(gone, 0)
     if joined:
-        columns_all = 2 * split + half
-        parts_z = call(
-            functools.partial(join_kernel, chip_rows),
-            [((chip_rows, columns_all), F32)] + [((chip_rows, columns_all), BF16)] * 3,
+        sum_q, sum_k, sum_v, sum_out, grad_router, gain_rows, table_sum = call(
+            functools.partial(finish_kernel, experts, buckets),
+            [((rows_dev, width), F32)] * 4
+            + [((rows_dev, experts), F32), ((8, rows_dev), F32), ((buckets, heads), F32)],
             where,
-            kept_a,
-            came_a,
-            kept_b,
-            came_b,
-            kept_o,
-            came_o,
-            part_gone,
-            in_specs=[smem()]
-            + [whole(v.shape) for v in (kept_a, came_a, kept_b, came_b, kept_o, came_o)]
-            + [anywhere()],
-            scratch=[VMEM((kept_a.shape[0], columns_all), F32)],
+            kept,
+            came,
+            w_query,
+            w_key,
+            w_value,
+            gain_attn[:, None],
+            smem_first=True,
         )
-        sums = parts_z[0]
-        for (_, mask), piece in zip(place.several(far)[1], parts_z[1:]):
-            sums = sums + place.swap_mask(piece, mask).astype(F32)
-    sums = sums.reshape(2, rows_dev, sums.shape[1])
-    gone = lax.dynamic_index_in_dim(sums, 1 - core, 0, keepdims=False)
-    kept = lax.dynamic_index_in_dim(sums, core, 0, keepdims=False)
-    came = place.swap(gone, 0)
-
-    def columns(first):
-        return place.ordered(
-            kept[:, first : first + half], came[:, first : first + half], 0, 1, jnp.concatenate
+        grad_gain_one, grad_gain_two = gain_rows[0], gain_rows[1]
+    else:
+
+        def columns(first):
+            return place.ordered(
+                kept[:, first : first + half], came[:, first : first + half], 0, 1, jnp.concatenate
+            )
+
+        sum_q, sum_k, sum_v = columns(0), columns(half), columns(2 * half)
+        sum_out = columns(3 * half + LANES)
+        extra_sum = kept[:, 3 * half : 3 * half + LANES] + came[:, 3 * half : 3 * half + LANES]
+        grad_router = extra_sum[:, :experts]
+        grad_gain_two = extra_sum[:, experts]
+        weighted = (
+            sum_q * w_query.astype(F32) + sum_k * w_key.astype(F32) + sum_v * w_value.astype(F32)
         )
-
-    sum_q, sum_k, sum_v = columns(0), columns(half), columns(2 * half)
-    sum_out = columns(3 * half + LANES)
-    extra_sum = kept[:, 3 * half : 3 * half + LANES] + came[:, 3 * half : 3 * half + LANES]
-    grad_router = extra_sum[:, :experts]
-    grad_gain_two = extra_sum[:, experts]
-    weighted = (
-        sum_q * w_query.astype(F32) + sum_k * w_key.astype(F32) + sum_v * w_value.astype(F32)
-    )
-    grad_gain_one = jnp.sum(weighted, axis=1) / gain_attn.astype(F32)
-
-    grad_hidden = part + place.swap(part_gone, 0)
-    tokens = x.astype(F32)
-    scale_one = lax.rsqrt(jnp.mean(tokens * tokens, axis=-1, keepdims=True) + EPSILON)
-    normed_one = tokens * scale_one
-    grad_normed = grad_hidden * gains[0:1]
-    grad_tokens = grad_mid + scale_one * (
-        grad_normed - normed_one * jnp.mean(grad_normed * normed_one, axis=-1, keepdims=True)
-    )
-
-    if joined:
-        first = 3 * half + LANES - buckets
-        table = kept[:mine_heads, first : first + buckets]
-        other = came[:mine_heads, first : first + buckets]
-        table_sum = place.ordered(table, other, 0, 0, jnp.concatenate).T
-    else:
+        grad_gain_one = jnp.sum(weighted, axis=1) / gain_attn.astype(F32)
         table = place.total(tab[:, :2].reshape(mine_heads, LANES))
         table = place.ordered(table, place.swap(table, 0), 0, 0, jnp.concatenate)
         table_sum = table[:, :buckets].T
 
     return (
         output[None],
-        grad_tokens.astype(BF16)[None],
+        grad_tokens[None],
         grad_gain_one,
         sum_q,
         sum_k,

time: 262 us -> 245 us (0.935)
  waiting for transfers between devices: 56.7 us -> 48.4 us
  Pallas kernels: 113 us -> 106 us
  starting transfers between devices: 62.3 us -> 67.4 us
  other arithmetic: 8.01 us -> 3.23 us
  local copies, waits for them, and re-layouts: 18.8 us -> 15.8 us
    pallas_call x17 -> x24, Pallas kernels: 113 us -> 106 us  [call(): pl.pallas_call(kernel, out_shape=shapes, grid=grid if grid is not None el...]
    ppermute x6 -> x9, waiting for transfers between devices: 23.4 us -> 16.8 us  [swap_mask(): return lax.ppermute(value, AXES, [(i, i ^ mask) for i in range(self.count)])]
    ppermute x6 -> x9, starting transfers between devices: 12.7 us -> 18.6 us  [swap_mask(): return lax.ppermute(value, AXES, [(i, i ^ mask) for i in range(self.count)])]
    ppermute x22 -> x21, starting transfers between devices: 19.8 us -> 18.1 us  [swap(): return lax.ppermute(value, AXES, pairs)]
    ppermute x22 -> x21, waiting for transfers between devices: 26.1 us -> 27.1 us  [swap(): return lax.ppermute(value, AXES, pairs)]
    unnamed x93 -> x108, local copies, waits for them, and re-layouts: 10 us -> 10.5 us
  transfers between devices with their start and end apart: 37 -> 39, of which waited for: 16 -> 19; matrix products, arithmetic and copies ran while one was open for 5% -> 2% of each run, Pallas kernels for 39% -> 39%
where the time goes in v2:
time: 245 us; the launch traced here: 242 us
  Pallas kernels  106 us (43%)
  starting transfers between devices  67.4 us (28%)
  waiting for transfers between devices  48.4 us (20%)
  local copies, waits for them, and re-layouts  15.8 us (6%)
  other arithmetic  3.23 us (1%)
    pallas_call x24, Pallas kernels, call(): pl.pallas_call(kernel, out_shape=shapes, grid=grid if grid is not None el...  106 us
    ppermute x21, waiting for transfers between devices, swap(): return lax.ppermute(value, AXES, pairs)  27.1 us
    ppermute x9, starting transfers between devices, swap_mask(): return lax.ppermute(value, AXES, [(i, i ^ mask) for i in range(self.count)])  18.6 us
    ppermute x21, starting transfers between devices, swap(): return lax.ppermute(value, AXES, pairs)  18.1 us
    ppermute x9, waiting for transfers between devices, swap_mask(): return lax.ppermute(value, AXES, [(i, i ^ mask) for i in range(self.count)])  16.8 us
    ppermute x6, starting transfers between devices, shift(): return lax.ppermute(value, AXES, pairs)  16.4 us
    all_to_all x3, starting transfers between devices, exchange(): lax.all_to_all(message, 'ctx', split_axis=0, concat_axis=0, tiled=True)  14.3 us
    unnamed x108, local copies, waits for them, and re-layouts  10.5 us
  transfers between devices with their start and end apart: 39, of which 19 were waited for; matrix products, arithmetic and copies ran while one was open for 2% of the time, Pallas kernels for 39%

profile of v2, /device:TPU:0, one launch (start us, length us, event | category | flops | bytes accessed | tf_op | source)
XLA Modules:
  0.0 242.3 jit_solution(15291764765892958975)
XLA Ops:
  7.1 4.6 %collective-permute-start.4 = (bf16[272,768]{1,0:T(8,128)(2,1)}, bf16[272,768]{1,0:T(8,128)(2,1)S(1)}, u32[]{:S(2)}, u32[]{:S(2)}) collective-permute-start(bf16[272,768]{1,0:T(8,128)(2,1)} %shard_map.230.refs_5_), channel_id=1, source_target_pairs={{0,2},{1,3},{2,4},{3,5},{4,6},{5,7},{6,8},{7,9},{8,10},{9,11},{10,... | collective-permute-start | bytes 1253384 | tf_op jit(solution)/shard_map/ppermute | solution.py:1188
  13.0 3.7 %collective-permute-start.1 = (bf16[48,1664]{1,0:T(8,128)(2,1)S(1)}, bf16[48,1664]{1,0:T(8,128)(2,1)S(1)}, u32[]{:S(2)}, u32[]{:S(2)}) collective-permute-start(bf16[48,1664]{1,0:T(8,128)(2,1)S(1)} %pad_maximum_fusion.5.refs_0_), channel_id=1, source_target_pairs={{0,4},{1,5},{2,6},{3,7},{4,0},{5,1},{6,2},{7,3},{8,12},{9,13},{10,... | collective-permute-start | bytes 479240 | tf_op jit(solution)/shard_map/ppermute | solution.py:1209
  16.6 2.6 %collective-permute-start.2 = (bf16[48,1664]{1,0:T(8,128)(2,1)S(1)}, bf16[48,1664]{1,0:T(8,128)(2,1)S(1)}, u32[]{:S(2)}, u32[]{:S(2)}) collective-permute-start(bf16[48,1664]{1,0:T(8,128)(2,1)S(1)} %pad_maximum_fusion.5.refs_0_), channel_id=1, source_target_pairs={{0,8},{1,9},{2,10},{3,11},{4,12},{5,13},{6,14},{7,15},{8,0},{9,1},... | collective-permute-start | bytes 479240 | tf_op jit(solution)/shard_map/ppermute | solution.py:1209
  21.4 3.3 %shard_map.229 = (bf16[6,256,512]{2,1,0:T(8,128)(2,1)}, bf16[6,128,256]{2,1,0:T(8,128)(2,1)}, bf16[6,128,256]{2,1,0:T(8,128)(2,1)}, f32[8,128]{1,0:T(8,128)}, s32[256,128]{1,0:T(8,128)}, /*index=5*/s32[8,256]{1,0:T(8,128)}) custom-call(s32[6]{0:T(128)} %stack.48.where_ref.core_ref.bits_ref, bf16[32,12]{1,0:T(8,128)(2,1)} %copy.38.table_ref, ...), custom_call_target="tpu_custom_call" | custom-call | flops 345000000 | tf_op jit(solution)/shard_map/pallas_call | solution.py:1266
  24.7 8.6 %collective-permute-done.1.refs_1_ = bf16[48,1664]{1,0:T(8,128)(2,1)S(1)} collective-permute-done((bf16[48,1664]{1,0:T(8,128)(2,1)S(1)}, bf16[48,1664]{1,0:T(8,128)(2,1)S(1)}, u32[]{:S(2)}, u32[]{:S(2)}) %collective-permute-start.1) | collective-permute-done | bytes 159776 | tf_op jit(solution)/shard_map/ppermute | solution.py:1209
  33.3 5.6 %collective-permute-done.3.refs_3_ = bf16[48,1664]{1,0:T(8,128)(2,1)S(1)} collective-permute-done((bf16[48,1664]{1,0:T(8,128)(2,1)S(1)}, bf16[48,1664]{1,0:T(8,128)(2,1)S(1)}, u32[]{:S(2)}, u32[]{:S(2)}) %collective-permute-start.3) | collective-permute-done | bytes 159776 | tf_op jit(solution)/shard_map/ppermute | solution.py:1209
  43.2 2.0 collective-permute-start.6
  46.8 3.4 %collective-permute-done.12 = bf16[2,2,48,384]{3,2,1,0:T(8,128)(2,1)S(1)} collective-permute-done((bf16[2,2,48,384]{3,2,1,0:T(8,128)(2,1)}, bf16[2,2,48,384]{3,2,1,0:T(8,128)(2,1)S(1)}, u32[]{:S(2)}, u32[]{:S(2)}) %collective-permute-start.12) | collective-permute-done | bytes 147488 | tf_op jit(solution)/shard_map/ppermute | solution.py:1177
  57.0 2.1 shard_map.232.refs_7_
  59.1 4.4 %all-to-all-start.1 = ((bf16[16,112,128]{2,1,0:T(8,128)(2,1)}), bf16[16,112,128]{2,1,0:T(8,128)(2,1)}, u32[]{:S(2)}, u32[]{:S(2)}) async-start(bf16[16,112,128]{2,1,0:T(8,128)(2,1)} %bitcast.65), calls=%async_computation.1 | async-start | bytes 917504 | tf_op jit(solution)/shard_map/all_to_all | solution.py:1436
  65.1 3.0 %collective-permute-done.7 = bf16[2,2,2,48,640]{4,3,2,1,0:T(8,128)(2,1)S(1)} collective-permute-done((bf16[2,2,2,48,640]{4,3,2,1,0:T(8,128)(2,1)S(1)}, bf16[2,2,2,48,640]{4,3,2,1,0:T(8,128)(2,1)S(1)}, u32[]{:S(2)}, u32[]{:S(2)}) %collective-permute-start.7) | collective-permute-done | bytes 491552 | tf_op jit(solution)/shard_map/ppermute | solution.py:1177
  68.9 18.2 %shard_map.233 = (bf16[512,768]{1,0:T(8,128)(2,1)}, bf16[512,384]{1,0:T(8,128)(2,1)}, bf16[1536,384]{1,0:T(8,128)(2,1)}, bf16[1536,384]{1,0:T(8,128)(2,1)}, f32[...) custom-call(f32[8,128]{1,0:T(8,128)} %get-tuple-element.89.far_ref.l, ...), custom_call_target="tpu_custom_call" | custom-call | flops 1150000000 | tf_op jit(solution)/shard_map/pallas_call | solution.py:1266
  89.9 4.2 %shard_map.234 = (f32[256,768]{1,0:T(8,128)}, bf16[256,768]{1,0:T(8,128)(2,1)}, f32[256,128]{1,0:T(8,128)}, bf16[1792,128]{1,0:T(8,128)(2,1)}) custom-call(s32[6]{0:T(128)} %stack.48.where_ref.core_ref.bits_ref, bf16[256,768]{1,0:T(8,128)(2,1)} %bitcast.59, bf16[512,384]{1,0:T(8,128)(2,1)} %get-tuple-element.95.own_ref.ctx_ref, bf16[512,384]{1,0:T(8,128)(2,1)} %copy-done.35, ...), custom_call_target="tpu_custom_call" | custom-call | flops 4600000000 | tf_op jit(solution)/shard_map/pallas_call | solution.py:1266
  94.1 4.4 %all-to-all-start = ((bf16[16,112,128]{2,1,0:T(8,128)(2,1)}), bf16[16,112,128]{2,1,0:T(8,128)(2,1)S(1)}, u32[]{:S(2)}, u32[]{:S(2)}) async-start(bf16[16,112,128]{2,1,0:T(8,128)(2,1)} %bitcast.69), calls=%async_computation | async-start | bytes 917504 | tf_op jit(solution)/shard_map/all_to_all | solution.py:1436
  98.4 3.8 %collective-permute-start.15 = (f32[3,8,512]{2,1,0:T(8,128)S(1)}, f32[3,8,512]{2,1,0:T(8,128)S(1)}, u32[]{:S(2)}, u32[]{:S(2)}) collective-permute-start(f32[3,8,512]{2,1,0:T(8,128)S(1)} %copy-done.38), channel_id=1, source_target_pairs={{0,2},{1,3},{2,4},{3,5},{4,6},{5,7},{6,8},{7,9},{8,10},{9,11},{10,... | collective-permute-start | bytes 147464 | tf_op jit(solution)/shard_map/ppermute | solution.py:1188
  107.2 4.2 %shard_map.236.earlier_a_ref.qp_ref.qn_ref = bf16[1024,384]{1,0:T(8,128)(2,1)} custom-call(s32[6]{0:T(128)} %stack.48.where_ref.core_ref.bits_ref, bf16[816,768]{1,0:T(8,128)(2,1)} %copy-done.2, bf16[816,768]{1,0:T(8,128)(2,1)} %collective-permute-done.10.refs_5_.came_ref, f32[8,768]{1,0:T(8,128)} %get-tuple-element.98.gain_ref, bf16[384,640]{1,0:T(8,128)(2,1)} %bitcast.47, ...), custom_call_target="tpu_custom_call" | custom-call | flops 345000000 | tf_op jit(solution)/shard_map/pallas_call | solution.py:1266
  114.5 12.4 %shard_map.237 = (bf16[288,768]{1,0:T(8,128)(2,1)}, bf16[288,768]{1,0:T(8,128)(2,1)}, bf16[288,3072]{1,0:T(8,128)(2,1)}, bf16[288,3072]{1,0:T(8,128)(2,1)}, bf16[3584,128]{1,0:T(8,128)(2,1)}) custom-call(bf16[1792,128]{1,0:T(8,128)(2,1)} %bitcast.68, bf16[288,768]{1,0:T(8,128)(2,1)} %shard_map.235.cot_ref, bf16[1,768,3072]{2,1,0:T(8,128)(2,1)} %win_ref.3, ...), custom_call_target="tpu_custom_call" | custom-call | flops 13799999488 | tf_op jit(solution)/shard_map/pallas_call | solution.py:1266
  126.8 5.6 %all-to-all-start.2 = ((bf16[16,224,128]{2,1,0:T(8,128)(2,1)}), bf16[16,224,128]{2,1,0:T(8,128)(2,1)S(1)}, u32[]{:S(2)}, u32[]{:S(2)}) async-start(bf16[16,224,128]{2,1,0:T(8,128)(2,1)} %bitcast.66), calls=%async_computation.2 | async-start | bytes 1835008 | tf_op jit(solution)/shard_map/all_to_all | solution.py:1436
  133.4 16.4 %shard_map.239 = (f32[1,768,3072]{2,1,0:T(8,128)}, f32[1,3072,768]{2,1,0:T(8,128)}) custom-call(bf16[288,768]{1,0:T(8,128)(2,1)} %get-tuple-element.110.rows_ref, bf16[288,768]{1,0:T(8,128)(2,1)} %get-tuple-element.111.grad_ref, bf16[288,3072]{1,0:T(8,128)(2,1)} %get-tuple-element.112.act_ref, bf16[288,3072]{1,0:T(8,128)(2,1)} %get-tuple-element.113.gbef_ref, ...), custom_call_target="tpu_custom_call" | custom-call | flops 18400000000 | tf_op jit(solution)/shard_map/pallas_call | solution.py:1266
  149.8 3.5 %all-to-all-done.2 = bf16[16,224,128]{2,1,0:T(8,128)(2,1)S(1)} async-done(((bf16[16,224,128]{2,1,0:T(8,128)(2,1)}), bf16[16,224,128]{2,1,0:T(8,128)(2,1)S(1)}, u32[]{:S(2)}, u32[]{:S(2)}) %all-to-all-start.2) | async-done | bytes 917536 | tf_op jit(solution)/shard_map/all_to_all | solution.py:1436
  154.2 6.6 %shard_map.240 = (f32[256,768]{1,0:T(8,128)}, bf16[256,384]{1,0:T(8,128)(2,1)}, bf16[256,384]{1,0:T(8,128)(2,1)}, bf16[272,384]{1,0:T(8,128)(2,1)}, bf16[272,384]{1,0:T(8,128)(2,1)}, /*index=5*/f32[768,128]{1,0:T(8,128)}) custom-call(s32[6]{0:T(128)} %stack.48.where_ref.core_ref.bits_ref, bf16[3584,128]{1,0:T(8,128)(2,1)} %bitcast.54, ...), custom_call_target="tpu_custom_call" | custom-call | flops 5750000128 | tf_op jit(solution)/shard_map/pallas_call | solution.py:1266
  163.7 3.7 %collective-permute-start.20 = (bf16[544,384]{1,0:T(8,128)(2,1)S(1)}, bf16[544,384]{1,0:T(8,128)(2,1)S(1)}, u32[]{:S(2)}, u32[]{:S(2)}) collective-permute-start(bf16[544,384]{1,0:T(8,128)(2,1)S(1)} %pad_maximum_fusion.3.msg_ref), channel_id=1, source_target_pairs={{0,2},{1,3},{2,4},{3,5},{4,6},{5,7},{6,8},{7,9},{8,10},{9,11},{10,... | collective-permute-start | bytes 1253384 | tf_op jit(solution)/shard_map/ppermute | solution.py:1188
  169.1 13.1 %shard_map.241 = (bf16[512,384]{1,0:T(8,128)(2,1)S(1)}, f32[512,384]{1,0:T(8,128)S(1)}, f32[512,384]{1,0:T(8,128)S(1)}, f32[3,8,128]{2,1,0:T(8,128)S(1)}) custom-call(f32[8,128]{1,0:T(8,128)S(1)} %copy-done.30, bf16[512,384]{1,0:T(8,128)(2,1)S(1)} %copy-done.34, bf16[1536,384]{1,0:T(8,128)(2,1)S(1)} %copy-done.31, bf16[1536,384]{1,0:T(8,128)(2,1)S(1)} %copy-done.32, ...), custom_call_target="tpu_custom_call" | custom-call | flops 16099999744 | tf_op jit(solution)/shard_map/pallas_call | solution.py:1266
  185.8 7.9 %shard_map.243 = (bf16[512,384]{1,0:T(8,128)(2,1)S(1)}, bf16[512,384]{1,0:T(8,128)(2,1)S(1)}) custom-call(f32[8,128]{1,0:T(8,128)S(1)} %copy-done.30, bf16[1024,384]{1,0:T(8,128)(2,1)S(1)} %copy-done.12, bf16[1024,384]{1,0:T(8,128)(2,1)S(1)} %copy-done.12, bf16[1536,384]{1,0:T(8,128)(2,1)S(1)} %copy-done.31, bf16[1536,384]{1,0:T(8,128)(2,1)S(1)} %copy-done.32, ...), custom_call_target="tpu_custom_call" | custom-call | flops 8049999872 | tf_op jit(solution)/shard_map/pallas_call | solution.py:1266
  193.7 2.2 shard_map.246
  196.0 2.7 %collective-permute-start.25 = (bf16[384,640]{1,0:T(8,128)(2,1)S(1)}, bf16[384,640]{1,0:T(8,128)(2,1)S(1)}, u32[]{:S(2)}, u32[]{:S(2)}) collective-permute-start(bf16[384,640]{1,0:T(8,128)(2,1)S(1)} %get-tuple-element.139), channel_id=1, source_target_pairs={{0,2},{1,3},{2,0},{3,1},{4,6},{5,7},{6,4},{7,5},{8,10},{9,11},{10,... | collective-permute-start | bytes 1474568 | tf_op jit(solution)/shard_map/ppermute | solution.py:1177
  201.3 2.1 shard_map.244
  203.5 6.3 %collective-permute-done.25.later_ref.refs_1_ = bf16[384,640]{1,0:T(8,128)(2,1)S(1)} collective-permute-done((bf16[384,640]{1,0:T(8,128)(2,1)S(1)}, bf16[384,640]{1,0:T(8,128)(2,1)S(1)}, u32[]{:S(2)}, u32[]{:S(2)}) %collective-permute-start.25) | collective-permute-done | bytes 491552 | tf_op jit(solution)/shard_map/ppermute | solution.py:1177
  213.3 4.0 %collective-permute-start.31 = (bf16[96,640]{1,0:T(8,128)(2,1)S(1)}, bf16[96,640]{1,0:T(8,128)(2,1)S(1)}, u32[]{:S(2)}, u32[]{:S(2)}) collective-permute-start(bf16[96,640]{1,0:T(8,128)(2,1)S(1)} %get-tuple-element.151), channel_id=1, source_target_pairs={{0,4},{1,5},{2,6},{3,7},{4,0},{5,1},{6,2},{7,3},{8,12},{9,13},{10,... | collective-permute-start | bytes 368648 | tf_op jit(solution)/shard_map/ppermute | solution.py:1209
  219.8 2.0 collective-permute-done.27.refs_1_
  222.5 3.2 %collective-permute-start.28 = (bf16[48,1024]{1,0:T(8,128)(2,1)S(1)}, bf16[48,1024]{1,0:T(8,128)(2,1)S(1)}, u32[]{:S(2)}, u32[]{:S(2)}) collective-permute-start(bf16[48,1024]{1,0:T(8,128)(2,1)S(1)} %get-tuple-element.146), channel_id=1, source_target_pairs={{0,4},{1,5},{2,6},{3,7},{4,0},{5,1},{6,2},{7,3},{8,12},{9,13},{10,... | collective-permute-start | bytes 294920 | tf_op jit(solution)/shard_map/ppermute | solution.py:1209
  232.4 2.7 %collective-permute-done.34.refs_5_ = bf16[48,640]{1,0:T(8,128)(2,1)S(1)} collective-permute-done((bf16[48,640]{1,0:T(8,128)(2,1)S(1)}, bf16[48,640]{1,0:T(8,128)(2,1)S(1)}, u32[]{:S(2)}, u32[]{:S(2)}) %collective-permute-start.34) | collective-permute-done | bytes 61472 | tf_op jit(solution)/shard_map/ppermute | solution.py:1177
  (201 shorter events, 68.5 us)
Async XLA Ops:
  4.8 8.2 %collective-permute-start = (bf16[24,1664]{1,0:T(8,128)(2,1)S(1)}, bf16[24,1664]{1,0:T(8,128)(2,1)S(1)}, u32[]{:S(2)}, u32[]{:S(2)}) collective-permute-start(bf16[24,1664]{1,0:T(8,128)(2,1)S(1)} %broadcast_select_fusion.5), channel_id=1, source_target_pairs={{0,1},{1,0},{2,3},{3,2},{4,5},{5,4},{6,7},{7,6},{8,9},{9,8},{10,11... | collective-permute-start | bytes 239624 | tf_op jit(solution)/shard_map/ppermute | solution.py:1177
  7.1 32.5 %collective-permute-start.4 = (bf16[272,768]{1,0:T(8,128)(2,1)}, bf16[272,768]{1,0:T(8,128)(2,1)S(1)}, u32[]{:S(2)}, u32[]{:S(2)}) collective-permute-start(bf16[272,768]{1,0:T(8,128)(2,1)} %shard_map.230.refs_5_), channel_id=1, source_target_pairs={{0,2},{1,3},{2,4},{3,5},{4,6},{5,7},{6,8},{7,9},{8,10},{9,11},{10,... | collective-permute-start | bytes 1253384 | tf_op jit(solution)/shard_map/ppermute | solution.py:1188
  11.6 27.9 %collective-permute-start.5 = (bf16[272,768]{1,0:T(8,128)(2,1)}, bf16[272,768]{1,0:T(8,128)(2,1)S(1)}, u32[]{:S(2)}, u32[]{:S(2)}) collective-permute-start(bf16[272,768]{1,0:T(8,128)(2,1)} %shard_map.230.refs_5_), channel_id=1, source_target_pairs={{2,0},{3,1},{4,2},{5,3},{6,4},{7,5},{8,6},{9,7},{10,8},{11,9},{12,... | collective-permute-start | bytes 1253384 | tf_op jit(solution)/shard_map/ppermute | solution.py:1188
  13.0 20.4 %collective-permute-start.1 = (bf16[48,1664]{1,0:T(8,128)(2,1)S(1)}, bf16[48,1664]{1,0:T(8,128)(2,1)S(1)}, u32[]{:S(2)}, u32[]{:S(2)}) collective-permute-start(bf16[48,1664]{1,0:T(8,128)(2,1)S(1)} %pad_maximum_fusion.5.refs_0_), channel_id=1, source_target_pairs={{0,4},{1,5},{2,6},{3,7},{4,0},{5,1},{6,2},{7,3},{8,12},{9,13},{10,... | collective-permute-start | bytes 479240 | tf_op jit(solution)/shard_map/ppermute | solution.py:1209
  16.6 16.7 %collective-permute-start.2 = (bf16[48,1664]{1,0:T(8,128)(2,1)S(1)}, bf16[48,1664]{1,0:T(8,128)(2,1)S(1)}, u32[]{:S(2)}, u32[]{:S(2)}) collective-permute-start(bf16[48,1664]{1,0:T(8,128)(2,1)S(1)} %pad_maximum_fusion.5.refs_0_), channel_id=1, source_target_pairs={{0,8},{1,9},{2,10},{3,11},{4,12},{5,13},{6,14},{7,15},{8,0},{9,1},... | collective-permute-start | bytes 479240 | tf_op jit(solution)/shard_map/ppermute | solution.py:1209
  19.2 19.7 %collective-permute-start.3 = (bf16[48,1664]{1,0:T(8,128)(2,1)S(1)}, bf16[48,1664]{1,0:T(8,128)(2,1)S(1)}, u32[]{:S(2)}, u32[]{:S(2)}) collective-permute-start(bf16[48,1664]{1,0:T(8,128)(2,1)S(1)} %pad_maximum_fusion.5.refs_0_), channel_id=1, source_target_pairs={{0,12},{1,13},{2,14},{3,15},{4,8},{5,9},{6,10},{7,11},{8,4},{9,5},... | collective-permute-start | bytes 479240 | tf_op jit(solution)/shard_map/ppermute | solution.py:1209
  43.2 10.6 %collective-permute-start.6 = (bf16[2,2,48,640]{3,2,1,0:T(8,128)(2,1)S(1)}, bf16[2,2,48,640]{3,2,1,0:T(8,128)(2,1)S(1)}, u32[]{:S(2)}, u32[]{:S(2)}) collective-permute-start(bf16[2,2,48,640]{3,2,1,0:T(8,128)(2,1)S(1)} %bitcast.61), channel_id=1, source_target_pairs={{0,2},{1,3},{2,0},{3,1},{4,6},{5,7},{6,4},{7,5},{8,10},{9,11},{10,... | collective-permute-start | bytes 737288 | tf_op jit(solution)/shard_map/ppermute | solution.py:1177
  46.8 21.4 %collective-permute-start.10 = (bf16[816,768]{1,0:T(8,128)(2,1)S(1)}, bf16[816,768]{1,0:T(8,128)(2,1)}, u32[]{:S(2)}, u32[]{:S(2)}) collective-permute-start(bf16[816,768]{1,0:T(8,128)(2,1)S(1)} %get-tuple-element.93.refs_4_.x_ref), channel_id=1, source_target_pairs={{0,1},{1,0},{2,3},{3,2},{4,5},{5,4},{6,7},{7,6},{8,9},{9,8},{10,11... | collective-permute-start | bytes 3760136 | tf_op jit(solution)/shard_map/ppermute | solution.py:1177
  52.0 13.1 %collective-permute-start.9 = (bf16[2,2,2,48,640]{4,3,2,1,0:T(8,128)(2,1)S(1)}, bf16[2,2,2,48,640]{4,3,2,1,0:T(8,128)(2,1)S(1)}, u32[]{:S(2)}, u32[]{:S(2)}) collective-permute-start(bf16[2,2,2,48,640]{4,3,2,1,0:T(8,128)(2,1)S(1)} %pad_maximum_fusion.2), channel_id=1, source_target_pairs={{0,2},{1,3},{2,0},{3,1},{4,6},{5,7},{6,4},{7,5},{8,10},{9,11},{10,... | collective-permute-start | bytes 1474568 | tf_op jit(solution)/shard_map/ppermute | solution.py:1177
  53.9 14.2 %collective-permute-start.7 = (bf16[2,2,2,48,640]{4,3,2,1,0:T(8,128)(2,1)S(1)}, bf16[2,2,2,48,640]{4,3,2,1,0:T(8,128)(2,1)S(1)}, u32[]{:S(2)}, u32[]{:S(2)}) collective-permute-start(bf16[2,2,2,48,640]{4,3,2,1,0:T(8,128)(2,1)S(1)} %pad_maximum_fusion.1.later_ref), channel_id=1, source_target_pairs={{0,16},{1,17},{2,18},{3,19},{4,20},{5,21},{6,22},{7,23},{8,24},{9,... | collective-permute-start | bytes 1474568 | tf_op jit(solution)/shard_map/ppermute | solution.py:1177
  56.5 30.7 %collective-permute-start.14 = (bf16[384,768]{1,0:T(8,128)(2,1)}, bf16[384,768]{1,0:T(8,128)(2,1)}, u32[]{:S(2)}, u32[]{:S(2)}) collective-permute-start(bf16[384,768]{1,0:T(8,128)(2,1)} %bitcast.25.wonear_ref), channel_id=1, source_target_pairs={{0,16},{1,17},{2,18},{3,19},{4,20},{5,21},{6,22},{7,23},{8,24},{9,... | collective-permute-start | bytes 1769480 | tf_op jit(solution)/shard_map/ppermute | solution.py:1177
  59.1 35.0 %all-to-all-start.1 = ((bf16[16,112,128]{2,1,0:T(8,128)(2,1)}), bf16[16,112,128]{2,1,0:T(8,128)(2,1)}, u32[]{:S(2)}, u32[]{:S(2)}) async-start(bf16[16,112,128]{2,1,0:T(8,128)(2,1)} %bitcast.65), calls=%async_computation.1 | async-start | bytes 917504 | tf_op jit(solution)/shard_map/all_to_all | solution.py:1436
  94.1 17.6 %all-to-all-start = ((bf16[16,112,128]{2,1,0:T(8,128)(2,1)}), bf16[16,112,128]{2,1,0:T(8,128)(2,1)S(1)}, u32[]{:S(2)}, u32[]{:S(2)}) async-start(bf16[16,112,128]{2,1,0:T(8,128)(2,1)} %bitcast.69), calls=%async_computation | async-start | bytes 917504 | tf_op jit(solution)/shard_map/all_to_all | solution.py:1436
  98.4 14.8 %collective-permute-start.15 = (f32[3,8,512]{2,1,0:T(8,128)S(1)}, f32[3,8,512]{2,1,0:T(8,128)S(1)}, u32[]{:S(2)}, u32[]{:S(2)}) collective-permute-start(f32[3,8,512]{2,1,0:T(8,128)S(1)} %copy-done.38), channel_id=1, source_target_pairs={{0,2},{1,3},{2,4},{3,5},{4,6},{5,7},{6,8},{7,9},{8,10},{9,11},{10,... | collective-permute-start | bytes 147464 | tf_op jit(solution)/shard_map/ppermute | solution.py:1188
  102.3 10.9 %collective-permute-start.16 = (f32[3,8,512]{2,1,0:T(8,128)S(1)}, f32[3,8,512]{2,1,0:T(8,128)S(1)}, u32[]{:S(2)}, u32[]{:S(2)}) collective-permute-start(f32[3,8,512]{2,1,0:T(8,128)S(1)} %copy-done.38), channel_id=1, source_target_pairs={{2,0},{3,1},{4,2},{5,3},{6,4},{7,5},{8,6},{9,7},{10,8},{11,9},{12,... | collective-permute-start | bytes 147464 | tf_op jit(solution)/shard_map/ppermute | solution.py:1188
  105.7 26.7 %collective-permute-start.18 = (bf16[288,768]{1,0:T(8,128)(2,1)}, bf16[288,768]{1,0:T(8,128)(2,1)S(1)}, u32[]{:S(2)}, u32[]{:S(2)}) collective-permute-start(bf16[288,768]{1,0:T(8,128)(2,1)} %shard_map.235.cot_ref), channel_id=1, source_target_pairs={{0,16},{1,17},{2,18},{3,19},{4,20},{5,21},{6,22},{7,23},{8,24},{9,... | collective-permute-start | bytes 1327112 | tf_op jit(solution)/shard_map/ppermute | solution.py:1177
  111.7 20.8 %collective-permute-start.17 = (bf16[1792,128]{1,0:T(8,128)(2,1)S(1)}, bf16[1792,128]{1,0:T(8,128)(2,1)S(1)}, u32[]{:S(2)}, u32[]{:S(2)}) collective-permute-start(bf16[1792,128]{1,0:T(8,128)(2,1)S(1)} %bitcast.67), channel_id=1, source_target_pairs={{0,16},{1,17},{2,18},{3,19},{4,20},{5,21},{6,22},{7,23},{8,24},{9,... | collective-permute-start | bytes 1376264 | tf_op jit(solution)/shard_map/ppermute | solution.py:1177
  126.8 26.4 %all-to-all-start.2 = ((bf16[16,224,128]{2,1,0:T(8,128)(2,1)}), bf16[16,224,128]{2,1,0:T(8,128)(2,1)S(1)}, u32[]{:S(2)}, u32[]{:S(2)}) async-start(bf16[16,224,128]{2,1,0:T(8,128)(2,1)} %bitcast.66), calls=%async_computation.2 | async-start | bytes 1835008 | tf_op jit(solution)/shard_map/all_to_all | solution.py:1436
  161.3 20.8 %collective-permute-start.22 = (bf16[256,384]{1,0:T(8,128)(2,1)}, bf16[256,384]{1,0:T(8,128)(2,1)S(1)}, u32[]{:S(2)}, u32[]{:S(2)}) collective-permute-start(bf16[256,384]{1,0:T(8,128)(2,1)} %get-tuple-element.124), channel_id=1, source_target_pairs={{0,1},{1,0},{2,3},{3,2},{4,5},{5,4},{6,7},{7,6},{8,9},{9,8},{10,11... | collective-permute-start | bytes 589832 | tf_op jit(solution)/shard_map/ppermute | solution.py:1177
  163.7 22.1 %collective-permute-start.20 = (bf16[544,384]{1,0:T(8,128)(2,1)S(1)}, bf16[544,384]{1,0:T(8,128)(2,1)S(1)}, u32[]{:S(2)}, u32[]{:S(2)}) collective-permute-start(bf16[544,384]{1,0:T(8,128)(2,1)S(1)} %pad_maximum_fusion.3.msg_ref), channel_id=1, source_target_pairs={{0,2},{1,3},{2,4},{3,5},{4,6},{5,7},{6,8},{7,9},{8,10},{9,11},{10,... | collective-permute-start | bytes 1253384 | tf_op jit(solution)/shard_map/ppermute | solution.py:1188
  167.4 18.3 %collective-permute-start.21 = (bf16[544,384]{1,0:T(8,128)(2,1)S(1)}, bf16[544,384]{1,0:T(8,128)(2,1)S(1)}, u32[]{:S(2)}, u32[]{:S(2)}) collective-permute-start(bf16[544,384]{1,0:T(8,128)(2,1)S(1)} %pad_maximum_fusion.3.msg_ref), channel_id=1, source_target_pairs={{2,0},{3,1},{4,2},{5,3},{6,4},{7,5},{8,6},{9,7},{10,8},{11,9},{12,... | collective-permute-start | bytes 1253384 | tf_op jit(solution)/shard_map/ppermute | solution.py:1188
  183.5 10.3 %collective-permute-start.24 = (bf16[384,384]{1,0:T(8,128)(2,1)S(1)}, bf16[384,384]{1,0:T(8,128)(2,1)S(1)}, u32[]{:S(2)}, u32[]{:S(2)}) collective-permute-start(bf16[384,384]{1,0:T(8,128)(2,1)S(1)} %get-tuple-element.138), channel_id=1, source_target_pairs={{0,16},{1,17},{2,18},{3,19},{4,20},{5,21},{6,22},{7,23},{8,24},{9,... | collective-permute-start | bytes 884744 | tf_op jit(solution)/shard_map/ppermute | solution.py:1177
  196.0 13.9 %collective-permute-start.25 = (bf16[384,640]{1,0:T(8,128)(2,1)S(1)}, bf16[384,640]{1,0:T(8,128)(2,1)S(1)}, u32[]{:S(2)}, u32[]{:S(2)}) collective-permute-start(bf16[384,640]{1,0:T(8,128)(2,1)S(1)} %get-tuple-element.139), channel_id=1, source_target_pairs={{0,2},{1,3},{2,0},{3,1},{4,6},{5,7},{6,4},{7,5},{8,10},{9,11},{10,... | collective-permute-start | bytes 1474568 | tf_op jit(solution)/shard_map/ppermute | solution.py:1177
  198.6 12.6 %collective-permute-start.26 = (bf16[384,640]{1,0:T(8,128)(2,1)S(1)}, bf16[384,640]{1,0:T(8,128)(2,1)S(1)}, u32[]{:S(2)}, u32[]{:S(2)}) collective-permute-start(bf16[384,640]{1,0:T(8,128)(2,1)S(1)} %get-tuple-element.141), channel_id=1, source_target_pairs={{0,16},{1,17},{2,18},{3,19},{4,20},{5,21},{6,22},{7,23},{8,24},{9,... | collective-permute-start | bytes 1474568 | tf_op jit(solution)/shard_map/ppermute | solution.py:1177
  203.4 23.5 %collective-permute-start.23 = (f32[256,768]{1,0:T(8,128)S(1)}, f32[256,768]{1,0:T(8,128)S(1)}, u32[]{:S(2)}, u32[]{:S(2)}) collective-permute-start(f32[256,768]{1,0:T(8,128)S(1)} %get-tuple-element.131), channel_id=1, source_target_pairs={{0,1},{1,0},{2,3},{3,2},{4,5},{5,4},{6,7},{7,6},{8,9},{9,8},{10,11... | collective-permute-start | bytes 2359304 | tf_op jit(solution)/shard_map/ppermute | solution.py:1177
  212.1 9.7 %collective-permute-start.27 = (bf16[192,1024]{1,0:T(8,128)(2,1)S(1)}, bf16[192,1024]{1,0:T(8,128)(2,1)S(1)}, u32[]{:S(2)}, u32[]{:S(2)}) collective-permute-start(bf16[192,1024]{1,0:T(8,128)(2,1)S(1)} %get-tuple-element.144), channel_id=1, source_target_pairs={{0,2},{1,3},{2,0},{3,1},{4,6},{5,7},{6,4},{7,5},{8,10},{9,11},{10,... | collective-permute-start | bytes 1179656 | tf_op jit(solution)/shard_map/ppermute | solution.py:1177
  213.3 12.4 %collective-permute-start.31 = (bf16[96,640]{1,0:T(8,128)(2,1)S(1)}, bf16[96,640]{1,0:T(8,128)(2,1)S(1)}, u32[]{:S(2)}, u32[]{:S(2)}) collective-permute-start(bf16[96,640]{1,0:T(8,128)(2,1)S(1)} %get-tuple-element.151), channel_id=1, source_target_pairs={{0,4},{1,5},{2,6},{3,7},{4,0},{5,1},{6,2},{7,3},{8,12},{9,13},{10,... | collective-permute-start | bytes 368648 | tf_op jit(solution)/shard_map/ppermute | solution.py:1209
  217.2 13.0 %collective-permute-start.32 = (bf16[96,640]{1,0:T(8,128)(2,1)S(1)}, bf16[96,640]{1,0:T(8,128)(2,1)S(1)}, u32[]{:S(2)}, u32[]{:S(2)}) collective-permute-start(bf16[96,640]{1,0:T(8,128)(2,1)S(1)} %get-tuple-element.152), channel_id=1, source_target_pairs={{0,8},{1,9},{2,10},{3,11},{4,12},{5,13},{6,14},{7,15},{8,0},{9,1},... | collective-permute-start | bytes 368648 | tf_op jit(solution)/shard_map/ppermute | solution.py:1209
  218.4 11.8 %collective-permute-start.33 = (bf16[96,640]{1,0:T(8,128)(2,1)S(1)}, bf16[96,640]{1,0:T(8,128)(2,1)S(1)}, u32[]{:S(2)}, u32[]{:S(2)}) collective-permute-start(bf16[96,640]{1,0:T(8,128)(2,1)S(1)} %get-tuple-element.153), channel_id=1, source_target_pairs={{0,12},{1,13},{2,14},{3,15},{4,8},{5,9},{6,10},{7,11},{8,4},{9,5},... | collective-permute-start | bytes 368648 | tf_op jit(solution)/shard_map/ppermute | solution.py:1209
  222.5 12.6 %collective-permute-start.28 = (bf16[48,1024]{1,0:T(8,128)(2,1)S(1)}, bf16[48,1024]{1,0:T(8,128)(2,1)S(1)}, u32[]{:S(2)}, u32[]{:S(2)}) collective-permute-start(bf16[48,1024]{1,0:T(8,128)(2,1)S(1)} %get-tuple-element.146), channel_id=1, source_target_pairs={{0,4},{1,5},{2,6},{3,7},{4,0},{5,1},{6,2},{7,3},{8,12},{9,13},{10,... | collective-permute-start | bytes 294920 | tf_op jit(solution)/shard_map/ppermute | solution.py:1209
  225.7 11.4 %collective-permute-start.29 = (bf16[48,1024]{1,0:T(8,128)(2,1)S(1)}, bf16[48,1024]{1,0:T(8,128)(2,1)S(1)}, u32[]{:S(2)}, u32[]{:S(2)}) collective-permute-start(bf16[48,1024]{1,0:T(8,128)(2,1)S(1)} %get-tuple-element.147), channel_id=1, source_target_pairs={{0,8},{1,9},{2,10},{3,11},{4,12},{5,13},{6,14},{7,15},{8,0},{9,1},... | collective-permute-start | bytes 294920 | tf_op jit(solution)/shard_map/ppermute | solution.py:1209
  226.9 10.1 %collective-permute-start.30 = (bf16[48,1024]{1,0:T(8,128)(2,1)S(1)}, bf16[48,1024]{1,0:T(8,128)(2,1)S(1)}, u32[]{:S(2)}, u32[]{:S(2)}) collective-permute-start(bf16[48,1024]{1,0:T(8,128)(2,1)S(1)} %get-tuple-element.148), channel_id=1, source_target_pairs={{0,12},{1,13},{2,14},{3,15},{4,8},{5,9},{6,10},{7,11},{8,4},{9,5},... | collective-permute-start | bytes 294920 | tf_op jit(solution)/shard_map/ppermute | solution.py:1209
  (59 other events, 488.3 us)

commit v3 on v2

--- a/solution.py
+++ b/solution.py
@@ -187,12 +187,41 @@
     return nt(pick, columns)
 
 
-def extend_kernel(x_ref, seg_ref, out_ref):
+def start_kernel(
+    experts,
+    where_ref,
+    wq_ref,
+    wk_ref,
+    wv_ref,
+    wo_ref,
+    router_ref,
+    gains_ref,
+    x_ref,
+    seg_ref,
+    ours_ref,
+    theirs_ref,
+    ext_ref,
+):
+    core = where_ref[0]
+    half = wq_ref.shape[1] // 2
+    rows = wq_ref.shape[0]
+    pick = iota((experts, LANES), 0) == iota((experts, LANES), 1)
+    small = tn(router_ref[...], pick.astype(BF16))
+    gains = jnp.concatenate([gains_ref[...].astype(F32), jnp.zeros((6, rows), F32)], axis=0)
+    pick = iota((8, LANES), 0) + experts == iota((8, LANES), 1)
+    small = (small + tn(gains.astype(BF16), pick.astype(BF16))).astype(BF16)
+    for out_ref, which in ((ours_ref, core), (theirs_ref, 1 - core)):
+        cols = pl.ds(pl.multiple_of(which * half, half), half)
+        out_ref[:, :half] = wq_ref[:, cols]
+        out_ref[:, half : 2 * half] = wk_ref[:, cols]
+        out_ref[:, 2 * half : 3 * half] = wv_ref[:, cols]
+        out_ref[:, 3 * half : 3 * half + LANES] = small
+        out_ref[:, 3 * half + LANES :] = wo_ref[:, cols]
     tok, width = x_ref.shape
-    out_ref[:tok, :] = x_ref[...]
+    ext_ref[:tok, :] = x_ref[...]
     code = (seg_ref[...] + 1).astype(F32)
     code = jnp.concatenate([code, jnp.zeros((1, width - tok), F32)], axis=1)
-    out_ref[tok:, :] = jnp.broadcast_to(code, (CODE_ROWS, width)).astype(BF16)
+    ext_ref[tok:, :] = jnp.broadcast_to(code, (CODE_ROWS, width)).astype(BF16)
 
 
 def arrange_kernel(where_ref, *refs):
@@ -1045,7 +1074,8 @@
     kept = kept_ref[:, last:]
     came = came_ref[:, last:]
     both = kept + came
-    router_ref[...] = both[:, :experts]
+    pick = iota((experts, LANES), 0) == iota((experts, LANES), 1)
+    router_ref[...] = exact_nt(pick.astype(F32), both)
     weighted = (
         q_ref[...] * wq_ref[...].astype(F32)
         + k_ref[...] * wk_ref[...].astype(F32)
@@ -1055,13 +1085,12 @@
     lane = iota(both.shape, 1)
     cols = jnp.where(lane == 0, gain_one, jnp.where(lane == 1, both[:, experts : experts + 1], 0.0))
     gains_ref[...] = exact_nt((iota((8, LANES), 0) == iota((8, LANES), 1)).astype(F32), cols)
-    heads = table_ref.shape[1] // 2
+    heads = table_ref.shape[0] // 2
     own = kept[:heads, LANES - buckets :]
     other = came[:heads, LANES - buckets :]
     first = jnp.where(core == 0, own, other)
     second = jnp.where(core == 0, other, own)
-    eye = (iota((buckets, buckets), 0) == iota((buckets, buckets), 1)).astype(F32)
-    table_ref[...] = exact_nt(eye, jnp.concatenate([first, second], axis=0))
+    table_ref[...] = jnp.concatenate([first, second], axis=0)
 
 
 def after_kernel(
@@ -1326,31 +1355,26 @@
         ]
     ).astype(jnp.int32)
 
-    small_w = jnp.concatenate(
-        [
-            w_router,
-            gain_attn[:, None],
-            gain_ffn[:, None],
-            jnp.zeros((rows_dev, LANES - experts - 2), BF16),
-        ],
-        axis=1,
-    )
-    both = [
-        jnp.concatenate(
-            [w[:, side * half : (side + 1) * half] for w in (w_query, w_key, w_value)]
-            + [small_w, w_output[:, side * half : (side + 1) * half]],
-            axis=1,
-        )
-        for side in range(2)
-    ]
-    ours = jnp.where(core == 0, both[0], both[1])
-    theirs = jnp.where(core == 0, both[1], both[0])
+    long = tok + CODE_ROWS
+    columns_all = 4 * half + LANES
+    ours, theirs, x_ext = call(
+        functools.partial(start_kernel, experts),
+        [((rows_dev, columns_all), BF16)] * 2 + [((long, width), BF16)],
+        where,
+        w_query,
+        w_key,
+        w_value,
+        w_output,
+        w_router.T,
+        jnp.stack([gain_attn, gain_ffn]),
+        x,
+        segments,
+        smem_first=True,
+    )
     block = place.ordered(ours, place.swap(theirs, 0), 0, 0, jnp.concatenate)
     chip_rows = 2 * rows_dev
     halved = chip_rows % 16 == 0
     split = (block.shape[-1] - half) // 2
-    long = tok + CODE_ROWS
-    x_ext = call(extend_kernel, [((long, width), BF16)], x, segments)[0]
     around = (place.shift(x_ext, 2), x_ext, place.shift(x_ext, -2))
     near = 2 * BLK
     bias, bias_prev, bias_next, far_bias, meta_col, meta_row = call(
@@ -1953,7 +1977,7 @@
         sum_q, sum_k, sum_v, sum_out, grad_router, gain_rows, table_sum = call(
             functools.partial(finish_kernel, experts, buckets),
             [((rows_dev, width), F32)] * 4
-            + [((rows_dev, experts), F32), ((8, rows_dev), F32), ((buckets, heads), F32)],
+            + [((experts, rows_dev), F32), ((8, rows_dev), F32), ((heads, buckets), F32)],
             where,
             kept,
             came,
@@ -1964,6 +1988,7 @@
             smem_first=True,
         )
         grad_gain_one, grad_gain_two = gain_rows[0], gain_rows[1]
+        grad_router, table_sum = grad_router.T, table_sum.T
     else:
 
         def columns(first):

time: 245 us -> 240 us (0.980)
  local copies, waits for them, and re-layouts: 15.8 us -> 11.4 us
    unnamed x108 -> x109, local copies, waits for them, and re-layouts: 10.5 us -> 9.34 us
where the time goes in v3:
time: 240 us; the launch traced here: 238 us
  Pallas kernels  106 us (44%)
  starting transfers between devices  67.3 us (28%)
  waiting for transfers between devices  47.9 us (20%)
  local copies, waits for them, and re-layouts  11.4 us (5%)
  other arithmetic  4.39 us (2%)
    pallas_call x24, Pallas kernels, call(): pl.pallas_call(kernel, out_shape=shapes, grid=grid if grid is not None el...  106 us
    ppermute x21, waiting for transfers between devices, swap(): return lax.ppermute(value, AXES, pairs)  27.6 us
    ppermute x9, starting transfers between devices, swap_mask(): return lax.ppermute(value, AXES, [(i, i ^ mask) for i in range(self.count)])  18.5 us
    ppermute x21, starting transfers between devices, swap(): return lax.ppermute(value, AXES, pairs)  18.1 us
    ppermute x6, starting transfers between devices, shift(): return lax.ppermute(value, AXES, pairs)  16.4 us
    ppermute x9, waiting for transfers between devices, swap_mask(): return lax.ppermute(value, AXES, [(i, i ^ mask) for i in range(self.count)])  15.8 us
    all_to_all x3, starting transfers between devices, exchange(): lax.all_to_all(message, 'ctx', split_axis=0, concat_axis=0, tiled=True)  14.3 us
    unnamed x109, local copies, waits for them, and re-layouts  9.34 us
  transfers between devices with their start and end apart: 39, of which 19 were waited for; matrix products, arithmetic and copies ran while one was open for 2% of the time, Pallas kernels for 39%

profile of v3, /device:TPU:0, one launch (start us, length us, event | category | flops | bytes accessed | tf_op | source)
XLA Modules:
  0.0 238.1 jit_solution(14072674855438465939)
XLA Ops:
  2.5 2.1 shard_map.230
  5.1 4.6 %collective-permute-start.4 = (bf16[272,768]{1,0:T(8,128)(2,1)}, bf16[272,768]{1,0:T(8,128)(2,1)S(1)}, u32[]{:S(2)}, u32[]{:S(2)}) collective-permute-start(bf16[272,768]{1,0:T(8,128)(2,1)} %get-tuple-element.95.refs_5_), channel_id=1, source_target_pairs={{0,2},{1,3},{2,4},{3,5},{4,6},{5,7},{6,8},{7,9},{8,10},{9,11},{10,... | collective-permute-start | bytes 1253384 | tf_op jit(solution)/shard_map/ppermute | solution.py:1217
  11.9 3.7 %collective-permute-start.1 = (bf16[48,1664]{1,0:T(8,128)(2,1)S(1)}, bf16[48,1664]{1,0:T(8,128)(2,1)S(1)}, u32[]{:S(2)}, u32[]{:S(2)}) collective-permute-start(bf16[48,1664]{1,0:T(8,128)(2,1)S(1)} %pad_maximum_fusion.5.refs_0_), channel_id=1, source_target_pairs={{0,4},{1,5},{2,6},{3,7},{4,0},{5,1},{6,2},{7,3},{8,12},{9,13},{10,... | collective-permute-start | bytes 479240 | tf_op jit(solution)/shard_map/ppermute | solution.py:1238
  15.5 2.6 %collective-permute-start.2 = (bf16[48,1664]{1,0:T(8,128)(2,1)S(1)}, bf16[48,1664]{1,0:T(8,128)(2,1)S(1)}, u32[]{:S(2)}, u32[]{:S(2)}) collective-permute-start(bf16[48,1664]{1,0:T(8,128)(2,1)S(1)} %pad_maximum_fusion.5.refs_0_), channel_id=1, source_target_pairs={{0,8},{1,9},{2,10},{3,11},{4,12},{5,13},{6,14},{7,15},{8,0},{9,1},... | collective-permute-start | bytes 479240 | tf_op jit(solution)/shard_map/ppermute | solution.py:1238
  19.6 3.3 %shard_map.229 = (bf16[6,256,512]{2,1,0:T(8,128)(2,1)}, bf16[6,128,256]{2,1,0:T(8,128)(2,1)}, bf16[6,128,256]{2,1,0:T(8,128)(2,1)}, f32[8,128]{1,0:T(8,128)}, s32[256,128]{1,0:T(8,128)}, /*index=5*/s32[8,256]{1,0:T(8,128)}) custom-call(s32[6]{0:T(128)} %stack.57.where_ref.core_ref.bits_ref, bf16[32,12]{1,0:T(8,128)(2,1)} %copy.30.table_ref, ...), custom_call_target="tpu_custom_call" | custom-call | flops 345000000 | tf_op jit(solution)/shard_map/pallas_call | solution.py:1295
  22.9 8.3 %collective-permute-done.1.refs_1_ = bf16[48,1664]{1,0:T(8,128)(2,1)S(1)} collective-permute-done((bf16[48,1664]{1,0:T(8,128)(2,1)S(1)}, bf16[48,1664]{1,0:T(8,128)(2,1)S(1)}, u32[]{:S(2)}, u32[]{:S(2)}) %collective-permute-start.1) | collective-permute-done | bytes 159776 | tf_op jit(solution)/shard_map/ppermute | solution.py:1238
  31.9 4.9 %collective-permute-done.3.refs_3_ = bf16[48,1664]{1,0:T(8,128)(2,1)S(1)} collective-permute-done((bf16[48,1664]{1,0:T(8,128)(2,1)S(1)}, bf16[48,1664]{1,0:T(8,128)(2,1)S(1)}, u32[]{:S(2)}, u32[]{:S(2)}) %collective-permute-start.3) | collective-permute-done | bytes 159776 | tf_op jit(solution)/shard_map/ppermute | solution.py:1238
  44.3 3.2 %collective-permute-done.12 = bf16[2,2,48,384]{3,2,1,0:T(8,128)(2,1)S(1)} collective-permute-done((bf16[2,2,48,384]{3,2,1,0:T(8,128)(2,1)S(1)}, bf16[2,2,48,384]{3,2,1,0:T(8,128)(2,1)S(1)}, u32[]{:S(2)}, u32[]{:S(2)}) %collective-permute-start.12) | collective-permute-done | bytes 147488 | tf_op jit(solution)/shard_map/ppermute | solution.py:1206
  54.1 2.1 shard_map.232.refs_7_
  56.2 4.4 %all-to-all-start.1 = ((bf16[16,112,128]{2,1,0:T(8,128)(2,1)}), bf16[16,112,128]{2,1,0:T(8,128)(2,1)}, u32[]{:S(2)}, u32[]{:S(2)}) async-start(bf16[16,112,128]{2,1,0:T(8,128)(2,1)} %bitcast.71), calls=%async_computation.1 | async-start | bytes 917504 | tf_op jit(solution)/shard_map/all_to_all | solution.py:1460
  61.5 3.8 %collective-permute-done.7 = bf16[2,2,2,48,640]{4,3,2,1,0:T(8,128)(2,1)S(1)} collective-permute-done((bf16[2,2,2,48,640]{4,3,2,1,0:T(8,128)(2,1)S(1)}, bf16[2,2,2,48,640]{4,3,2,1,0:T(8,128)(2,1)S(1)}, u32[]{:S(2)}, u32[]{:S(2)}) %collective-permute-start.7) | collective-permute-done | bytes 491552 | tf_op jit(solution)/shard_map/ppermute | solution.py:1206
  66.1 18.1 %shard_map.233 = (bf16[512,768]{1,0:T(8,128)(2,1)}, bf16[512,384]{1,0:T(8,128)(2,1)}, bf16[1536,384]{1,0:T(8,128)(2,1)}, bf16[1536,384]{1,0:T(8,128)(2,1)}, f32[...) custom-call(f32[8,128]{1,0:T(8,128)} %get-tuple-element.92.far_ref.l, ...), custom_call_target="tpu_custom_call" | custom-call | flops 1150000000 | tf_op jit(solution)/shard_map/pallas_call | solution.py:1295
  87.0 4.2 %shard_map.234 = (f32[256,768]{1,0:T(8,128)}, bf16[256,768]{1,0:T(8,128)(2,1)}, f32[256,128]{1,0:T(8,128)}, bf16[1792,128]{1,0:T(8,128)(2,1)}) custom-call(s32[6]{0:T(128)} %stack.57.where_ref.core_ref.bits_ref, bf16[256,768]{1,0:T(8,128)(2,1)} %bitcast.63, bf16[512,384]{1,0:T(8,128)(2,1)} %get-tuple-element.101.own_ref.ctx_ref, ...), custom_call_target="tpu_custom_call" | custom-call | flops 4600000000 | tf_op jit(solution)/shard_map/pallas_call | solution.py:1295
  91.2 4.4 %all-to-all-start = ((bf16[16,112,128]{2,1,0:T(8,128)(2,1)}), bf16[16,112,128]{2,1,0:T(8,128)(2,1)S(1)}, u32[]{:S(2)}, u32[]{:S(2)}) async-start(bf16[16,112,128]{2,1,0:T(8,128)(2,1)} %bitcast.75), calls=%async_computation | async-start | bytes 917504 | tf_op jit(solution)/shard_map/all_to_all | solution.py:1460
  95.5 3.8 %collective-permute-start.15 = (f32[3,8,512]{2,1,0:T(8,128)S(1)}, f32[3,8,512]{2,1,0:T(8,128)S(1)}, u32[]{:S(2)}, u32[]{:S(2)}) collective-permute-start(f32[3,8,512]{2,1,0:T(8,128)S(1)} %copy-done.37), channel_id=1, source_target_pairs={{0,2},{1,3},{2,4},{3,5},{4,6},{5,7},{6,8},{7,9},{8,10},{9,11},{10,... | collective-permute-start | bytes 147464 | tf_op jit(solution)/shard_map/ppermute | solution.py:1217
  104.3 4.2 %shard_map.236.earlier_a_ref.qp_ref.qn_ref = bf16[1024,384]{1,0:T(8,128)(2,1)} custom-call(s32[6]{0:T(128)} %stack.57.where_ref.core_ref.bits_ref, bf16[816,768]{1,0:T(8,128)(2,1)} %copy-done.2, bf16[816,768]{1,0:T(8,128)(2,1)} %collective-permute-done.10.refs_5_.came_ref, f32[8,768]{1,0:T(8,128)} %get-tuple-element.104.gain_ref, bf16[384,640]{1,0:T(8,128)(2,1)} %bitcast.51, ...), custom_call_target="tpu_custom_call" | custom-call | flops 345000000 | tf_op jit(solution)/shard_map/pallas_call | solution.py:1295
  111.6 12.5 %shard_map.237 = (bf16[288,768]{1,0:T(8,128)(2,1)}, bf16[288,768]{1,0:T(8,128)(2,1)}, bf16[288,3072]{1,0:T(8,128)(2,1)}, bf16[288,3072]{1,0:T(8,128)(2,1)}, bf16[3584,128]{1,0:T(8,128)(2,1)}) custom-call(bf16[1792,128]{1,0:T(8,128)(2,1)} %bitcast.74, bf16[288,768]{1,0:T(8,128)(2,1)} %shard_map.235.cot_ref, bf16[1,768,3072]{2,1,0:T(8,128)(2,1)} %win_ref.3, ...), custom_call_target="tpu_custom_call" | custom-call | flops 13799999488 | tf_op jit(solution)/shard_map/pallas_call | solution.py:1295
  124.0 5.6 %all-to-all-start.2 = ((bf16[16,224,128]{2,1,0:T(8,128)(2,1)}), bf16[16,224,128]{2,1,0:T(8,128)(2,1)S(1)}, u32[]{:S(2)}, u32[]{:S(2)}) async-start(bf16[16,224,128]{2,1,0:T(8,128)(2,1)} %bitcast.72), calls=%async_computation.2 | async-start | bytes 1835008 | tf_op jit(solution)/shard_map/all_to_all | solution.py:1460
  130.5 16.4 %shard_map.239 = (f32[1,768,3072]{2,1,0:T(8,128)}, f32[1,3072,768]{2,1,0:T(8,128)}) custom-call(bf16[288,768]{1,0:T(8,128)(2,1)} %get-tuple-element.116.rows_ref, bf16[288,768]{1,0:T(8,128)(2,1)} %get-tuple-element.117.grad_ref, bf16[288,3072]{1,0:T(8,128)(2,1)} %get-tuple-element.118.act_ref, bf16[288,3072]{1,0:T(8,128)(2,1)} %get-tuple-element.119.gbef_ref, ...), custom_call_target="tpu_custom_call" | custom-call | flops 18400000000 | tf_op jit(solution)/shard_map/pallas_call | solution.py:1295
  146.9 3.5 %all-to-all-done.2 = bf16[16,224,128]{2,1,0:T(8,128)(2,1)S(1)} async-done(((bf16[16,224,128]{2,1,0:T(8,128)(2,1)}), bf16[16,224,128]{2,1,0:T(8,128)(2,1)S(1)}, u32[]{:S(2)}, u32[]{:S(2)}) %all-to-all-start.2) | async-done | bytes 917536 | tf_op jit(solution)/shard_map/all_to_all | solution.py:1460
  151.4 6.5 %shard_map.240 = (f32[256,768]{1,0:T(8,128)}, bf16[256,384]{1,0:T(8,128)(2,1)}, bf16[256,384]{1,0:T(8,128)(2,1)}, bf16[272,384]{1,0:T(8,128)(2,1)}, bf16[272,384]{1,0:T(8,128)(2,1)}, /*index=5*/f32[768,128]{1,0:T(8,128)}) custom-call(s32[6]{0:T(128)} %stack.57.where_ref.core_ref.bits_ref, bf16[3584,128]{1,0:T(8,128)(2,1)} %bitcast.58, ...), custom_call_target="tpu_custom_call" | custom-call | flops 5750000128 | tf_op jit(solution)/shard_map/pallas_call | solution.py:1295
  160.8 3.7 %collective-permute-start.20 = (bf16[544,384]{1,0:T(8,128)(2,1)S(1)}, bf16[544,384]{1,0:T(8,128)(2,1)S(1)}, u32[]{:S(2)}, u32[]{:S(2)}) collective-permute-start(bf16[544,384]{1,0:T(8,128)(2,1)S(1)} %pad_maximum_fusion.3.msg_ref), channel_id=1, source_target_pairs={{0,2},{1,3},{2,4},{3,5},{4,6},{5,7},{6,8},{7,9},{8,10},{9,11},{10,... | collective-permute-start | bytes 1253384 | tf_op jit(solution)/shard_map/ppermute | solution.py:1217
  166.2 13.1 %shard_map.241 = (bf16[512,384]{1,0:T(8,128)(2,1)S(1)}, f32[512,384]{1,0:T(8,128)S(1)}, f32[512,384]{1,0:T(8,128)S(1)}, f32[3,8,128]{2,1,0:T(8,128)S(1)}) custom-call(f32[8,128]{1,0:T(8,128)S(1)} %copy-done.29, bf16[512,384]{1,0:T(8,128)(2,1)S(1)} %copy-done.33, bf16[1536,384]{1,0:T(8,128)(2,1)S(1)} %copy-done.30, bf16[1536,384]{1,0:T(8,128)(2,1)S(1)} %copy-done.31, ...), custom_call_target="tpu_custom_call" | custom-call | flops 16099999744 | tf_op jit(solution)/shard_map/pallas_call | solution.py:1295
  182.9 7.8 %shard_map.243 = (bf16[512,384]{1,0:T(8,128)(2,1)S(1)}, bf16[512,384]{1,0:T(8,128)(2,1)S(1)}) custom-call(f32[8,128]{1,0:T(8,128)S(1)} %copy-done.29, bf16[1024,384]{1,0:T(8,128)(2,1)S(1)} %copy-done.12, bf16[1024,384]{1,0:T(8,128)(2,1)S(1)} %copy-done.12, bf16[1536,384]{1,0:T(8,128)(2,1)S(1)} %copy-done.30, bf16[1536,384]{1,0:T(8,128)(2,1)S(1)} %copy-done.31, ...), custom_call_target="tpu_custom_call" | custom-call | flops 8049999872 | tf_op jit(solution)/shard_map/pallas_call | solution.py:1295
  190.8 2.2 shard_map.246
  193.0 2.7 %collective-permute-start.25 = (bf16[384,640]{1,0:T(8,128)(2,1)S(1)}, bf16[384,640]{1,0:T(8,128)(2,1)S(1)}, u32[]{:S(2)}, u32[]{:S(2)}) collective-permute-start(bf16[384,640]{1,0:T(8,128)(2,1)S(1)} %get-tuple-element.145), channel_id=1, source_target_pairs={{0,2},{1,3},{2,0},{3,1},{4,6},{5,7},{6,4},{7,5},{8,10},{9,11},{10,... | collective-permute-start | bytes 1474568 | tf_op jit(solution)/shard_map/ppermute | solution.py:1206
  198.3 2.1 shard_map.244
  200.5 6.4 %collective-permute-done.25.later_ref.refs_1_ = bf16[384,640]{1,0:T(8,128)(2,1)S(1)} collective-permute-done((bf16[384,640]{1,0:T(8,128)(2,1)S(1)}, bf16[384,640]{1,0:T(8,128)(2,1)S(1)}, u32[]{:S(2)}, u32[]{:S(2)}) %collective-permute-start.25) | collective-permute-done | bytes 491552 | tf_op jit(solution)/shard_map/ppermute | solution.py:1206
  210.4 3.9 %collective-permute-start.31 = (bf16[96,640]{1,0:T(8,128)(2,1)S(1)}, bf16[96,640]{1,0:T(8,128)(2,1)S(1)}, u32[]{:S(2)}, u32[]{:S(2)}) collective-permute-start(bf16[96,640]{1,0:T(8,128)(2,1)S(1)} %get-tuple-element.157), channel_id=1, source_target_pairs={{0,4},{1,5},{2,6},{3,7},{4,0},{5,1},{6,2},{7,3},{8,12},{9,13},{10,... | collective-permute-start | bytes 368648 | tf_op jit(solution)/shard_map/ppermute | solution.py:1238
  216.8 2.1 collective-permute-done.27.refs_1_
  219.6 3.1 %collective-permute-start.28 = (bf16[48,1024]{1,0:T(8,128)(2,1)S(1)}, bf16[48,1024]{1,0:T(8,128)(2,1)S(1)}, u32[]{:S(2)}, u32[]{:S(2)}) collective-permute-start(bf16[48,1024]{1,0:T(8,128)(2,1)S(1)} %get-tuple-element.152), channel_id=1, source_target_pairs={{0,4},{1,5},{2,6},{3,7},{4,0},{5,1},{6,2},{7,3},{8,12},{9,13},{10,... | collective-permute-start | bytes 294920 | tf_op jit(solution)/shard_map/ppermute | solution.py:1238
  229.5 2.7 %collective-permute-done.34.refs_5_ = bf16[48,640]{1,0:T(8,128)(2,1)S(1)} collective-permute-done((bf16[48,640]{1,0:T(8,128)(2,1)S(1)}, bf16[48,640]{1,0:T(8,128)(2,1)S(1)}, u32[]{:S(2)}, u32[]{:S(2)}) %collective-permute-start.34) | collective-permute-done | bytes 61472 | tf_op jit(solution)/shard_map/ppermute | solution.py:1206
  (196 shorter events, 64.6 us)
Async XLA Ops:
  5.1 32.4 %collective-permute-start.4 = (bf16[272,768]{1,0:T(8,128)(2,1)}, bf16[272,768]{1,0:T(8,128)(2,1)S(1)}, u32[]{:S(2)}, u32[]{:S(2)}) collective-permute-start(bf16[272,768]{1,0:T(8,128)(2,1)} %get-tuple-element.95.refs_5_), channel_id=1, source_target_pairs={{0,2},{1,3},{2,4},{3,5},{4,6},{5,7},{6,8},{7,9},{8,10},{9,11},{10,... | collective-permute-start | bytes 1253384 | tf_op jit(solution)/shard_map/ppermute | solution.py:1217
  9.6 27.8 %collective-permute-start.5 = (bf16[272,768]{1,0:T(8,128)(2,1)}, bf16[272,768]{1,0:T(8,128)(2,1)S(1)}, u32[]{:S(2)}, u32[]{:S(2)}) collective-permute-start(bf16[272,768]{1,0:T(8,128)(2,1)} %get-tuple-element.95.refs_5_), channel_id=1, source_target_pairs={{2,0},{3,1},{4,2},{5,3},{6,4},{7,5},{8,6},{9,7},{10,8},{11,9},{12,... | collective-permute-start | bytes 1253384 | tf_op jit(solution)/shard_map/ppermute | solution.py:1217
  11.9 19.3 %collective-permute-start.1 = (bf16[48,1664]{1,0:T(8,128)(2,1)S(1)}, bf16[48,1664]{1,0:T(8,128)(2,1)S(1)}, u32[]{:S(2)}, u32[]{:S(2)}) collective-permute-start(bf16[48,1664]{1,0:T(8,128)(2,1)S(1)} %pad_maximum_fusion.5.refs_0_), channel_id=1, source_target_pairs={{0,4},{1,5},{2,6},{3,7},{4,0},{5,1},{6,2},{7,3},{8,12},{9,13},{10,... | collective-permute-start | bytes 479240 | tf_op jit(solution)/shard_map/ppermute | solution.py:1238
  15.5 15.7 %collective-permute-start.2 = (bf16[48,1664]{1,0:T(8,128)(2,1)S(1)}, bf16[48,1664]{1,0:T(8,128)(2,1)S(1)}, u32[]{:S(2)}, u32[]{:S(2)}) collective-permute-start(bf16[48,1664]{1,0:T(8,128)(2,1)S(1)} %pad_maximum_fusion.5.refs_0_), channel_id=1, source_target_pairs={{0,8},{1,9},{2,10},{3,11},{4,12},{5,13},{6,14},{7,15},{8,0},{9,1},... | collective-permute-start | bytes 479240 | tf_op jit(solution)/shard_map/ppermute | solution.py:1238
  18.1 18.6 %collective-permute-start.3 = (bf16[48,1664]{1,0:T(8,128)(2,1)S(1)}, bf16[48,1664]{1,0:T(8,128)(2,1)S(1)}, u32[]{:S(2)}, u32[]{:S(2)}) collective-permute-start(bf16[48,1664]{1,0:T(8,128)(2,1)S(1)} %pad_maximum_fusion.5.refs_0_), channel_id=1, source_target_pairs={{0,12},{1,13},{2,14},{3,15},{4,8},{5,9},{6,10},{7,11},{8,4},{9,5},... | collective-permute-start | bytes 479240 | tf_op jit(solution)/shard_map/ppermute | solution.py:1238
  40.7 6.8 %collective-permute-start.12 = (bf16[2,2,48,384]{3,2,1,0:T(8,128)(2,1)S(1)}, bf16[2,2,48,384]{3,2,1,0:T(8,128)(2,1)S(1)}, u32[]{:S(2)}, u32[]{:S(2)}) collective-permute-start(bf16[2,2,48,384]{3,2,1,0:T(8,128)(2,1)S(1)} %bitcast.69), channel_id=1, source_target_pairs={{0,2},{1,3},{2,0},{3,1},{4,6},{5,7},{6,4},{7,5},{8,10},{9,11},{10,... | collective-permute-start | bytes 442376 | tf_op jit(solution)/shard_map/ppermute | solution.py:1206
  40.8 10.2 %collective-permute-start.6 = (bf16[2,2,48,640]{3,2,1,0:T(8,128)(2,1)S(1)}, bf16[2,2,48,640]{3,2,1,0:T(8,128)(2,1)S(1)}, u32[]{:S(2)}, u32[]{:S(2)}) collective-permute-start(bf16[2,2,48,640]{3,2,1,0:T(8,128)(2,1)S(1)} %bitcast.65), channel_id=1, source_target_pairs={{0,2},{1,3},{2,0},{3,1},{4,6},{5,7},{6,4},{7,5},{8,10},{9,11},{10,... | collective-permute-start | bytes 737288 | tf_op jit(solution)/shard_map/ppermute | solution.py:1206
  44.3 21.0 %collective-permute-start.10 = (bf16[816,768]{1,0:T(8,128)(2,1)S(1)}, bf16[816,768]{1,0:T(8,128)(2,1)}, u32[]{:S(2)}, u32[]{:S(2)}) collective-permute-start(bf16[816,768]{1,0:T(8,128)(2,1)S(1)} %get-tuple-element.99.refs_4_.x_ref), channel_id=1, source_target_pairs={{0,1},{1,0},{2,3},{3,2},{4,5},{5,4},{6,7},{7,6},{8,9},{9,8},{10,11... | collective-permute-start | bytes 3760136 | tf_op jit(solution)/shard_map/ppermute | solution.py:1206
  49.4 12.1 %collective-permute-start.9 = (bf16[2,2,2,48,640]{4,3,2,1,0:T(8,128)(2,1)S(1)}, bf16[2,2,2,48,640]{4,3,2,1,0:T(8,128)(2,1)S(1)}, u32[]{:S(2)}, u32[]{:S(2)}) collective-permute-start(bf16[2,2,2,48,640]{4,3,2,1,0:T(8,128)(2,1)S(1)} %pad_maximum_fusion.2), channel_id=1, source_target_pairs={{0,2},{1,3},{2,0},{3,1},{4,6},{5,7},{6,4},{7,5},{8,10},{9,11},{10,... | collective-permute-start | bytes 1474568 | tf_op jit(solution)/shard_map/ppermute | solution.py:1206
  51.1 14.2 %collective-permute-start.7 = (bf16[2,2,2,48,640]{4,3,2,1,0:T(8,128)(2,1)S(1)}, bf16[2,2,2,48,640]{4,3,2,1,0:T(8,128)(2,1)S(1)}, u32[]{:S(2)}, u32[]{:S(2)}) collective-permute-start(bf16[2,2,2,48,640]{4,3,2,1,0:T(8,128)(2,1)S(1)} %pad_maximum_fusion.1.later_ref), channel_id=1, source_target_pairs={{0,16},{1,17},{2,18},{3,19},{4,20},{5,21},{6,22},{7,23},{8,24},{9,... | collective-permute-start | bytes 1474568 | tf_op jit(solution)/shard_map/ppermute | solution.py:1206
  53.6 30.7 %collective-permute-start.14 = (bf16[384,768]{1,0:T(8,128)(2,1)}, bf16[384,768]{1,0:T(8,128)(2,1)}, u32[]{:S(2)}, u32[]{:S(2)}) collective-permute-start(bf16[384,768]{1,0:T(8,128)(2,1)} %bitcast.26.wonear_ref), channel_id=1, source_target_pairs={{0,16},{1,17},{2,18},{3,19},{4,20},{5,21},{6,22},{7,23},{8,24},{9,... | collective-permute-start | bytes 1769480 | tf_op jit(solution)/shard_map/ppermute | solution.py:1206
  56.2 34.9 %all-to-all-start.1 = ((bf16[16,112,128]{2,1,0:T(8,128)(2,1)}), bf16[16,112,128]{2,1,0:T(8,128)(2,1)}, u32[]{:S(2)}, u32[]{:S(2)}) async-start(bf16[16,112,128]{2,1,0:T(8,128)(2,1)} %bitcast.71), calls=%async_computation.1 | async-start | bytes 917504 | tf_op jit(solution)/shard_map/all_to_all | solution.py:1460
  91.2 17.6 %all-to-all-start = ((bf16[16,112,128]{2,1,0:T(8,128)(2,1)}), bf16[16,112,128]{2,1,0:T(8,128)(2,1)S(1)}, u32[]{:S(2)}, u32[]{:S(2)}) async-start(bf16[16,112,128]{2,1,0:T(8,128)(2,1)} %bitcast.75), calls=%async_computation | async-start | bytes 917504 | tf_op jit(solution)/shard_map/all_to_all | solution.py:1460
  95.5 14.8 %collective-permute-start.15 = (f32[3,8,512]{2,1,0:T(8,128)S(1)}, f32[3,8,512]{2,1,0:T(8,128)S(1)}, u32[]{:S(2)}, u32[]{:S(2)}) collective-permute-start(f32[3,8,512]{2,1,0:T(8,128)S(1)} %copy-done.37), channel_id=1, source_target_pairs={{0,2},{1,3},{2,4},{3,5},{4,6},{5,7},{6,8},{7,9},{8,10},{9,11},{10,... | collective-permute-start | bytes 147464 | tf_op jit(solution)/shard_map/ppermute | solution.py:1217
  99.4 10.9 %collective-permute-start.16 = (f32[3,8,512]{2,1,0:T(8,128)S(1)}, f32[3,8,512]{2,1,0:T(8,128)S(1)}, u32[]{:S(2)}, u32[]{:S(2)}) collective-permute-start(f32[3,8,512]{2,1,0:T(8,128)S(1)} %copy-done.37), channel_id=1, source_target_pairs={{2,0},{3,1},{4,2},{5,3},{6,4},{7,5},{8,6},{9,7},{10,8},{11,9},{12,... | collective-permute-start | bytes 147464 | tf_op jit(solution)/shard_map/ppermute | solution.py:1217
  102.8 26.8 %collective-permute-start.18 = (bf16[288,768]{1,0:T(8,128)(2,1)}, bf16[288,768]{1,0:T(8,128)(2,1)S(1)}, u32[]{:S(2)}, u32[]{:S(2)}) collective-permute-start(bf16[288,768]{1,0:T(8,128)(2,1)} %shard_map.235.cot_ref), channel_id=1, source_target_pairs={{0,16},{1,17},{2,18},{3,19},{4,20},{5,21},{6,22},{7,23},{8,24},{9,... | collective-permute-start | bytes 1327112 | tf_op jit(solution)/shard_map/ppermute | solution.py:1206
  108.8 20.8 %collective-permute-start.17 = (bf16[1792,128]{1,0:T(8,128)(2,1)S(1)}, bf16[1792,128]{1,0:T(8,128)(2,1)S(1)}, u32[]{:S(2)}, u32[]{:S(2)}) collective-permute-start(bf16[1792,128]{1,0:T(8,128)(2,1)S(1)} %bitcast.73), channel_id=1, source_target_pairs={{0,16},{1,17},{2,18},{3,19},{4,20},{5,21},{6,22},{7,23},{8,24},{9,... | collective-permute-start | bytes 1376264 | tf_op jit(solution)/shard_map/ppermute | solution.py:1206
  124.0 26.4 %all-to-all-start.2 = ((bf16[16,224,128]{2,1,0:T(8,128)(2,1)}), bf16[16,224,128]{2,1,0:T(8,128)(2,1)S(1)}, u32[]{:S(2)}, u32[]{:S(2)}) async-start(bf16[16,224,128]{2,1,0:T(8,128)(2,1)} %bitcast.72), calls=%async_computation.2 | async-start | bytes 1835008 | tf_op jit(solution)/shard_map/all_to_all | solution.py:1460
  158.4 20.9 %collective-permute-start.22 = (bf16[256,384]{1,0:T(8,128)(2,1)}, bf16[256,384]{1,0:T(8,128)(2,1)S(1)}, u32[]{:S(2)}, u32[]{:S(2)}) collective-permute-start(bf16[256,384]{1,0:T(8,128)(2,1)} %get-tuple-element.130), channel_id=1, source_target_pairs={{0,1},{1,0},{2,3},{3,2},{4,5},{5,4},{6,7},{7,6},{8,9},{9,8},{10,11... | collective-permute-start | bytes 589832 | tf_op jit(solution)/shard_map/ppermute | solution.py:1206
  160.8 22.1 %collective-permute-start.20 = (bf16[544,384]{1,0:T(8,128)(2,1)S(1)}, bf16[544,384]{1,0:T(8,128)(2,1)S(1)}, u32[]{:S(2)}, u32[]{:S(2)}) collective-permute-start(bf16[544,384]{1,0:T(8,128)(2,1)S(1)} %pad_maximum_fusion.3.msg_ref), channel_id=1, source_target_pairs={{0,2},{1,3},{2,4},{3,5},{4,6},{5,7},{6,8},{7,9},{8,10},{9,11},{10,... | collective-permute-start | bytes 1253384 | tf_op jit(solution)/shard_map/ppermute | solution.py:1217
  164.5 18.3 %collective-permute-start.21 = (bf16[544,384]{1,0:T(8,128)(2,1)S(1)}, bf16[544,384]{1,0:T(8,128)(2,1)S(1)}, u32[]{:S(2)}, u32[]{:S(2)}) collective-permute-start(bf16[544,384]{1,0:T(8,128)(2,1)S(1)} %pad_maximum_fusion.3.msg_ref), channel_id=1, source_target_pairs={{2,0},{3,1},{4,2},{5,3},{6,4},{7,5},{8,6},{9,7},{10,8},{11,9},{12,... | collective-permute-start | bytes 1253384 | tf_op jit(solution)/shard_map/ppermute | solution.py:1217
  180.6 10.2 %collective-permute-start.24 = (bf16[384,384]{1,0:T(8,128)(2,1)S(1)}, bf16[384,384]{1,0:T(8,128)(2,1)S(1)}, u32[]{:S(2)}, u32[]{:S(2)}) collective-permute-start(bf16[384,384]{1,0:T(8,128)(2,1)S(1)} %get-tuple-element.144), channel_id=1, source_target_pairs={{0,16},{1,17},{2,18},{3,19},{4,20},{5,21},{6,22},{7,23},{8,24},{9,... | collective-permute-start | bytes 884744 | tf_op jit(solution)/shard_map/ppermute | solution.py:1206
  193.0 13.9 %collective-permute-start.25 = (bf16[384,640]{1,0:T(8,128)(2,1)S(1)}, bf16[384,640]{1,0:T(8,128)(2,1)S(1)}, u32[]{:S(2)}, u32[]{:S(2)}) collective-permute-start(bf16[384,640]{1,0:T(8,128)(2,1)S(1)} %get-tuple-element.145), channel_id=1, source_target_pairs={{0,2},{1,3},{2,0},{3,1},{4,6},{5,7},{6,4},{7,5},{8,10},{9,11},{10,... | collective-permute-start | bytes 1474568 | tf_op jit(solution)/shard_map/ppermute | solution.py:1206
  195.7 12.7 %collective-permute-start.26 = (bf16[384,640]{1,0:T(8,128)(2,1)S(1)}, bf16[384,640]{1,0:T(8,128)(2,1)S(1)}, u32[]{:S(2)}, u32[]{:S(2)}) collective-permute-start(bf16[384,640]{1,0:T(8,128)(2,1)S(1)} %get-tuple-element.147), channel_id=1, source_target_pairs={{0,16},{1,17},{2,18},{3,19},{4,20},{5,21},{6,22},{7,23},{8,24},{9,... | collective-permute-start | bytes 1474568 | tf_op jit(solution)/shard_map/ppermute | solution.py:1206
  200.4 23.5 %collective-permute-start.23 = (f32[256,768]{1,0:T(8,128)S(1)}, f32[256,768]{1,0:T(8,128)S(1)}, u32[]{:S(2)}, u32[]{:S(2)}) collective-permute-start(f32[256,768]{1,0:T(8,128)S(1)} %get-tuple-element.137), channel_id=1, source_target_pairs={{0,1},{1,0},{2,3},{3,2},{4,5},{5,4},{6,7},{7,6},{8,9},{9,8},{10,11... | collective-permute-start | bytes 2359304 | tf_op jit(solution)/shard_map/ppermute | solution.py:1206
  209.2 9.7 %collective-permute-start.27 = (bf16[192,1024]{1,0:T(8,128)(2,1)S(1)}, bf16[192,1024]{1,0:T(8,128)(2,1)S(1)}, u32[]{:S(2)}, u32[]{:S(2)}) collective-permute-start(bf16[192,1024]{1,0:T(8,128)(2,1)S(1)} %get-tuple-element.150), channel_id=1, source_target_pairs={{0,2},{1,3},{2,0},{3,1},{4,6},{5,7},{6,4},{7,5},{8,10},{9,11},{10,... | collective-permute-start | bytes 1179656 | tf_op jit(solution)/shard_map/ppermute | solution.py:1206
  210.4 12.4 %collective-permute-start.31 = (bf16[96,640]{1,0:T(8,128)(2,1)S(1)}, bf16[96,640]{1,0:T(8,128)(2,1)S(1)}, u32[]{:S(2)}, u32[]{:S(2)}) collective-permute-start(bf16[96,640]{1,0:T(8,128)(2,1)S(1)} %get-tuple-element.157), channel_id=1, source_target_pairs={{0,4},{1,5},{2,6},{3,7},{4,0},{5,1},{6,2},{7,3},{8,12},{9,13},{10,... | collective-permute-start | bytes 368648 | tf_op jit(solution)/shard_map/ppermute | solution.py:1238
  214.3 13.0 %collective-permute-start.32 = (bf16[96,640]{1,0:T(8,128)(2,1)S(1)}, bf16[96,640]{1,0:T(8,128)(2,1)S(1)}, u32[]{:S(2)}, u32[]{:S(2)}) collective-permute-start(bf16[96,640]{1,0:T(8,128)(2,1)S(1)} %get-tuple-element.158), channel_id=1, source_target_pairs={{0,8},{1,9},{2,10},{3,11},{4,12},{5,13},{6,14},{7,15},{8,0},{9,1},... | collective-permute-start | bytes 368648 | tf_op jit(solution)/shard_map/ppermute | solution.py:1238
  215.4 11.8 %collective-permute-start.33 = (bf16[96,640]{1,0:T(8,128)(2,1)S(1)}, bf16[96,640]{1,0:T(8,128)(2,1)S(1)}, u32[]{:S(2)}, u32[]{:S(2)}) collective-permute-start(bf16[96,640]{1,0:T(8,128)(2,1)S(1)} %get-tuple-element.159), channel_id=1, source_target_pairs={{0,12},{1,13},{2,14},{3,15},{4,8},{5,9},{6,10},{7,11},{8,4},{9,5},... | collective-permute-start | bytes 368648 | tf_op jit(solution)/shard_map/ppermute | solution.py:1238
  219.6 12.6 %collective-permute-start.28 = (bf16[48,1024]{1,0:T(8,128)(2,1)S(1)}, bf16[48,1024]{1,0:T(8,128)(2,1)S(1)}, u32[]{:S(2)}, u32[]{:S(2)}) collective-permute-start(bf16[48,1024]{1,0:T(8,128)(2,1)S(1)} %get-tuple-element.152), channel_id=1, source_target_pairs={{0,4},{1,5},{2,6},{3,7},{4,0},{5,1},{6,2},{7,3},{8,12},{9,13},{10,... | collective-permute-start | bytes 294920 | tf_op jit(solution)/shard_map/ppermute | solution.py:1238
  222.7 11.4 %collective-permute-start.29 = (bf16[48,1024]{1,0:T(8,128)(2,1)S(1)}, bf16[48,1024]{1,0:T(8,128)(2,1)S(1)}, u32[]{:S(2)}, u32[]{:S(2)}) collective-permute-start(bf16[48,1024]{1,0:T(8,128)(2,1)S(1)} %get-tuple-element.153), channel_id=1, source_target_pairs={{0,8},{1,9},{2,10},{3,11},{4,12},{5,13},{6,14},{7,15},{8,0},{9,1},... | collective-permute-start | bytes 294920 | tf_op jit(solution)/shard_map/ppermute | solution.py:1238
  223.9 10.1 %collective-permute-start.30 = (bf16[48,1024]{1,0:T(8,128)(2,1)S(1)}, bf16[48,1024]{1,0:T(8,128)(2,1)S(1)}, u32[]{:S(2)}, u32[]{:S(2)}) collective-permute-start(bf16[48,1024]{1,0:T(8,128)(2,1)S(1)} %get-tuple-element.154), channel_id=1, source_target_pairs={{0,12},{1,13},{2,14},{3,15},{4,8},{5,9},{6,10},{7,11},{8,4},{9,5},... | collective-permute-start | bytes 294920 | tf_op jit(solution)/shard_map/ppermute | solution.py:1238
  (61 other events, 522.4 us)
